TPU v7x, 32 devices: a whole 2x2x4 slice. The times are simulated.
32 devices in a mesh: section: 4 (over y, x), dp: 8 (over z, core).
Axes of the slice: x: 2, y: 2, z: 4, core: 2. Of those that a mesh axis runs over, the one named last changes fastest.
Arguments:
- activations: bfloat16 [4, 1024, 8192], P('section', 'dp'), may hold values from -6 to 6
- out_grads: bfloat16 [4, 1024, 1024], P('section', 'dp'), may hold values from -1.5 to 1.5
- in_basis: bfloat16 [4, 8192, 256], P('section', 'dp'), may hold values from -0.375 to 0.375
- out_basis: bfloat16 [4, 1024, 1024], P('section', 'dp'), may hold values from -0.1875 to 0.1875
- curvature: bfloat16 [4, 1024, 8192], P('section', None, 'dp'), may hold values from 2 to 32
- left_factors: bfloat16 [4, 8, 32, 1024], P('section', 'dp'), may hold values from -0.1875 to 0.1875
- right_factors: bfloat16 [4, 8, 32, 8192], P('section', None, None, 'dp'), may hold values from -0.0625 to 0.0625
- sequence_ids: int32 [8], replicated, may hold values from 0 to 7, each once
- query_order: int32 [8], replicated, may hold values from 0 to 7, each once
Outputs:
- influence: float32 [4, 8, 8], P('section', 'dp')
Inputs may be any that keep to these rules, and one draw needn't show every extreme that they name: `sequence_ids`: a permutation: each output row receives exactly one training sequence. `query_order`: a permutation: each query is stored in exactly one slot.
All inputs are finite; a program needn't handle non-finite values.
Results may differ from a plain program's by a relative error of at most 0.0057.
Values may be sent and summed in bfloat16 or wider, within the bound.
No kernel may reach another device: no remote copies, remote signals or barrier semaphores. Data moves between devices by JAX's collectives and lax.ppermute only.
A program may use at most 128 MiB of HBM per device.

v0:
```python
import math

import jax
import jax.numpy as jnp
from jax import lax
from jax.sharding import PartitionSpec as P

SEQ_LEN = 128


def on_device(
    activations,
    out_grads,
    in_basis,
    out_basis,
    curvature,
    left_factors,
    right_factors,
    sequence_ids,
    query_order,
):
    layer_acts = activations[0]
    layer_grads = out_grads[0]
    block_basis = in_basis[0]
    columns = block_basis.shape[0]
    block_size = block_basis.shape[1]
    n_blocks = columns // block_size
    grouped_basis = block_basis.reshape(n_blocks, block_size, block_size)
    basis_rows, left_all = (
        lax.all_gather(out_basis[0], "dp", axis=0, tiled=True),
        lax.all_gather(left_factors[0], "dp", axis=0, tiled=True),
    )
    rotated_own = jnp.dot(layer_grads, basis_rows, preferred_element_type=jnp.float32).astype(
        jnp.bfloat16
    )
    all_signals = lax.all_gather(rotated_own, "dp", axis=0, tiled=True)
    feature_cols = lax.all_to_all(layer_acts, "dp", split_axis=1, concat_axis=0, tiled=True)
    token_count = feature_cols.shape[0]
    grouped_cols = feature_cols.reshape(token_count, n_blocks, block_size)
    rotated_acts = jnp.einsum(
        "tbi,bij->tbj", grouped_cols, grouped_basis, preferred_element_type=jnp.float32
    )
    rotated_acts = rotated_acts.astype(jnp.bfloat16).reshape(token_count, columns)
    seq_count = token_count // SEQ_LEN
    group_size = math.gcd(seq_count, 8)
    out_width = all_signals.shape[1]
    signal_groups = all_signals.reshape(seq_count // group_size, group_size, SEQ_LEN, out_width)
    act_groups = rotated_acts.reshape(seq_count // group_size, group_size, SEQ_LEN, columns)
    divisor = curvature[0].astype(jnp.float32)

    def rescale(operands):
        gradient = jnp.einsum(
            "nti,ntj->nij", operands[0], operands[1], preferred_element_type=jnp.float32
        )
        return (gradient / divisor).astype(jnp.bfloat16)

    scaled = lax.map(rescale, (signal_groups, act_groups)).reshape(seq_count, out_width * columns)
    right_all = right_factors[0]
    query_count = right_all.shape[0]
    rank_size = right_all.shape[1]
    query_group = math.gcd(query_count, 8)

    def expand(operands):
        product = jnp.einsum(
            "qri,qrj->qij", operands[0], operands[1], preferred_element_type=jnp.float32
        )
        return product.astype(jnp.bfloat16)

    query_mats = lax.map(
        expand,
        (
            left_all.reshape(query_count // query_group, query_group, rank_size, out_width),
            right_all.reshape(query_count // query_group, query_group, rank_size, columns),
        ),
    )
    query_mats = query_mats.reshape(query_count, out_width * columns)
    scores = lax.dot_general(
        scaled, query_mats, (((1,), (1,)), ((), ())), preferred_element_type=jnp.float32
    )
    row_pick = (sequence_ids[None, :] == jnp.arange(seq_count, dtype=jnp.int32)[:, None]).astype(
        jnp.float32
    )
    col_pick = (query_order[:, None] == jnp.arange(query_count, dtype=jnp.int32)[None, :]).astype(
        jnp.float32
    )
    placed = jnp.dot(
        jnp.dot(row_pick, scores, precision=lax.Precision.HIGHEST),
        col_pick,
        precision=lax.Precision.HIGHEST,
    )
    layer_part = lax.psum_scatter(placed, "dp", scatter_dimension=0, tiled=True)
    every_layer = lax.all_gather(layer_part[None], "section", axis=0, tiled=True)
    depth = jnp.arange(every_layer.shape[0], dtype=jnp.int32)
    keep_mask = (depth >= lax.axis_index("section")).astype(jnp.float32)
    total = jnp.sum(every_layer * keep_mask[:, None, None], axis=0)
    return total[None]


def solution(mesh):
    placed = (
        P("section", "dp", None),
        P("section", "dp", None),
        P("section", "dp", None),
        P("section", "dp", None),
        P("section", None, "dp"),
        P("section", "dp", None, None),
        P("section", None, None, "dp"),
        P(),
        P(),
    )
    return jax.shard_map(
        on_device, mesh=mesh, in_specs=placed, out_specs=P("section", "dp", None), check_vma=False
    )
```

profile of v0, /device:TPU:0, one launch (start us, length us, event | category | flops | bytes accessed | tf_op | source)
XLA Modules:
  0.0 231.3 jit_solution(9531767181207952798)
XLA Ops:
  6.5 0.0 copy-start
  6.5 0.0 all-gather.9.cloned.1.call-start
  6.5 0.7 all-gather.9.cloned.1.call-update
  7.3 4.1 %copy.14 = bf16[1,128,8192]{1,2,0:T(8,128)(2,1)} copy(bf16[1,128,8192]{2,1,0:T(8,128)(2,1)} %param.9) | data formatting | bytes 4194304 | tf_op args[0]
  11.3 6.5 %all-to-all-start = ((bf16[128,8,1024]{0,2,1:T(8,128)(2,1)}), bf16[128,8,1024]{0,2,1:T(8,128)(2,1)S(1)}, u32[]{:S(2)}, u32[]{:S(2)}) async-start(bf16[128,8,1024]{0,2,1:T(8,128)(2,1)} %bitcast.41), calls=%async_computation | async-start | bytes 4194304 | tf_op jit(solution)/shard_map/all_to_all | solution.py:37
  17.8 0.0 copy-start.3
  17.8 0.0 all-gather.7.cloned.1.call-start
  17.9 40.3 %all-gather.9.cloned.1.call-done = bf16[1,1024,1024]{2,1,0:T(8,128)(2,1)} async-done(((bf16[1,128,1024]{2,1,0:T(8,128)(2,1)}), bf16[1,1024,1024]{2,1,0:T(8,128)(2,1)}) %all-gather.9.cloned.1.call-update) | async-done | bytes 2097168 | tf_op jit(solution)/shard_map/all_gather | solution.py:30
  58.2 0.0 copy-done.2
  58.2 2.7 %fusion.6 = bf16[128,1024]{1,0:T(8,128)(2,1)} fusion(bf16[1,1024,1024]{2,1,0:T(8,128)(2,1)} %all-gather.9.cloned.1.call-done, bf16[1,128,1024]{2,1,0:T(8,128)(2,1)S(1)} %copy-done.2), kind=kOutput, calls=%fused_computation.10 | convolution fusion | flops 268566528 | bytes 2621440 | tf_op jit(solution)/shard_map/dot_general | solution.py:33
  60.9 0.0 all-gather.7.cloned.1.call-update
  60.9 0.0 copy-done.6
  61.0 0.6 dynamic-slice.1
  61.5 0.0 copy-done.3
  61.5 47.1 %all-gather.1 = bf16[8,1,32,1024]{3,2,1,0:T(8,128)(2,1)S(1)} all-gather(bf16[1,1,32,1024]{3,2,1,0:T(8,128)(2,1)S(1)} %copy-done.3), channel_id=3, replica_groups=mesh['section'=4,'dp'=8] {'dp'}, dimensions={0}, use_global_device_ids=true | all-gather | bytes 589824 | tf_op jit(solution)/shard_map/all_gather | solution.py:31
  108.7 4.1 %bitcast_convert_fusion = f32[1024,1024]{1,0:T(8,128)} fusion(bf16[1,1024,1024]{2,1,0:T(8,128)(2,1)} %param.13), kind=kLoop, calls=%fused_computation.5 | loop fusion | flops 1048576 | bytes 6291456 | tf_op jit(solution)/shard_map/while/body/eval_jaxpr/div | solution.py:55
  112.8 8.1 %convolution_convert_fusion = bf16[8,1024,1024]{2,1,0:T(8,128)(2,1)} fusion(bf16[1,8,32,1024]{3,2,1,0:T(8,128)(2,1)S(1)} %copy-done, bf16[8,1,32,1024]{3,2,1,0:T(8,128)(2,1)S(1)} %all-gather.1), kind=kOutput, calls=%fused_computation.4 | convolution fusion | flops 545259520 | bytes 17825792 | tf_op jit(solution)/shard_map/while/body/eval_jaxpr/qri,qrj->qij/dot_general | solution.py:64
  120.9 0.0 all-to-all-done
  120.9 2.7 %copy.15 = bf16[8,128,1024]{1,0,2:T(8,128)(2,1)} copy(bf16[8,128,1024]{1,2,0:T(8,128)(2,1)S(1)} %bitcast.40) | data formatting | bytes 4194304 | tf_op jit(solution)/shard_map/all_to_all | solution.py:37
  123.6 2.9 %reshape.29 = bf16[1024,4,256]{0,2,1:T(8,128)(2,1)S(1)} reshape(bf16[8,128,1024]{1,0,2:T(8,128)(2,1)} %copy.15) | data formatting | bytes 4194304 | tf_op jit(solution)/shard_map/reshape | solution.py:39
  126.5 0.8 convolution_convert_fusion.1
  127.3 0.6 copy.25
  127.9 0.0 all-gather.7.cloned.1.call-done
  127.9 10.7 %divide_convert_fusion = bf16[8,1024,1024]{2,1,0:T(8,128)(2,1)} fusion(f32[1024,1024]{1,0:T(8,128)} %bitcast_convert_fusion, bf16[8,128,1024]{2,1,0:T(8,128)(2,1)} %bitcast.45, bf16[8,128,1024]{1,0,2:T(8,128)(2,1)S(1)} %bitcast.43), kind=kOutput, calls=%fused_computation | convolution fusion | flops 2164260864 | bytes 25165824 | tf_op jit(solution)/shard_map/while/body/eval_jaxpr/nti,ntj->nij/dot_general | solution.py:52
  138.6 60.0 %fusion.9 = f32[8,8]{1,0:T(8,128)S(1)} fusion(bf16[8,1024,1024]{2,1,0:T(8,128)(2,1)} %convolution_convert_fusion, bf16[8,1024,1024]{2,1,0:T(8,128)(2,1)} %divide_convert_fusion), kind=kOutput, calls=%fused_computation.11 | convolution fusion | flops 134217728 | bytes 33554688 | tf_op jit(solution)/shard_map/dot_general | solution.py:77
  198.6 0.0 copy-done.4
  198.6 0.1 fusion.17
  198.7 0.2 fusion.18
  198.9 16.4 %all-reduce = f32[8,8]{1,0:T(8,128)S(1)} all-reduce(f32[8,8]{1,0:T(8,128)S(1)} %fusion.18), channel_id=5, replica_groups=mesh['section'=4,'dp'=8] {'dp'}, use_global_device_ids=true, to_apply=%region_0.1.clone | all-reduce | flops 64 | bytes 512
  215.3 0.6 dynamic-slice_bitcast_fusion
  215.9 7.9 %all-gather.3 = f32[4,1,8]{2,1,0:T(1,128)S(1)} all-gather(f32[1,1,8]{2,1,0:T(1,128)S(1)} %dynamic-slice_bitcast_fusion), channel_id=4, replica_groups=mesh['section'=4,'dp'=8] {'section'}, dimensions={0}, use_global_device_ids=true | all-gather | bytes 160 | tf_op jit(solution)/shard_map/all_gather | solution.py:92
  223.9 0.6 multiply_reduce_fusion
  (9 shorter events, 0.0 us)
Async XLA Ops:
  6.5 106.2 %copy-start = (bf16[1,8,32,1024]{3,2,1,0:T(8,128)(2,1)S(1)}, bf16[1,8,32,1024]{3,2,1,0:T(8,128)(2,1)}, u32[]{:S(2)}) copy-start(bf16[1,8,32,1024]{3,2,1,0:T(8,128)(2,1)} %param.15) | copy-start | bytes 1572868
  6.5 51.6 %all-gather.9.cloned.1.call-start = ((), (), s32[]{:S(2)}) async-start(), calls=%async_computation.2 | async-start | bytes 2359296 | tf_op jit(solution)/shard_map/all_gather | solution.py:30
  11.3 46.8 %copy-start.2 = (bf16[1,128,1024]{2,1,0:T(8,128)(2,1)S(1)}, bf16[1,128,1024]{2,1,0:T(8,128)(2,1)}, u32[]{:S(2)}) copy-start(bf16[1,128,1024]{2,1,0:T(8,128)(2,1)} %param.10) | copy-start | bytes 786436
  11.3 109.6 %all-to-all-start = ((bf16[128,8,1024]{0,2,1:T(8,128)(2,1)}), bf16[128,8,1024]{0,2,1:T(8,128)(2,1)S(1)}, u32[]{:S(2)}, u32[]{:S(2)}) async-start(bf16[128,8,1024]{0,2,1:T(8,128)(2,1)} %bitcast.41), calls=%async_computation | async-start | bytes 4194304 | tf_op jit(solution)/shard_map/all_to_all | solution.py:37
  17.8 43.1 %copy-start.6 = (u32[32]{0:T(128)S(1)}, u32[32]{0:T(128)}, u32[]{:S(2)}) copy-start(u32[32]{0:T(128)} %constant.35) | copy-start | bytes 388
  17.8 43.7 %copy-start.3 = (bf16[1,1,32,1024]{3,2,1,0:T(8,128)(2,1)S(1)}, bf16[1,1,32,1024]{3,2,1,0:T(8,128)(2,1)}, u32[]{:S(2)}) copy-start(bf16[1,1,32,1024]{3,2,1,0:T(8,128)(2,1)} %param.14) | copy-start | bytes 196612
  17.8 110.1 %all-gather.7.cloned.1.call-start = ((), (), s32[]{:S(2)}) async-start(), calls=%async_computation.1 | async-start | bytes 2359296 | tf_op jit(solution)/shard_map/all_gather | solution.py:36
  123.6 2.9 %copy-start.1 = (bf16[1,1024,256]{2,1,0:T(8,128)(2,1)S(1)}, bf16[1,1024,256]{2,1,0:T(8,128)(2,1)}, u32[]{:S(2)}) copy-start(bf16[1,1024,256]{2,1,0:T(8,128)(2,1)} %param.11) | copy-start | bytes 1572868
  138.6 60.0 %copy-start.4 = (s32[8]{0:T(128)S(1)}, s32[8]{0:T(128)}, u32[]{:S(2)}) copy-start(s32[8]{0:T(128)} %param.16) | copy-start | bytes 100
  138.6 60.1 %copy-start.5 = (s32[8]{0:T(128)S(1)}, s32[8]{0:T(128)}, u32[]{:S(2)}) copy-start(s32[8]{0:T(128)} %param.17) | copy-start | bytes 100
Sparse Core Ops, SparseCore 0:
  9.0 49.1 all-gather.8
  61.1 42.5 all-gather.6
where the time goes:
time: 232 us; the launch traced here: 231 us
  matrix products  82.6 us (36%)
  blocking collectives  71.4 us (31%)
  waiting for transfers between devices  41.1 us (18%)
  between operations  13.5 us (6%)
  local copies, waits for them, and re-layouts  11.5 us (5%)
  starting transfers between devices  6.5 us (3%)
  other arithmetic  4.73 us (2%)
    dot_general x1, matrix products, on_device(): lax.dot_general(scaled, query_mats, (((1,), (1,)), ((), ())), preferred_e...  60 us
    all_gather x1, blocking collectives, on_device(): lax.all_gather(left_factors[0], 'dp', axis=0, tiled=True)  47.1 us
    all_gather x1, waiting for transfers between devices, on_device(): lax.all_gather(out_basis[0], 'dp', axis=0, tiled=True)  40.3 us
    unnamed x1, blocking collectives  16.4 us
    dot_general x1, matrix products, rescale(): jnp.einsum('nti,ntj->nij', operands[0], operands[1], preferred_element_ty...  10.7 us
    dot_general x1, matrix products, expand(): jnp.einsum('qri,qrj->qij', operands[0], operands[1], preferred_element_ty...  8.11 us
    all_gather x1, blocking collectives, on_device(): lax.all_gather(layer_part[None], 'section', axis=0, tiled=True)  7.93 us
    all_to_all x1, starting transfers between devices, on_device(): lax.all_to_all(layer_acts, 'dp', split_axis=1, concat_axis=0, tiled=True)  6.46 us
  transfers between devices with their start and end apart: 3, of which 1 were waited for; matrix products, arithmetic and copies ran while one was open for 11% of the time, Pallas kernels for 0%

commit v1 on v0

v1 whole, which is shorter than its diff:
```python
import functools

import jax
import jax.numpy as jnp
from jax import lax
from jax.experimental import pallas as pl
from jax.experimental.pallas import tpu as pltpu
from jax.sharding import PartitionSpec as P

SEQ_LEN = 128
VMEM_BYTES = 56 * 2**20
F32 = jnp.float32
BF16 = jnp.bfloat16


def contract(a, b, dim_a, dim_b):
    return lax.dot_general(a, b, (((dim_a,), (dim_b,)), ((), ())), preferred_element_type=F32)


def rotate_kernel(count, sizes, place, *refs):
    pieces = refs[:count]
    grads_out, left_out, basis, grads, left, sem = refs[count:]
    copies = []
    for j in range(count):
        first = 0
        for part, (rows, buffer) in enumerate(zip(sizes, (basis, grads, left))):
            at = pl.multiple_of(place[j] * rows, rows)
            copies.append(
                pltpu.make_async_copy(
                    pieces[j].at[pl.ds(first, rows)], buffer.at[pl.ds(at, rows)], sem.at[part, j]
                )
            )
            first += rows
    for copy in copies:
        copy.start()
    for copy in copies:
        copy.wait()
    left_out[...] = left[...].T
    rows = sizes[1]

    def body(j, carry):
        own = pl.ds(pl.multiple_of(j * rows, rows), rows)
        grads_out[own, :] = contract(grads[own, :], basis[...], 1, 0).astype(BF16)
        return carry

    lax.fori_loop(0, count, body, 0)


def rotate_grads(place, pieces, sizes):
    count = len(pieces)
    width = pieces[0].shape[1]
    basis_rows, grad_rows, left_rows = (count * rows for rows in sizes)
    return pl.pallas_call(
        functools.partial(rotate_kernel, count, sizes),
        out_shape=(
            jax.ShapeDtypeStruct((grad_rows, width), BF16),
            jax.ShapeDtypeStruct((width, left_rows), BF16),
        ),
        in_specs=[pl.BlockSpec(memory_space=pltpu.SMEM)]
        + [pl.BlockSpec(memory_space=pl.ANY)] * count,
        out_specs=[pl.BlockSpec(memory_space=pltpu.VMEM)] * 2,
        scratch_shapes=[
            pltpu.VMEM((basis_rows, width), BF16),
            pltpu.VMEM((grad_rows, width), BF16),
            pltpu.VMEM((left_rows, width), BF16),
            pltpu.SemaphoreType.DMA((3, count)),
        ],
        compiler_params=pltpu.CompilerParams(vmem_limit_bytes=VMEM_BYTES),
        cost_estimate=pl.CostEstimate(
            flops=2 * grad_rows * basis_rows * width,
            bytes_accessed=2 * (basis_rows + 2 * grad_rows + 2 * left_rows) * width,
            transcendentals=0,
        ),
    )(place, *pieces)


def score_kernel(count, seq, *refs):
    acts, grads = refs[:count], refs[count : 2 * count]
    basis, curvature, right, left, out, rotated = refs[2 * count :]
    columns, size = basis.shape

    @pl.when(pl.program_id(0) == 0)
    def _():
        for q in range(count):
            for b in range(columns // size):
                own = slice(b * size, (b + 1) * size)
                rotated[q, :, own] = contract(acts[q][:, own], basis[own, :], 1, 0).astype(BF16)
        out[...] = jnp.zeros_like(out)

    inverse = 1.0 / curvature[...].astype(F32)
    weights = left[...].astype(F32)
    for q in range(count):
        scaled = (contract(grads[q][...], rotated[q], 0, 0) * inverse).astype(BF16)
        terms = contract(scaled, right[...], 1, 1) * weights
        out[q] += jnp.sum(terms.reshape(terms.shape[0] // 8, 8, terms.shape[1]), axis=0)


def score(sequences, acts, grads, basis, curvature, right, left):
    count = len(acts)
    width, columns = curvature.shape
    ranks = right.shape[0]
    block = min(width, 512)

    def whole(shape):
        return pl.BlockSpec(shape, lambda i, seq: (0, 0))

    def rows_of(at):
        return pl.BlockSpec((SEQ_LEN, columns), lambda i, seq: (at, 0))

    def grads_of(q):
        return pl.BlockSpec((SEQ_LEN, block), lambda i, seq: (seq[q], i))

    return pl.pallas_call(
        functools.partial(score_kernel, count),
        out_shape=jax.ShapeDtypeStruct((count, 8, ranks), F32),
        grid_spec=pltpu.PrefetchScalarGridSpec(
            num_scalar_prefetch=1,
            grid=(width // block,),
            in_specs=[rows_of(at) for _, at in acts]
            + [grads_of(q) for q in range(count)]
            + [
                whole(basis.shape),
                pl.BlockSpec((block, columns), lambda i, seq: (i, 0)),
                whole(right.shape),
                pl.BlockSpec((block, ranks), lambda i, seq: (i, 0)),
            ],
            out_specs=pl.BlockSpec((count, 8, ranks), lambda i, seq: (0, 0, 0)),
            scratch_shapes=[pltpu.VMEM((count, SEQ_LEN, columns), BF16)],
        ),
        compiler_params=pltpu.CompilerParams(vmem_limit_bytes=VMEM_BYTES),
        cost_estimate=pl.CostEstimate(
            flops=2 * count * width * columns * (SEQ_LEN + ranks),
            bytes_accessed=2 * (width * columns + count * SEQ_LEN * (width + columns)),
            transcendentals=0,
        ),
    )(sequences, *[array for array, _ in acts], *([grads] * count), basis, curvature, right, left)


def swap(x, k, n):
    return lax.ppermute(x, "dp", [(i, i ^ k) for i in range(n)])


def hop(x, pairs):
    return lax.ppermute(x, "dp", [(2 * a + c, 2 * b + c) for a, b in pairs for c in range(2)])


def gather_line(mine, me):
    chip = me // 2
    inner = (chip == 1) | (chip == 2)
    second_in = hop(mine, [(1, 2), (2, 1)])
    third_in = hop(mine, [(0, 2), (3, 1)])
    first = hop(mine, [(0, 1), (1, 0), (2, 3), (3, 2)])
    second_end = hop(second_in, [(2, 3), (1, 0)])
    third_end = hop(third_in, [(2, 3), (1, 0)])
    second = jnp.where(inner, second_in, second_end)
    third = jnp.where(inner, third_in, third_end)
    near, far = chip ^ 2, chip ^ 3
    chips = jnp.stack(
        [chip, chip ^ 1, jnp.where(inner, far, near), jnp.where(inner, near, far)]
    ).astype(jnp.int32)
    own = [mine, first, second, third]
    other = [swap(x, 1, 8) for x in own]
    core = me % 2
    return own + other, jnp.concatenate([2 * chips + core, 2 * chips + 1 - core])


def on_device(n, activations, out_grads, in_basis, out_basis, curvature, left_factors, right_factors,
              sequence_ids, query_order):
    me = lax.axis_index("dp")
    acts = activations[0]
    columns = in_basis.shape[1]
    width = out_basis.shape[2]
    left_own = left_factors[0].reshape(-1, width)
    sizes = (out_basis.shape[1], out_grads.shape[1], left_own.shape[0])
    mine = jnp.concatenate([out_basis[0], out_grads[0], left_own])
    if n == 8:
        pieces, place = gather_line(mine, me)
    else:
        every = lax.all_gather(mine, "dp", axis=0)
        pieces, place = [every[j] for j in range(n)], jnp.arange(n, dtype=jnp.int32)
    grads, left = rotate_grads(place, pieces, sizes)

    each = acts.shape[0] // SEQ_LEN
    right = right_factors[0].reshape(-1, columns)
    if n & (n - 1) == 0 and n <= 8:
        parts = [
            lax.dynamic_slice(acts, (0, (me ^ k) * columns), (acts.shape[0], columns))
            for k in range(n)
        ]
        parts = parts[:1] + [swap(parts[k], k, n) for k in range(1, n)]
        operands = [(part, j) for part in parts for j in range(each)]
        owners = jnp.stack([me ^ k for k in range(n)])
    else:
        part = lax.all_to_all(acts, "dp", split_axis=1, concat_axis=0, tiled=True)
        operands = [(part, j) for j in range(n * each)]
        owners = jnp.arange(n, dtype=jnp.int32)
    sequences = (owners[:, None] * each + jnp.arange(each)[None, :]).reshape(-1).astype(jnp.int32)
    step = min(len(operands), 4)
    sums = []
    for at in range(0, len(operands), step):
        sums.append(
            score(sequences[at : at + step], operands[at : at + step], grads, in_basis[0],
                  curvature[0], right, left)
        )
    sums = jnp.concatenate(sums)
    seqs = sums.shape[0]
    queries = right_factors.shape[1]
    scores = jnp.sum(sums.reshape(seqs, 8, queries, -1), axis=(1, 3))

    rows = jnp.sum(
        jnp.where(jnp.arange(seqs)[None, :, None] == sequences[:, None, None],
                  sequence_ids[None, :, None], 0), axis=1)
    row_pick = (rows.reshape(1, seqs) == jnp.arange(seqs)[:, None]).astype(F32)
    col_pick = (query_order[:, None] == jnp.arange(queries)[None, :]).astype(F32)
    placed = jnp.dot(jnp.dot(row_pick, scores, precision=lax.Precision.HIGHEST), col_pick,
                     precision=lax.Precision.HIGHEST)
    layers = lax.axis_size("section")
    wanted = jnp.arange(layers) <= lax.axis_index("section")
    outgoing = jnp.where(wanted[:, None, None], placed[None], 0.0)
    outgoing = outgoing.reshape(layers * n, seqs // n, queries)
    arrived = lax.all_to_all(outgoing, ("section", "dp"), split_axis=0, concat_axis=0, tiled=True)
    return jnp.sum(arrived, axis=0)[None]


def solution(mesh):
    placed = (
        P("section", "dp", None),
        P("section", "dp", None),
        P("section", "dp", None),
        P("section", "dp", None),
        P("section", None, "dp"),
        P("section", "dp", None, None),
        P("section", None, None, "dp"),
        P(),
        P(),
    )
    return jax.shard_map(
        functools.partial(on_device, mesh.shape["dp"]), mesh=mesh, in_specs=placed,
        out_specs=P("section", "dp", None), check_vma=False,
    )
```

time: 232 us -> 135 us (0.58)
  matrix products: 82.6 us -> 0.31 us
  blocking collectives: 71.4 us -> 21.9 us
  Pallas kernels: 0 us -> 26.6 us
  waiting for transfers between devices: 41.1 us -> 57.1 us
  between operations: 13.5 us -> 0.34 us
  starting transfers between devices: 6.5 us -> 19 us
  local copies, waits for them, and re-layouts: 11.5 us -> 4.84 us
    dot_general x5 -> x0, matrix products: 82.2 us -> none  [the longest x1 60 us: on_device(): lax.dot_general(scaled, query_mats, (((1,), (1,)), ((), ())), preferred_e...]
    ppermute x0 -> x16, waiting for transfers between devices: none -> 57.1 us  [the longest x5 43.8 us: hop(): lax.ppermute(x, 'dp', [(2 * a + c, 2 * b + c) for a, b in pairs for c in...]
    all_gather x2 -> x0, blocking collectives: 55 us -> none  [the longest x1 47.1 us: on_device(): lax.all_gather(left_factors[0], 'dp', axis=0, tiled=True)]
    all_gather x2 -> x0, waiting for transfers between devices: 40.3 us -> none  [the longest x1 40.3 us: on_device(): lax.all_gather(out_basis[0], 'dp', axis=0, tiled=True)]
    pallas_call x0 -> x3, Pallas kernels: none -> 26.6 us  [the longest x2 18.3 us: score(): pl.pallas_call(functools.partial(score_kernel, count), out_shape=jax.Shap...]
    all_to_all x0 -> x1, blocking collectives: none -> 21.9 us  [on_device(): lax.all_to_all(outgoing, ('section', 'dp'), split_axis=0, concat_axis=0,...]
    ppermute x0 -> x16, starting transfers between devices: none -> 19 us  [the longest x5 11 us: hop(): lax.ppermute(x, 'dp', [(2 * a + c, 2 * b + c) for a, b in pairs for c in...]
    unnamed x1 -> x0, blocking collectives: 16.4 us -> none
  transfers between devices with their start and end apart: 3 -> 16, of which waited for: 1 -> 7; matrix products, arithmetic and copies ran while one was open for 11% -> 4% of each run, Pallas kernels for 0% -> 13%
where the time goes in v1:
time: 135 us; the launch traced here: 134 us
  waiting for transfers between devices  57.1 us (42%)
  Pallas kernels  26.6 us (20%)
  blocking collectives  21.9 us (16%)
  starting transfers between devices  19 us (14%)
  local copies, waits for them, and re-layouts  4.84 us (4%)
  other arithmetic  4.23 us (3%)
    ppermute x5, waiting for transfers between devices, hop(): lax.ppermute(x, 'dp', [(2 * a + c, 2 * b + c) for a, b in pairs for c in...  43.8 us
    all_to_all x1, blocking collectives, on_device(): lax.all_to_all(outgoing, ('section', 'dp'), split_axis=0, concat_axis=0,...  21.9 us
    pallas_call x2, Pallas kernels, score(): pl.pallas_call(functools.partial(score_kernel, count), out_shape=jax.Shap...  18.3 us
    ppermute x11, waiting for transfers between devices, swap(): return lax.ppermute(x, 'dp', [(i, i ^ k) for i in range(n)])  13.3 us
    ppermute x5, starting transfers between devices, hop(): lax.ppermute(x, 'dp', [(2 * a + c, 2 * b + c) for a, b in pairs for c in...  11 us
    pallas_call x1, Pallas kernels, rotate_grads(): pl.pallas_call(functools.partial(rotate_kernel, count, sizes), out_shape=...  8.32 us
    ppermute x11, starting transfers between devices, swap(): return lax.ppermute(x, 'dp', [(i, i ^ k) for i in range(n)])  8 us
    dynamic_slice x1, local copies, waits for them, and re-layouts, on_device(): lax.dynamic_slice(acts, (0, (me ^ k) * columns), (acts.shape[0], columns))  2.89 us
  transfers between devices with their start and end apart: 16, of which 7 were waited for; matrix products, arithmetic and copies ran while one was open for 4% of the time, Pallas kernels for 13%

profile of v1, /device:TPU:0, one launch (start us, length us, event | category | flops | bytes accessed | tf_op | source)
XLA Modules:
  0.0 134.3 jit_solution(4339992611000164849)
XLA Ops:
  0.0 1.1 pad_maximum_fusion.refs_0_
  1.1 0.7 collective-permute-start.4
  1.8 7.6 %collective-permute-start.6 = (bf16[288,1024]{1,0:T(8,128)(2,1)S(1)}, bf16[288,1024]{1,0:T(8,128)(2,1)S(1)}, u32[]{:S(2)}, u32[]{:S(2)}) collective-permute-start(bf16[288,1024]{1,0:T(8,128)(2,1)S(1)} %pad_maximum_fusion.refs_0_), channel_id=1, source_target_pairs={{0,4},{1,5},{6,2},{7,3},{8,12},{9,13},{14,10},{15,11},{16,20},{17,... | collective-permute-start | bytes 1769480 | tf_op jit(solution)/shard_map/ppermute | solution.py:144
  9.6 1.3 collective-permute-start.5
  10.9 12.3 %collective-permute-done.6 = bf16[288,1024]{1,0:T(8,128)(2,1)S(1)} collective-permute-done((bf16[288,1024]{1,0:T(8,128)(2,1)S(1)}, bf16[288,1024]{1,0:T(8,128)(2,1)S(1)}, u32[]{:S(2)}, u32[]{:S(2)}) %collective-permute-start.6) | collective-permute-done | bytes 589856 | tf_op jit(solution)/shard_map/ppermute | solution.py:144
  23.2 1.3 collective-permute-start.7
  24.6 2.9 %dynamic-slice_bitcast_fusion.4 = (bf16[128,1024]{1,0:T(8,128)(2,1)}, bf16[128,1024]{1,0:T(8,128)(2,1)}, bf16[128,1024]{1,0:T(8,128)(2,1)}, bf16[128,1024]{1,0:T...) fusion(bf16[1,128,8192]{2,1,0:T(8,128)(2,1)} %param.9, ...), kind=kLoop, calls=%fused_computation.7 | loop fusion | bytes 4194336 | tf_op jit(solution)/shard_map/dynamic_slice | solution.py:187
  27.5 0.5 collective-permute-start
  28.0 0.6 pad_add_fusion
  28.6 5.8 %collective-permute-done.3.refs_1_ = bf16[288,1024]{1,0:T(8,128)(2,1)} collective-permute-done((bf16[288,1024]{1,0:T(8,128)(2,1)S(1)}, bf16[288,1024]{1,0:T(8,128)(2,1)}, u32[]{:S(2)}, u32[]{:S(2)}) %collective-permute-start.3) | collective-permute-done | bytes 589856 | tf_op jit(solution)/shard_map/ppermute | solution.py:144
  34.4 14.8 %collective-permute-done.5 = bf16[288,1024]{1,0:T(8,128)(2,1)S(1)} collective-permute-done((bf16[288,1024]{1,0:T(8,128)(2,1)S(1)}, bf16[288,1024]{1,0:T(8,128)(2,1)S(1)}, u32[]{:S(2)}, u32[]{:S(2)}) %collective-permute-start.5) | collective-permute-done | bytes 589856 | tf_op jit(solution)/shard_map/ppermute | solution.py:144
  49.4 10.8 %collective-permute-done.7 = bf16[288,1024]{1,0:T(8,128)(2,1)S(1)} collective-permute-done((bf16[288,1024]{1,0:T(8,128)(2,1)S(1)}, bf16[288,1024]{1,0:T(8,128)(2,1)S(1)}, u32[]{:S(2)}, u32[]{:S(2)}) %collective-permute-start.7) | collective-permute-done | bytes 589856 | tf_op jit(solution)/shard_map/ppermute | solution.py:144
  60.7 0.2 select_reduce_fusion
  61.0 1.8 %collective-permute-start.2 = (bf16[128,1024]{1,0:T(8,128)(2,1)}, bf16[128,1024]{1,0:T(8,128)(2,1)S(1)}, u32[]{:S(2)}, u32[]{:S(2)}) collective-permute-start(bf16[128,1024]{1,0:T(8,128)(2,1)} %get-tuple-element.11), channel_id=1, source_target_pairs={{0,3},{1,2},{2,1},{3,0},{4,7},{5,6},{6,5},{7,4},{8,11},{9,10},{10,... | collective-permute-start | bytes 786440 | tf_op jit(solution)/shard_map/ppermute | solution.py:140
  62.8 0.6 pad_add_fusion.1.place
  63.4 1.4 %collective-permute-start.12 = (bf16[128,1024]{1,0:T(8,128)(2,1)S(1)}, bf16[128,1024]{1,0:T(8,128)(2,1)S(1)}, u32[]{:S(2)}, u32[]{:S(2)}) collective-permute-start(bf16[128,1024]{1,0:T(8,128)(2,1)S(1)} %copy-done.6), channel_id=1, source_target_pairs={{0,4},{1,5},{2,6},{3,7},{4,0},{5,1},{6,2},{7,3},{8,12},{9,13},{10,... | collective-permute-start | bytes 786440 | tf_op jit(solution)/shard_map/ppermute | solution.py:140
  64.8 1.3 collective-permute-start.13
  66.1 8.3 %shard_map.91 = (bf16[1024,1024]{1,0:T(8,128)(2,1)}, bf16[1024,256]{1,0:T(8,128)(2,1)}) custom-call(s32[8]{0:T(128)} %pad_add_fusion.1.place, bf16[288,1024]{1,0:T(8,128)(2,1)} %copy-done, bf16[288,1024]{1,0:T(8,128)(2,1)} %collective-permute-done.3.refs_1_, bf16[288,1024]{1,0:T(8,128)(2,1)} %copy-done.1, bf16[288,1024]{1,0:T(8,128)(2,1)} %copy-done.2, ...), custom_call_target="tpu_custom_call" | custom-call | flops 2147483648 | bytes 7340032 | tf_op jit(solution)/shard_map/pallas_call | solution.py:53
  74.4 2.6 %collective-permute-start.14 = (bf16[128,1024]{1,0:T(8,128)(2,1)S(1)}, bf16[128,1024]{1,0:T(8,128)(2,1)S(1)}, u32[]{:S(2)}, u32[]{:S(2)}) collective-permute-start(bf16[128,1024]{1,0:T(8,128)(2,1)S(1)} %copy-done.4), channel_id=1, source_target_pairs={{0,6},{1,7},{2,4},{3,5},{4,2},{5,3},{6,0},{7,1},{8,14},{9,15},{10,... | collective-permute-start | bytes 786440 | tf_op jit(solution)/shard_map/ppermute | solution.py:140
  77.0 2.3 %collective-permute-done.1.refs_2_ = bf16[128,1024]{1,0:T(8,128)(2,1)S(1)} collective-permute-done((bf16[128,1024]{1,0:T(8,128)(2,1)}, bf16[128,1024]{1,0:T(8,128)(2,1)S(1)}, u32[]{:S(2)}, u32[]{:S(2)}) %collective-permute-start.1) | collective-permute-done | bytes 262176 | tf_op jit(solution)/shard_map/ppermute | solution.py:140
  79.4 0.2 collective-permute-start.15
  79.6 4.5 %collective-permute-done.2.refs_3_ = bf16[128,1024]{1,0:T(8,128)(2,1)S(1)} collective-permute-done((bf16[128,1024]{1,0:T(8,128)(2,1)}, bf16[128,1024]{1,0:T(8,128)(2,1)S(1)}, u32[]{:S(2)}, u32[]{:S(2)}) %collective-permute-start.2) | collective-permute-done | bytes 262176 | tf_op jit(solution)/shard_map/ppermute | solution.py:140
  84.1 0.7 copy-done.10
  84.8 9.1 %shard_map.92 = f32[4,8,256]{2,1,0:T(8,128)} custom-call(s32[4]{0:T(128)} %get-tuple-element.19.seq, bf16[128,1024]{1,0:T(8,128)(2,1)} %get-tuple-element.16.refs_0_, bf16[128,1024]{1,0:T(8,128)(2,1)} %collective-permute-done.refs_1_, bf16[128,1024]{1,0:T(8,128)(2,1)} %copy-done.8, bf16[128,1024]{1,0:T(8,128)(2,1)} %copy-done.10, ...), custom_call_target="tpu_custom_call" | custom-call | flops 3221225472 | bytes 4194304 | tf_op jit(solution)/shard_map/pallas_call | solution.py:113
  93.9 6.4 %collective-permute-done.13.refs_1_ = bf16[128,1024]{1,0:T(8,128)(2,1)S(1)} collective-permute-done((bf16[128,1024]{1,0:T(8,128)(2,1)S(1)}, bf16[128,1024]{1,0:T(8,128)(2,1)S(1)}, u32[]{:S(2)}, u32[]{:S(2)}) %collective-permute-start.13) | collective-permute-done | bytes 262176 | tf_op jit(solution)/shard_map/ppermute | solution.py:140
  100.4 0.7 copy-done.9
  101.3 9.2 %shard_map.93 = f32[4,8,256]{2,1,0:T(8,128)} custom-call(s32[4]{0:T(128)} %get-tuple-element.20.seq, bf16[128,1024]{1,0:T(8,128)(2,1)} %copy-done.7, bf16[128,1024]{1,0:T(8,128)(2,1)} %copy-done.9, bf16[128,1024]{1,0:T(8,128)(2,1)} %copy-done.11, bf16[128,1024]{1,0:T(8,128)(2,1)} %copy-done.12, ...), custom_call_target="tpu_custom_call" | custom-call | flops 3221225472 | bytes 4194304 | tf_op jit(solution)/shard_map/pallas_call | solution.py:113
  110.5 0.8 maximum_reduce_fusion
  111.4 0.1 fusion
  111.6 0.2 fusion.1
  111.9 21.9 %all_to_all.5 = f32[32,1,8]{2,1,0:T(1,128)S(1)} all-to-all(f32[32,1,8]{2,1,0:T(1,128)S(1)} %broadcast_select_fusion.2), channel_id=1, replica_groups=mesh['section'=4,'dp'=8] {'section','dp'}, dimensions={0} | all-to-all | bytes 2048 | tf_op jit(solution)/shard_map/all_to_all | solution.py:221
  133.7 0.6 reduce_sum.38
  (59 shorter events, 1.4 us)
Async XLA Ops:
  1.1 26.4 %copy-start = (bf16[288,1024]{1,0:T(8,128)(2,1)}, bf16[288,1024]{1,0:T(8,128)(2,1)S(1)}, u32[]{:S(2)}) copy-start(bf16[288,1024]{1,0:T(8,128)(2,1)S(1)} %pad_maximum_fusion.refs_0_) | copy-start | bytes 1769476
  1.1 8.4 %collective-permute-start.4 = (bf16[288,1024]{1,0:T(8,128)(2,1)S(1)}, bf16[288,1024]{1,0:T(8,128)(2,1)S(1)}, u32[]{:S(2)}, u32[]{:S(2)}) collective-permute-start(bf16[288,1024]{1,0:T(8,128)(2,1)S(1)} %pad_maximum_fusion.refs_0_), channel_id=1, source_target_pairs={{2,4},{3,5},{4,2},{5,3},{10,12},{11,13},{12,10},{13,11},{18,20},{1... | collective-permute-start | bytes 1769480 | tf_op jit(solution)/shard_map/ppermute | solution.py:144
  1.8 21.4 %collective-permute-start.6 = (bf16[288,1024]{1,0:T(8,128)(2,1)S(1)}, bf16[288,1024]{1,0:T(8,128)(2,1)S(1)}, u32[]{:S(2)}, u32[]{:S(2)}) collective-permute-start(bf16[288,1024]{1,0:T(8,128)(2,1)S(1)} %pad_maximum_fusion.refs_0_), channel_id=1, source_target_pairs={{0,4},{1,5},{6,2},{7,3},{8,12},{9,13},{14,10},{15,11},{16,20},{17,... | collective-permute-start | bytes 1769480 | tf_op jit(solution)/shard_map/ppermute | solution.py:144
  9.5 24.9 %collective-permute-start.3 = (bf16[288,1024]{1,0:T(8,128)(2,1)S(1)}, bf16[288,1024]{1,0:T(8,128)(2,1)}, u32[]{:S(2)}, u32[]{:S(2)}) collective-permute-start(bf16[288,1024]{1,0:T(8,128)(2,1)S(1)} %pad_maximum_fusion.refs_0_), channel_id=1, source_target_pairs={{0,2},{1,3},{2,0},{3,1},{4,6},{5,7},{6,4},{7,5},{8,10},{9,11},{10,... | collective-permute-start | bytes 1769480 | tf_op jit(solution)/shard_map/ppermute | solution.py:144
  9.6 39.7 %collective-permute-start.5 = (bf16[288,1024]{1,0:T(8,128)(2,1)S(1)}, bf16[288,1024]{1,0:T(8,128)(2,1)S(1)}, u32[]{:S(2)}, u32[]{:S(2)}) collective-permute-start(bf16[288,1024]{1,0:T(8,128)(2,1)S(1)} %collective-permute-done.4), channel_id=1, source_target_pairs={{4,6},{5,7},{2,0},{3,1},{12,14},{13,15},{10,8},{11,9},{20,22},{21,... | collective-permute-start | bytes 1769480 | tf_op jit(solution)/shard_map/ppermute | solution.py:144
  23.2 37.0 %collective-permute-start.7 = (bf16[288,1024]{1,0:T(8,128)(2,1)S(1)}, bf16[288,1024]{1,0:T(8,128)(2,1)S(1)}, u32[]{:S(2)}, u32[]{:S(2)}) collective-permute-start(bf16[288,1024]{1,0:T(8,128)(2,1)S(1)} %collective-permute-done.6), channel_id=1, source_target_pairs={{4,6},{5,7},{2,0},{3,1},{12,14},{13,15},{10,8},{11,9},{20,22},{21,... | collective-permute-start | bytes 1769480 | tf_op jit(solution)/shard_map/ppermute | solution.py:144
  24.5 36.4 %collective-permute-start.8 = (bf16[288,1024]{1,0:T(8,128)(2,1)S(1)}, bf16[288,1024]{1,0:T(8,128)(2,1)}, u32[]{:S(2)}, u32[]{:S(2)}) collective-permute-start(bf16[288,1024]{1,0:T(8,128)(2,1)S(1)} %pad_maximum_fusion.refs_0_), channel_id=1, source_target_pairs={{0,1},{1,0},{2,3},{3,2},{4,5},{5,4},{6,7},{7,6},{8,9},{9,8},{10,11... | collective-permute-start | bytes 1769480 | tf_op jit(solution)/shard_map/ppermute | solution.py:140
  27.5 46.9 %collective-permute-start = (bf16[128,1024]{1,0:T(8,128)(2,1)}, bf16[128,1024]{1,0:T(8,128)(2,1)}, u32[]{:S(2)}, u32[]{:S(2)}) collective-permute-start(bf16[128,1024]{1,0:T(8,128)(2,1)} %get-tuple-element.15), channel_id=1, source_target_pairs={{0,1},{1,0},{2,3},{3,2},{4,5},{5,4},{6,7},{7,6},{8,9},{9,8},{10,11... | collective-permute-start | bytes 786440 | tf_op jit(solution)/shard_map/ppermute | solution.py:140
  34.4 26.6 %collective-permute-start.9 = (bf16[288,1024]{1,0:T(8,128)(2,1)}, bf16[288,1024]{1,0:T(8,128)(2,1)}, u32[]{:S(2)}, u32[]{:S(2)}) collective-permute-start(bf16[288,1024]{1,0:T(8,128)(2,1)} %collective-permute-done.3.refs_1_), channel_id=1, source_target_pairs={{0,1},{1,0},{2,3},{3,2},{4,5},{5,4},{6,7},{7,6},{8,9},{9,8},{10,11... | collective-permute-start | bytes 1769480 | tf_op jit(solution)/shard_map/ppermute | solution.py:140
  49.3 16.8 %copy-start.1 = (bf16[288,1024]{1,0:T(8,128)(2,1)}, bf16[288,1024]{1,0:T(8,128)(2,1)S(1)}, u32[]{:S(2)}) copy-start(bf16[288,1024]{1,0:T(8,128)(2,1)S(1)} %broadcast_select_fusion.1.refs_2_) | copy-start | bytes 1769476
  49.3 11.4 %copy-start.15 = (s32[8]{0:T(128)S(1)}, s32[8]{0:T(128)}, u32[]{:S(2)}) copy-start(s32[8]{0:T(128)} %param.16) | copy-start | bytes 100
  49.3 14.1 %copy-start.6 = (bf16[128,1024]{1,0:T(8,128)(2,1)S(1)}, bf16[128,1024]{1,0:T(8,128)(2,1)}, u32[]{:S(2)}) copy-start(bf16[128,1024]{1,0:T(8,128)(2,1)} %get-tuple-element.13) | copy-start | bytes 786436
  49.4 15.4 %copy-start.5 = (bf16[128,1024]{1,0:T(8,128)(2,1)S(1)}, bf16[128,1024]{1,0:T(8,128)(2,1)}, u32[]{:S(2)}) copy-start(bf16[128,1024]{1,0:T(8,128)(2,1)} %get-tuple-element.12) | copy-start | bytes 786436
  49.4 14.0 %collective-permute-start.10 = (bf16[288,1024]{1,0:T(8,128)(2,1)S(1)}, bf16[288,1024]{1,0:T(8,128)(2,1)}, u32[]{:S(2)}, u32[]{:S(2)}) collective-permute-start(bf16[288,1024]{1,0:T(8,128)(2,1)S(1)} %broadcast_select_fusion.1.refs_2_), channel_id=1, source_target_pairs={{0,1},{1,0},{2,3},{3,2},{4,5},{5,4},{6,7},{7,6},{8,9},{9,8},{10,11... | collective-permute-start | bytes 1769480 | tf_op jit(solution)/shard_map/ppermute | solution.py:140
  60.3 5.8 %copy-start.2 = (bf16[288,1024]{1,0:T(8,128)(2,1)}, bf16[288,1024]{1,0:T(8,128)(2,1)S(1)}, u32[]{:S(2)}) copy-start(bf16[288,1024]{1,0:T(8,128)(2,1)S(1)} %broadcast_select_fusion.refs_3_) | copy-start | bytes 1769476
  60.3 4.5 %collective-permute-start.11 = (bf16[288,1024]{1,0:T(8,128)(2,1)S(1)}, bf16[288,1024]{1,0:T(8,128)(2,1)S(1)}, u32[]{:S(2)}, u32[]{:S(2)}) collective-permute-start(bf16[288,1024]{1,0:T(8,128)(2,1)S(1)} %broadcast_select_fusion.refs_3_), channel_id=1, source_target_pairs={{0,1},{1,0},{2,3},{3,2},{4,5},{5,4},{6,7},{7,6},{8,9},{9,8},{10,11... | collective-permute-start | bytes 1769480 | tf_op jit(solution)/shard_map/ppermute | solution.py:140
  60.9 18.4 %collective-permute-start.1 = (bf16[128,1024]{1,0:T(8,128)(2,1)}, bf16[128,1024]{1,0:T(8,128)(2,1)S(1)}, u32[]{:S(2)}, u32[]{:S(2)}) collective-permute-start(bf16[128,1024]{1,0:T(8,128)(2,1)} %get-tuple-element.14), channel_id=1, source_target_pairs={{0,2},{1,3},{2,0},{3,1},{4,6},{5,7},{6,4},{7,5},{8,10},{9,11},{10,... | collective-permute-start | bytes 786440 | tf_op jit(solution)/shard_map/ppermute | solution.py:140
  61.0 23.1 %collective-permute-start.2 = (bf16[128,1024]{1,0:T(8,128)(2,1)}, bf16[128,1024]{1,0:T(8,128)(2,1)S(1)}, u32[]{:S(2)}, u32[]{:S(2)}) collective-permute-start(bf16[128,1024]{1,0:T(8,128)(2,1)} %get-tuple-element.11), channel_id=1, source_target_pairs={{0,3},{1,2},{2,1},{3,0},{4,7},{5,6},{6,5},{7,4},{8,11},{9,10},{10,... | collective-permute-start | bytes 786440 | tf_op jit(solution)/shard_map/ppermute | solution.py:140
  63.4 30.5 %collective-permute-start.12 = (bf16[128,1024]{1,0:T(8,128)(2,1)S(1)}, bf16[128,1024]{1,0:T(8,128)(2,1)S(1)}, u32[]{:S(2)}, u32[]{:S(2)}) collective-permute-start(bf16[128,1024]{1,0:T(8,128)(2,1)S(1)} %copy-done.6), channel_id=1, source_target_pairs={{0,4},{1,5},{2,6},{3,7},{4,0},{5,1},{6,2},{7,3},{8,12},{9,13},{10,... | collective-permute-start | bytes 786440 | tf_op jit(solution)/shard_map/ppermute | solution.py:140
  64.8 1.3 copy-start.14
  64.8 9.6 %copy-start.4 = (bf16[128,1024]{1,0:T(8,128)(2,1)S(1)}, bf16[128,1024]{1,0:T(8,128)(2,1)}, u32[]{:S(2)}) copy-start(bf16[128,1024]{1,0:T(8,128)(2,1)} %get-tuple-element.18) | copy-start | bytes 786436
  64.8 14.6 %copy-start.3 = (bf16[128,1024]{1,0:T(8,128)(2,1)S(1)}, bf16[128,1024]{1,0:T(8,128)(2,1)}, u32[]{:S(2)}) copy-start(bf16[128,1024]{1,0:T(8,128)(2,1)} %get-tuple-element.17) | copy-start | bytes 786436
  64.8 35.6 %collective-permute-start.13 = (bf16[128,1024]{1,0:T(8,128)(2,1)S(1)}, bf16[128,1024]{1,0:T(8,128)(2,1)S(1)}, u32[]{:S(2)}, u32[]{:S(2)}) collective-permute-start(bf16[128,1024]{1,0:T(8,128)(2,1)S(1)} %copy-done.5), channel_id=1, source_target_pairs={{0,5},{1,4},{2,7},{3,6},{4,1},{5,0},{6,3},{7,2},{8,13},{9,12},{10,... | collective-permute-start | bytes 786440 | tf_op jit(solution)/shard_map/ppermute | solution.py:140
  74.4 26.0 %collective-permute-start.14 = (bf16[128,1024]{1,0:T(8,128)(2,1)S(1)}, bf16[128,1024]{1,0:T(8,128)(2,1)S(1)}, u32[]{:S(2)}, u32[]{:S(2)}) collective-permute-start(bf16[128,1024]{1,0:T(8,128)(2,1)S(1)} %copy-done.4), channel_id=1, source_target_pairs={{0,6},{1,7},{2,4},{3,5},{4,2},{5,3},{6,0},{7,1},{8,14},{9,15},{10,... | collective-permute-start | bytes 786440 | tf_op jit(solution)/shard_map/ppermute | solution.py:140
  79.4 4.8 %copy-start.8 = (bf16[128,1024]{1,0:T(8,128)(2,1)}, bf16[128,1024]{1,0:T(8,128)(2,1)S(1)}, u32[]{:S(2)}) copy-start(bf16[128,1024]{1,0:T(8,128)(2,1)S(1)} %collective-permute-done.1.refs_2_) | copy-start | bytes 786436
  79.4 21.0 %collective-permute-start.15 = (bf16[128,1024]{1,0:T(8,128)(2,1)S(1)}, bf16[128,1024]{1,0:T(8,128)(2,1)S(1)}, u32[]{:S(2)}, u32[]{:S(2)}) collective-permute-start(bf16[128,1024]{1,0:T(8,128)(2,1)S(1)} %copy-done.3), channel_id=1, source_target_pairs={{0,7},{1,6},{2,5},{3,4},{4,3},{5,2},{6,1},{7,0},{8,15},{9,14},{10,... | collective-permute-start | bytes 786440 | tf_op jit(solution)/shard_map/ppermute | solution.py:140
  84.1 0.7 copy-start.10
  93.9 6.5 %copy-start.7 = (bf16[128,1024]{1,0:T(8,128)(2,1)}, bf16[128,1024]{1,0:T(8,128)(2,1)S(1)}, u32[]{:S(2)}) copy-start(bf16[128,1024]{1,0:T(8,128)(2,1)S(1)} %collective-permute-done.12.refs_0_) | copy-start | bytes 786436
  100.4 0.8 copy-start.11
  100.4 0.9 copy-start.12
  101.3 9.2 %copy-start.13 = (f32[4,8,256]{2,1,0:T(8,128)S(1)}, f32[4,8,256]{2,1,0:T(8,128)}, u32[]{:S(2)}) copy-start(f32[4,8,256]{2,1,0:T(8,128)} %shard_map.92) | copy-start | bytes 98308
  101.3 10.3 %copy-start.16 = (s32[8]{0:T(128)S(1)}, s32[8]{0:T(128)}, u32[]{:S(2)}) copy-start(s32[8]{0:T(128)} %param.17) | copy-start | bytes 100
  (1 other events, 0.7 us)

commit v2 on v1

v2 whole, which is shorter than its diff:
```python
import functools

import jax
import jax.numpy as jnp
from jax import lax
from jax.experimental import pallas as pl
from jax.experimental.pallas import tpu as pltpu
from jax.sharding import PartitionSpec as P

SEQ_LEN = 128
VMEM_BYTES = 28 * 2**20
F32 = jnp.float32
BF16 = jnp.bfloat16


def contract(a, b, dim_a, dim_b):
    return lax.dot_general(a, b, (((dim_a,), (dim_b,)), ((), ())), preferred_element_type=F32)


def run_copies(pairs, sem):
    copies = [pltpu.make_async_copy(src, dst, sem.at[j]) for j, (src, dst) in enumerate(pairs)]
    for copy in copies:
        copy.start()
    for copy in copies:
        copy.wait()


def cut_kernel(rows, columns, place, acts, *refs):
    parts, (mine, beside, own, near, skip, across, sem) = refs[:3], refs[3:]
    chip, core = place[0] // 2, place[0] % 2

    def part(m, c):
        first = pl.multiple_of((2 * (chip ^ m) + c) * columns, columns)
        return acts.at[:, pl.ds(first, columns)]

    pairs, at = [], 0
    for x in parts:
        length = x.shape[0]
        pairs.append((x, mine.at[pl.ds(at, length)]))
        pairs.append((x, beside.at[pl.ds(4 * rows + at, length)]))
        at += length
    for m, out in enumerate((own, near, skip, across)):
        pairs.append((part(m, 1 - core), beside.at[pl.ds(m * rows, rows)]))
        pairs.append((part(m, core), out))
    run_copies(pairs, sem)


def cut(me, acts, parts, columns):
    rows = acts.shape[0]
    total = sum(part.shape[0] for part in parts)
    lengths = (total, 4 * rows + total, rows, rows, rows, rows)
    return pl.pallas_call(
        functools.partial(cut_kernel, rows, columns),
        out_shape=[jax.ShapeDtypeStruct((length, columns), BF16) for length in lengths],
        in_specs=[pl.BlockSpec(memory_space=pltpu.SMEM)]
        + [pl.BlockSpec(memory_space=pltpu.HBM)] * (1 + len(parts)),
        out_specs=[pl.BlockSpec(memory_space=pltpu.VMEM)] * len(lengths),
        scratch_shapes=[pltpu.SemaphoreType.DMA((14,))],
    )(me.reshape(1).astype(jnp.int32), acts, *parts)


def join_kernel(rows, beside, *refs):
    parts, outs, sem = refs[:3], refs[3:6], refs[6]
    pairs = [(part, out.at[pl.ds(0, rows)]) for part, out in zip(parts, outs)]
    for m, out in enumerate(outs):
        pairs.append((beside.at[pl.ds((m + 1) * rows, rows)], out.at[pl.ds(rows, rows)]))
    run_copies(pairs, sem)


def join_parts(rows, beside, parts):
    columns = beside.shape[1]
    return pl.pallas_call(
        functools.partial(join_kernel, rows),
        out_shape=[jax.ShapeDtypeStruct((2 * rows, columns), BF16)] * 3,
        in_specs=[pl.BlockSpec(memory_space=pltpu.HBM)] * 4,
        out_specs=[pl.BlockSpec(memory_space=pltpu.VMEM)] * 3,
        scratch_shapes=[pltpu.SemaphoreType.DMA((6,))],
    )(beside, *parts)


def rotate_kernel(count, sizes, starts, place, *refs):
    pieces = refs[:count]
    out, left, basis, grads, sem = refs[count:]
    copies = []
    for j in range(count):
        first = starts[j]
        for part, (rows, buffer) in enumerate(zip(sizes, (basis, grads, left))):
            at = pl.multiple_of(place[j] * rows, rows)
            copies.append(
                pltpu.make_async_copy(
                    pieces[j].at[pl.ds(first, rows)], buffer.at[pl.ds(at, rows)], sem.at[part, j]
                )
            )
            first += rows
    for copy in copies:
        copy.start()
    for copy in copies:
        copy.wait()
    width = basis.shape[1]
    size = min(width, 256)
    for j in range(0, width, size):
        out[:, j : j + size] = contract(grads[...], basis[:, j : j + size], 1, 0).astype(BF16)


def rotate_grads(place, pieces, sizes):
    count = len(pieces)
    width = pieces[0][0].shape[1]
    basis_rows, grad_rows, left_rows = (count * rows for rows in sizes)
    return pl.pallas_call(
        functools.partial(rotate_kernel, count, sizes, tuple(at for _, at in pieces)),
        out_shape=(
            jax.ShapeDtypeStruct((grad_rows, width), BF16),
            jax.ShapeDtypeStruct((left_rows, width), BF16),
        ),
        in_specs=[pl.BlockSpec(memory_space=pltpu.SMEM)]
        + [pl.BlockSpec(memory_space=pltpu.HBM)] * count,
        out_specs=[pl.BlockSpec(memory_space=pltpu.VMEM)] * 2,
        scratch_shapes=[
            pltpu.VMEM((basis_rows, width), BF16),
            pltpu.VMEM((grad_rows, width), BF16),
            pltpu.SemaphoreType.DMA((3, count)),
        ],
        compiler_params=pltpu.CompilerParams(
            vmem_limit_bytes=8 * 2**20 + 2 * width * (basis_rows + 2 * grad_rows + left_rows)
        ),
        cost_estimate=pl.CostEstimate(
            flops=2 * grad_rows * basis_rows * width,
            bytes_accessed=2 * (basis_rows + 2 * grad_rows + 2 * left_rows) * width,
            transcendentals=0,
        ),
    )(place.astype(jnp.int32), *[array for array, _ in pieces])


def score_kernel(blocks, parts, queries, info, *refs):
    count = len(blocks)
    arrays = refs[:parts]
    turned, left_in, basis_in, curvature_in, right_in, out = refs[parts : parts + 6]
    acts, rotated, grads, left, basis, curvature, right, sem = refs[parts + 6 :]
    columns, size = basis.shape
    width = curvature.shape[0]
    ranks = right.shape[0]
    step = min(width, 512)

    def acts_copy(q, array, at):
        src = arrays[array].at[pl.ds(at * SEQ_LEN, SEQ_LEN)]
        return pltpu.make_async_copy(src, acts.at[q], sem.at[q])

    def grads_copy(q):
        src = turned.at[pl.ds(pl.multiple_of(info[q] * SEQ_LEN, SEQ_LEN), SEQ_LEN)]
        return pltpu.make_async_copy(src, grads.at[q], sem.at[count + q])

    def curvature_copy(i):
        rows = pl.ds(i * step, step)
        return pltpu.make_async_copy(
            curvature_in.at[rows], curvature.at[rows], sem.at[2 * count + 3 + i]
        )

    basis_copy = pltpu.make_async_copy(basis_in, basis, sem.at[2 * count])
    left_copy = pltpu.make_async_copy(left_in, left, sem.at[2 * count + 1])
    right_copy = pltpu.make_async_copy(right_in, right, sem.at[2 * count + 2])
    basis_copy.start()
    for q, (one, other) in enumerate(blocks):
        if one == other:
            acts_copy(q, *one).start()
        else:
            @pl.when(info[count] == 1)
            def _():
                acts_copy(q, *one).start()

            @pl.when(info[count] == 0)
            def _():
                acts_copy(q, *other).start()
    for q in range(count):
        grads_copy(q).start()
    curvature_copy(0).start()
    right_copy.start()
    left_copy.start()
    for i in range(1, width // step):
        curvature_copy(i).start()
    basis_copy.wait()
    for q, (one, _) in enumerate(blocks):
        acts_copy(q, *one).wait()
        for b in range(columns // size):
            own = slice(b * size, (b + 1) * size)
            rotated[q, :, own] = contract(acts[q, :, own], basis[own, :], 1, 0).astype(BF16)
    for q in range(count):
        grads_copy(q).wait()
    for i in range(width // step):
        rows = slice(i * step, (i + 1) * step)
        curvature_copy(i).wait()
        if i == 0:
            right_copy.wait()
            left_copy.wait()
        inverse = 1.0 / curvature[rows, :].astype(F32)
        weights = left[:, rows].astype(F32)
        for q in range(count):
            scaled = (contract(grads[q, :, rows], rotated[q], 0, 0) * inverse).astype(BF16)
            terms = contract(right[...], scaled, 1, 1) * weights
            total = terms[:, :128]
            for j in range(128, step, 128):
                total = total + terms[:, j : j + 128]
            total = jnp.sum(total.reshape(queries, ranks // queries, 128), axis=1)
            out[q] = total if i == 0 else out[q] + total


def score(sequences, inner, acts, turned, left, basis, curvature, right, queries):
    count = len(acts)
    width, columns = curvature.shape
    ranks = right.shape[0]
    arrays = []

    def index(x):
        if not any(x is y for y in arrays):
            arrays.append(x)
        return [x is y for y in arrays].index(True)

    blocks = tuple(((index(x), i), (index(y), j)) for (x, i), (y, j) in acts)
    info = jnp.concatenate([sequences, inner.reshape(1)]).astype(jnp.int32)
    in_vmem = pl.BlockSpec(memory_space=pltpu.VMEM)
    in_hbm = pl.BlockSpec(memory_space=pltpu.HBM)
    return pl.pallas_call(
        functools.partial(score_kernel, blocks, len(arrays), queries),
        out_shape=jax.ShapeDtypeStruct((count, queries, 128), F32),
        in_specs=[pl.BlockSpec(memory_space=pltpu.SMEM)] + [in_hbm] * (len(arrays) + 5),
        out_specs=in_vmem,
        scratch_shapes=[
            pltpu.VMEM((count, SEQ_LEN, columns), BF16),
            pltpu.VMEM((count, SEQ_LEN, columns), BF16),
            pltpu.VMEM((count, SEQ_LEN, width), BF16),
            pltpu.VMEM(left.shape, BF16),
            pltpu.VMEM(basis.shape, BF16),
            pltpu.VMEM(curvature.shape, BF16),
            pltpu.VMEM(right.shape, BF16),
            pltpu.SemaphoreType.DMA((2 * count + 3 + width // min(width, 512),)),
        ],
        compiler_params=pltpu.CompilerParams(vmem_limit_bytes=VMEM_BYTES),
        cost_estimate=pl.CostEstimate(
            flops=2 * count * width * columns * (SEQ_LEN + ranks),
            bytes_accessed=2 * (width * columns + count * SEQ_LEN * (width + columns)),
            transcendentals=0,
        ),
    )(info, *arrays, turned, left, basis, curvature, right)


def swap(x, k, n):
    return lax.ppermute(x, "dp", [(i, i ^ k) for i in range(n)])


def hop(x, pairs, cross=False):
    pairs = [(2 * a + c, 2 * b + (c ^ int(cross))) for a, b in pairs for c in range(2)]
    return lax.ppermute(x, "dp", pairs)


def after(x, *others):
    return lax.optimization_barrier((x, *others))[0]


def exchange_line(acts, parts, columns, me, sizes):
    chip, core = me // 2, me % 2
    inner = (chip == 1) | (chip == 2)
    rows = acts.shape[0]
    outward = [(1, 0), (2, 3)]
    mine, to_beside, own, near, skip, across = cut(me, acts, parts, columns)
    second_in = hop(mine, [(1, 2), (2, 1)])
    third_in = hop(mine, [(0, 2), (3, 1)])
    first = hop(mine, [(0, 1), (1, 0), (2, 3), (3, 2)])
    beside = swap(to_beside, 1, 8)
    near, skip, across = join_parts(rows, beside, (near, skip, across))
    near_out = hop(near, outward)
    second_end = hop(after(second_in, first, near_out), outward)
    third_end = hop(third_in, outward)
    across_in = hop(after(across, second_in), [(1, 2), (2, 1)])
    skip_in = hop(after(skip, third_in), [(0, 2), (3, 1)])
    first_x = swap(first, 1, 8)
    second = jnp.where(inner, second_in, after(second_end, across_in))
    third = jnp.where(inner, third_in, after(third_end, skip_in))
    near_in = hop(after(near, first), [(0, 1), (3, 2)])
    skip_out = hop(after(skip, skip_in, across_in), [(1, 3), (2, 0)])
    across_out = hop(after(across, skip_in, across_in), [(0, 3), (3, 0)])
    chips = jnp.stack(
        [chip, chip ^ 1, jnp.where(inner, chip ^ 3, chip ^ 2), jnp.where(inner, chip ^ 2, chip ^ 3)]
    )
    pieces = [(x, 0) for x in (mine, first, second, third)]
    pieces += [(beside, 4 * rows)] + [(x, 0) for x in (first_x, swap(second, 1, 8), swap(third, 1, 8))]
    place = jnp.concatenate([2 * chips + core, 2 * chips + 1 - core])
    turned, left = rotate_grads(place, pieces, sizes)
    each = rows // SEQ_LEN
    owners = [me, me ^ 1]
    blocks = [((x, j), (x, j)) for x in (own, beside) for j in range(each)]
    for inside, x, outside, y in (
        (6, (across_in, across_in), 2, (near_out, near_out)),
        (4, (skip_in, skip_in), 4, (skip_out, skip_out)),
        (2, (near_in, near_in), 6, (across_out, across_out)),
    ):
        for c in range(2):
            owners.append(me ^ (jnp.where(inner, inside, outside) + c))
            for j in range(each):
                at = [c * each + j if z[0] is z[1] else j for z in (x, y)]
                blocks.append(((x[c], at[0]), (y[c], at[1])))
    return inner, turned, left, jnp.stack(owners), blocks


def on_device(n, activations, out_grads, in_basis, out_basis, curvature, left_factors, right_factors,
              sequence_ids, query_order):
    me = lax.axis_index("dp")
    acts = activations[0]
    columns = in_basis.shape[1]
    width = out_basis.shape[2]
    left_own = left_factors[0].reshape(-1, width)
    parts = [out_basis[0], out_grads[0], left_own]
    sizes = tuple(part.shape[0] for part in parts)
    right = right_factors[0].reshape(-1, columns)
    queries = right_factors.shape[1]
    each = acts.shape[0] // SEQ_LEN
    if n == 8:
        inner, turned, left, owners, operands = exchange_line(acts, parts, columns, me, sizes)
    else:
        every = lax.all_gather(jnp.concatenate(parts), "dp", axis=0)
        pieces, place = [(every[j], 0) for j in range(n)], jnp.arange(n, dtype=jnp.int32)
        turned, left = rotate_grads(place, pieces, sizes)
        part = lax.all_to_all(acts, "dp", split_axis=1, concat_axis=0, tiled=True)
        operands = [((part, j), (part, j)) for j in range(n * each)]
        inner = jnp.bool_(True)
        owners = jnp.arange(n, dtype=jnp.int32)
    sequences = (owners[:, None] * each + jnp.arange(each)[None, :]).reshape(-1).astype(jnp.int32)
    sums = []
    at = 0
    while at < len(operands):
        step = (4 if at == 0 else 2) * each
        sums.append(
            score(sequences[at : at + step], inner, operands[at : at + step], turned, left, in_basis[0],
                  curvature[0], right, queries)
        )
        at += step
    scores = jnp.sum(jnp.concatenate(sums), axis=2)
    seqs = scores.shape[0]

    rows = jnp.sum(
        jnp.where(jnp.arange(seqs)[None, :, None] == sequences[:, None, None],
                  sequence_ids[None, :, None], 0), axis=1)
    row_pick = (rows.reshape(1, seqs) == jnp.arange(seqs)[:, None]).astype(F32)
    col_pick = (query_order[:, None] == jnp.arange(queries)[None, :]).astype(F32)
    placed = jnp.dot(jnp.dot(row_pick, scores, precision=lax.Precision.HIGHEST), col_pick,
                     precision=lax.Precision.HIGHEST)
    layers = lax.axis_size("section")
    wanted = jnp.arange(layers) <= lax.axis_index("section")
    outgoing = jnp.where(wanted[:, None, None], placed[None], 0.0)
    outgoing = outgoing.reshape(layers * n, seqs // n, queries)
    arrived = lax.all_to_all(outgoing, ("section", "dp"), split_axis=0, concat_axis=0, tiled=True)
    return jnp.sum(arrived, axis=0)[None]


def solution(mesh):
    placed = (
        P("section", "dp", None),
        P("section", "dp", None),
        P("section", "dp", None),
        P("section", "dp", None),
        P("section", None, "dp"),
        P("section", "dp", None, None),
        P("section", None, None, "dp"),
        P(),
        P(),
    )
    return jax.shard_map(
        functools.partial(on_device, mesh.shape["dp"]), mesh=mesh, in_specs=placed,
        out_specs=P("section", "dp", None), check_vma=False,
    )
```

time: 135 us -> 113 us (0.84)
  waiting for transfers between devices: 57.1 us -> 37.6 us
  blocking collectives: 21.9 us -> 10.6 us
  starting transfers between devices: 19 us -> 29.7 us
    ppermute x5 -> x11, starting transfers between devices: 11 us -> 29.1 us  [hop(): return lax.ppermute(x, 'dp', pairs)]
    ppermute x11 -> x4, waiting for transfers between devices: 13.3 us -> 0.01 us  [swap(): return lax.ppermute(x, 'dp', [(i, i ^ k) for i in range(n)])]
    all_to_all x1, blocking collectives: 21.9 us -> 10.6 us  [on_device(): lax.all_to_all(outgoing, ('section', 'dp'), split_axis=0, concat_axis=0,...]
    ppermute x11 -> x4, starting transfers between devices: 8 us -> 0.68 us  [swap(): return lax.ppermute(x, 'dp', [(i, i ^ k) for i in range(n)])]
    ppermute x5 -> x11, waiting for transfers between devices: 43.8 us -> 37.6 us  [hop(): return lax.ppermute(x, 'dp', pairs)]
    dynamic_slice x1 -> x0, local copies, waits for them, and re-layouts: 2.89 us -> none  [on_device(): lax.dynamic_slice(acts, (0, (me ^ k) * columns), (acts.shape[0], columns))]
    unnamed x34 -> x26, local copies, waits for them, and re-layouts: 1.62 us -> 3.89 us
    select_n x2, other arithmetic: 0.13 us -> 2.26 us  [the longest x1 1.13 us: exchange_line(): third = jnp.where(inner, third_in, after(third_end, skip_in))]
  transfers between devices with their start and end apart: 16 -> 15, of which waited for: 7 -> 7; matrix products, arithmetic and copies ran while one was open for 4% -> 3% of each run, Pallas kernels for 13% -> 16%
where the time goes in v2:
time: 113 us
  waiting for transfers between devices  37.6 us (33%)
  starting transfers between devices  29.7 us (26%)
  Pallas kernels  26.4 us (23%)
  blocking collectives  10.6 us (9%)
  local copies, waits for them, and re-layouts  4.23 us (4%)
  other arithmetic  3.44 us (3%)
    ppermute x11, waiting for transfers between devices, hop(): return lax.ppermute(x, 'dp', pairs)  37.6 us
    ppermute x11, starting transfers between devices, hop(): return lax.ppermute(x, 'dp', pairs)  29.1 us
    pallas_call x3, Pallas kernels, score(): pl.pallas_call(functools.partial(score_kernel, blocks, len(arrays), queri...  15.1 us
    all_to_all x1, blocking collectives, on_device(): lax.all_to_all(outgoing, ('section', 'dp'), split_axis=0, concat_axis=0,...  10.6 us
    pallas_call x1, Pallas kernels, rotate_grads(): pl.pallas_call(functools.partial(rotate_kernel, count, sizes, tuple((at f...  5.04 us
    unnamed x26, local copies, waits for them, and re-layouts  3.89 us
    pallas_call x1, Pallas kernels, cut(): pl.pallas_call(functools.partial(cut_kernel, rows, columns), out_shape=[j...  3.73 us
    pallas_call x1, Pallas kernels, join_parts(): pl.pallas_call(functools.partial(join_kernel, rows), out_shape=[jax.Shape...  2.55 us
  transfers between devices with their start and end apart: 15, of which 7 were waited for; matrix products, arithmetic and copies ran while one was open for 3% of the time, Pallas kernels for 16%

profile of v2, /device:TPU:0, one launch (start us, length us, event | category | flops | bytes accessed | tf_op | source)
XLA Modules:
  0.0 112.6 jit_solution(9937137120725858098)
XLA Ops:
  0.0 3.7 %shard_map.91 = (bf16[288,1024]{1,0:T(8,128)(2,1)}, bf16[800,1024]{1,0:T(8,128)(2,1)}, bf16[128,1024]{1,0:T(8,128)(2,1)}, bf16[128,1024]{1,0:T(8,128)(2,1)}, bf1...) custom-call(s32[1]{0:T(128)} %bitcast.place, bf16[128,8192]{1,0:T(8,128)(2,1)} %bitcast.33, bf16[128,1024]{1,0:T(8,128)(2,1)} %bitcast.34, ...), custom_call_target="tpu_custom_call" | custom-call | tf_op jit(solution)/shard_map/pallas_call | solution.py:52
  3.7 0.5 collective-permute-start
  4.3 6.3 %collective-permute-start.6 = (bf16[288,1024]{1,0:T(8,128)(2,1)}, bf16[288,1024]{1,0:T(8,128)(2,1)}, u32[]{:S(2)}, u32[]{:S(2)}) collective-permute-start(bf16[288,1024]{1,0:T(8,128)(2,1)} %get-tuple-element.30.refs_0_), channel_id=1, source_target_pairs={{0,4},{1,5},{6,2},{7,3},{8,12},{9,13},{14,10},{15,11},{16,20},{17,... | collective-permute-start | bytes 1769480 | tf_op jit(solution)/shard_map/ppermute | solution.py:251
  10.6 1.5 %collective-permute-start.1 = (bf16[288,1024]{1,0:T(8,128)(2,1)}, bf16[288,1024]{1,0:T(8,128)(2,1)}, u32[]{:S(2)}, u32[]{:S(2)}) collective-permute-start(bf16[288,1024]{1,0:T(8,128)(2,1)} %get-tuple-element.30.refs_0_), channel_id=1, source_target_pairs={{2,4},{3,5},{4,2},{5,3},{10,12},{11,13},{12,10},{13,11},{18,20},{1... | collective-permute-start | bytes 1769480 | tf_op jit(solution)/shard_map/ppermute | solution.py:251
  12.1 1.2 %copy-done.3 = bf16[800,1024]{1,0:T(8,128)(2,1)} copy-done((bf16[800,1024]{1,0:T(8,128)(2,1)}, bf16[800,1024]{1,0:T(8,128)(2,1)S(1)}, u32[]{:S(2)}) %copy-start.3) | copy-done | bytes 1638424
  13.3 2.6 %shard_map.92 = (bf16[256,1024]{1,0:T(8,128)(2,1)}, bf16[256,1024]{1,0:T(8,128)(2,1)}, bf16[256,1024]{1,0:T(8,128)(2,1)}) custom-call(bf16[800,1024]{1,0:T(8,128)(2,1)} %copy-done.3, bf16[128,1024]{1,0:T(8,128)(2,1)} %get-tuple-element.26.refs_0_, bf16[128,1024]{1,0:T(8,128)(2,1)} %get-tuple-element.27.refs_1_, bf16[128,1024]{1,0:T(8,128)(2,1)} %get-tuple-element.28.refs_2_), custom_call_target="tpu_custom_call" | custom-call | tf_op jit(solution)/shard_map/pallas_call | solution.py:72
  15.8 1.4 %collective-permute-start.3 = (bf16[256,1024]{1,0:T(8,128)(2,1)}, bf16[256,1024]{1,0:T(8,128)(2,1)S(1)}, u32[]{:S(2)}, u32[]{:S(2)}) collective-permute-start(bf16[256,1024]{1,0:T(8,128)(2,1)} %get-tuple-element.41), channel_id=1, source_target_pairs={{2,0},{3,1},{4,6},{5,7},{10,8},{11,9},{12,14},{13,15},{18,16},{19,... | collective-permute-start | bytes 1572872 | tf_op jit(solution)/shard_map/ppermute | solution.py:251
  17.3 6.5 %collective-permute-done.6 = bf16[288,1024]{1,0:T(8,128)(2,1)} collective-permute-done((bf16[288,1024]{1,0:T(8,128)(2,1)}, bf16[288,1024]{1,0:T(8,128)(2,1)}, u32[]{:S(2)}, u32[]{:S(2)}) %collective-permute-start.6) | collective-permute-done | bytes 589856 | tf_op jit(solution)/shard_map/ppermute | solution.py:251
  23.8 1.3 %collective-permute-start.7 = (bf16[288,1024]{1,0:T(8,128)(2,1)}, bf16[288,1024]{1,0:T(8,128)(2,1)}, u32[]{:S(2)}, u32[]{:S(2)}) collective-permute-start(bf16[288,1024]{1,0:T(8,128)(2,1)} %collective-permute-done.6), channel_id=1, source_target_pairs={{2,0},{3,1},{4,6},{5,7},{10,8},{11,9},{12,14},{13,15},{18,16},{19,... | collective-permute-start | bytes 1769480 | tf_op jit(solution)/shard_map/ppermute | solution.py:251
  25.0 6.1 %collective-permute-start.8 = (bf16[256,1024]{1,0:T(8,128)(2,1)}, bf16[256,1024]{1,0:T(8,128)(2,1)S(1)}, u32[]{:S(2)}, u32[]{:S(2)}) collective-permute-start(bf16[256,1024]{1,0:T(8,128)(2,1)} %get-tuple-element.40), channel_id=1, source_target_pairs={{0,4},{1,5},{6,2},{7,3},{8,12},{9,13},{14,10},{15,11},{16,20},{17,... | collective-permute-start | bytes 1572872 | tf_op jit(solution)/shard_map/ppermute | solution.py:251
  31.2 5.2 %collective-permute-done.4.refs_1_ = bf16[288,1024]{1,0:T(8,128)(2,1)} collective-permute-done((bf16[288,1024]{1,0:T(8,128)(2,1)}, bf16[288,1024]{1,0:T(8,128)(2,1)}, u32[]{:S(2)}, u32[]{:S(2)}) %collective-permute-start.4) | collective-permute-done | bytes 589856 | tf_op jit(solution)/shard_map/ppermute | solution.py:251
  36.4 1.8 %collective-permute-done.3.refs_3_ = bf16[256,1024]{1,0:T(8,128)(2,1)S(1)} collective-permute-done((bf16[256,1024]{1,0:T(8,128)(2,1)}, bf16[256,1024]{1,0:T(8,128)(2,1)S(1)}, u32[]{:S(2)}, u32[]{:S(2)}) %collective-permute-start.3) | collective-permute-done | bytes 524320 | tf_op jit(solution)/shard_map/ppermute | solution.py:251
  38.2 0.8 copy-done.6
  39.0 1.3 %collective-permute-start.5 = (bf16[288,1024]{1,0:T(8,128)(2,1)}, bf16[288,1024]{1,0:T(8,128)(2,1)}, u32[]{:S(2)}, u32[]{:S(2)}) collective-permute-start(bf16[288,1024]{1,0:T(8,128)(2,1)} %collective-permute-done.1), channel_id=1, source_target_pairs={{2,0},{3,1},{4,6},{5,7},{10,8},{11,9},{12,14},{13,15},{18,16},{19,... | collective-permute-start | bytes 1769480 | tf_op jit(solution)/shard_map/ppermute | solution.py:251
  40.3 0.7 collective-permute-start.2
  41.1 9.8 %collective-permute-done.7 = bf16[288,1024]{1,0:T(8,128)(2,1)} collective-permute-done((bf16[288,1024]{1,0:T(8,128)(2,1)}, bf16[288,1024]{1,0:T(8,128)(2,1)}, u32[]{:S(2)}, u32[]{:S(2)}) %collective-permute-start.7) | collective-permute-done | bytes 589856 | tf_op jit(solution)/shard_map/ppermute | solution.py:251
  51.0 1.1 %broadcast_select_fusion.refs_3_ = bf16[288,1024]{1,0:T(8,128)(2,1)S(1)} fusion(bf16[288,1024]{1,0:T(8,128)(2,1)} %collective-permute-done.6, bf16[288,1024]{1,0:T(8,128)(2,1)} %collective-permute-done.7, pred[]{:T(512)S(6)} %or.3), kind=kLoop, calls=%fused_computation | loop fusion | flops 294912 | bytes 1769473 | tf_op jit(solution)/shard_map/jit(_where)/select_n | solution.py:276
  52.2 0.8 copy-done.8
  53.0 9.9 %collective-permute-done.5 = bf16[288,1024]{1,0:T(8,128)(2,1)} collective-permute-done((bf16[288,1024]{1,0:T(8,128)(2,1)}, bf16[288,1024]{1,0:T(8,128)(2,1)}, u32[]{:S(2)}, u32[]{:S(2)}) %collective-permute-start.5) | collective-permute-done | bytes 589856 | tf_op jit(solution)/shard_map/ppermute | solution.py:251
  62.9 1.1 %broadcast_select_fusion.1.refs_2_ = bf16[288,1024]{1,0:T(8,128)(2,1)S(1)} fusion(bf16[288,1024]{1,0:T(8,128)(2,1)} %collective-permute-done.1, bf16[288,1024]{1,0:T(8,128)(2,1)} %collective-permute-done.5, pred[]{:T(512)S(6)} %or.3), kind=kLoop, calls=%fused_computation.1 | loop fusion | flops 294912 | bytes 1769473 | tf_op jit(solution)/shard_map/jit(_where)/select_n | solution.py:275
  64.4 1.3 %collective-permute-start.12 = (bf16[256,1024]{1,0:T(8,128)(2,1)}, bf16[256,1024]{1,0:T(8,128)(2,1)S(1)}, u32[]{:S(2)}, u32[]{:S(2)}) collective-permute-start(bf16[256,1024]{1,0:T(8,128)(2,1)} %get-tuple-element.40), channel_id=1, source_target_pairs={{2,6},{3,7},{4,0},{5,1},{10,14},{11,15},{12,8},{13,9},{18,22},{19,... | collective-permute-start | bytes 1572872 | tf_op jit(solution)/shard_map/ppermute | solution.py:251
  66.1 4.8 %collective-permute-start.13 = (bf16[256,1024]{1,0:T(8,128)(2,1)}, bf16[256,1024]{1,0:T(8,128)(2,1)S(1)}, u32[]{:S(2)}, u32[]{:S(2)}) collective-permute-start(bf16[256,1024]{1,0:T(8,128)(2,1)} %get-tuple-element.41), channel_id=1, source_target_pairs={{0,2},{1,3},{6,4},{7,5},{8,10},{9,11},{14,12},{15,13},{16,18},{17,... | collective-permute-start | bytes 1572872 | tf_op jit(solution)/shard_map/ppermute | solution.py:251
  70.9 4.4 %collective-permute-start.14 = (bf16[256,1024]{1,0:T(8,128)(2,1)}, bf16[256,1024]{1,0:T(8,128)(2,1)S(1)}, u32[]{:S(2)}, u32[]{:S(2)}) collective-permute-start(bf16[256,1024]{1,0:T(8,128)(2,1)} %get-tuple-element.42), channel_id=1, source_target_pairs={{0,6},{1,7},{6,0},{7,1},{8,14},{9,15},{14,8},{15,9},{16,22},{17,23... | collective-permute-start | bytes 1572872 | tf_op jit(solution)/shard_map/ppermute | solution.py:251
  75.3 1.1 copy-done.5
  76.4 5.0 %shard_map.93 = (bf16[1024,1024]{1,0:T(8,128)(2,1)S(1)}, bf16[256,1024]{1,0:T(8,128)(2,1)S(1)}) custom-call(s32[8]{0:T(128)S(1)} %pad_add_fusion.place, bf16[288,1024]{1,0:T(8,128)(2,1)S(1)} %copy-done.5, bf16[288,1024]{1,0:T(8,128)(2,1)} %collective-permute-done.4.refs_1_, bf16[288,1024]{1,0:T(8,128)(2,1)S(1)} %broadcast_select_fusion.1.refs_2_, ...), custom_call_target="tpu_custom_call" | custom-call | flops 2147483648 | bytes 7340032 | tf_op jit(solution)/shard_map/pallas_call | solution.py:109
  81.4 0.3 collective-permute-done.12.refs_1_
  81.8 4.0 %shard_map.95 = f32[2,8,128]{2,1,0:T(8,128)S(1)} custom-call(s32[3]{0:T(128)S(1)} %get-tuple-element.45.info, bf16[256,1024]{1,0:T(8,128)(2,1)S(1)} %collective-permute-done.8.refs_0_, bf16[256,1024]{1,0:T(8,128)(2,1)S(1)} %collective-permute-done.12.refs_1_, bf16[1024,1024]{1,0:T(8,128)(2,1)S(1)} %get-tuple-element.38.refs_4_.refs_2_, ...), custom_call_target="tpu_custom_call" | custom-call | flops 1610612736 | bytes 3145728 | tf_op jit(solution)/shard_map/pallas_call | solution.py:221
  85.9 6.8 %shard_map.94 = f32[4,8,128]{2,1,0:T(8,128)S(1)} custom-call(s32[5]{0:T(128)S(1)} %concatenate.21.info, bf16[128,1024]{1,0:T(8,128)(2,1)S(1)} %copy-done.10, bf16[800,1024]{1,0:T(8,128)(2,1)S(1)} %copy-done.4, bf16[256,1024]{1,0:T(8,128)(2,1)S(1)} %copy-done.9, bf16[256,1024]{1,0:T(8,128)(2,1)S(1)} %copy-done.7, ...), custom_call_target="tpu_custom_call" | custom-call | flops 3221225472 | bytes 4194304 | tf_op jit(solution)/shard_map/pallas_call | solution.py:221
  92.7 4.0 %collective-permute-done.14.refs_1_ = bf16[256,1024]{1,0:T(8,128)(2,1)S(1)} collective-permute-done((bf16[256,1024]{1,0:T(8,128)(2,1)}, bf16[256,1024]{1,0:T(8,128)(2,1)S(1)}, u32[]{:S(2)}, u32[]{:S(2)}) %collective-permute-start.14) | collective-permute-done | bytes 524320 | tf_op jit(solution)/shard_map/ppermute | solution.py:251
  96.7 4.2 %shard_map.96 = f32[2,8,128]{2,1,0:T(8,128)S(1)} custom-call(s32[3]{0:T(128)S(1)} %get-tuple-element.46.info, bf16[256,1024]{1,0:T(8,128)(2,1)S(1)} %collective-permute-done.13.refs_0_, bf16[256,1024]{1,0:T(8,128)(2,1)S(1)} %collective-permute-done.14.refs_1_, bf16[1024,1024]{1,0:T(8,128)(2,1)S(1)} %get-tuple-element.38.refs_4_.refs_2_, ...), custom_call_target="tpu_custom_call" | custom-call | flops 1610612736 | bytes 3145728 | tf_op jit(solution)/shard_map/pallas_call | solution.py:221
  101.5 10.6 %all_to_all.5 = f32[32,1,8]{2,1,0:T(1,128)S(1)} all-to-all(f32[32,1,8]{2,1,0:T(1,128)S(1)} %broadcast_select_fusion.2), channel_id=1, replica_groups=mesh['section'=4,'dp'=8] {'section','dp'}, dimensions={0} | all-to-all | bytes 2048 | tf_op jit(solution)/shard_map/all_to_all | solution.py:349
  112.1 0.6 reduce_sum.29
  (49 shorter events, 1.5 us)
Async XLA Ops:
  3.7 8.3 %collective-permute-start = (bf16[800,1024]{1,0:T(8,128)(2,1)}, bf16[800,1024]{1,0:T(8,128)(2,1)S(1)}, u32[]{:S(2)}, u32[]{:S(2)}) collective-permute-start(bf16[800,1024]{1,0:T(8,128)(2,1)} %get-tuple-element.25), channel_id=1, source_target_pairs={{0,1},{1,0},{2,3},{3,2},{4,5},{5,4},{6,7},{7,6},{8,9},{9,8},{10,11... | collective-permute-start | bytes 4915208 | tf_op jit(solution)/shard_map/ppermute | solution.py:246
  4.3 19.5 %collective-permute-start.6 = (bf16[288,1024]{1,0:T(8,128)(2,1)}, bf16[288,1024]{1,0:T(8,128)(2,1)}, u32[]{:S(2)}, u32[]{:S(2)}) collective-permute-start(bf16[288,1024]{1,0:T(8,128)(2,1)} %get-tuple-element.30.refs_0_), channel_id=1, source_target_pairs={{0,4},{1,5},{6,2},{7,3},{8,12},{9,13},{14,10},{15,11},{16,20},{17,... | collective-permute-start | bytes 1769480 | tf_op jit(solution)/shard_map/ppermute | solution.py:251
  10.6 25.8 %collective-permute-start.4 = (bf16[288,1024]{1,0:T(8,128)(2,1)}, bf16[288,1024]{1,0:T(8,128)(2,1)}, u32[]{:S(2)}, u32[]{:S(2)}) collective-permute-start(bf16[288,1024]{1,0:T(8,128)(2,1)} %get-tuple-element.30.refs_0_), channel_id=1, source_target_pairs={{0,2},{1,3},{2,0},{3,1},{4,6},{5,7},{6,4},{7,5},{8,10},{9,11},{10,... | collective-permute-start | bytes 1769480 | tf_op jit(solution)/shard_map/ppermute | solution.py:251
  10.6 25.8 %collective-permute-start.1 = (bf16[288,1024]{1,0:T(8,128)(2,1)}, bf16[288,1024]{1,0:T(8,128)(2,1)}, u32[]{:S(2)}, u32[]{:S(2)}) collective-permute-start(bf16[288,1024]{1,0:T(8,128)(2,1)} %get-tuple-element.30.refs_0_), channel_id=1, source_target_pairs={{2,4},{3,5},{4,2},{5,3},{10,12},{11,13},{12,10},{13,11},{18,20},{1... | collective-permute-start | bytes 1769480 | tf_op jit(solution)/shard_map/ppermute | solution.py:251
  12.1 1.2 %copy-start.3 = (bf16[800,1024]{1,0:T(8,128)(2,1)}, bf16[800,1024]{1,0:T(8,128)(2,1)S(1)}, u32[]{:S(2)}) copy-start(bf16[800,1024]{1,0:T(8,128)(2,1)S(1)} %collective-permute-done.beside.refs_4_.refs_1_) | copy-start | bytes 4915204
  15.8 50.1 %copy-start.11 = (s32[8]{0:T(128)S(1)}, s32[8]{0:T(128)}, u32[]{:S(2)}) copy-start(s32[8]{0:T(128)} %param.16) | copy-start | bytes 100
  15.8 59.5 %copy-start.4 = (bf16[800,1024]{1,0:T(8,128)(2,1)S(1)}, bf16[800,1024]{1,0:T(8,128)(2,1)}, u32[]{:S(2)}) copy-start(bf16[800,1024]{1,0:T(8,128)(2,1)} %copy-done.3) | copy-start | bytes 4915204
  15.8 22.4 %collective-permute-start.3 = (bf16[256,1024]{1,0:T(8,128)(2,1)}, bf16[256,1024]{1,0:T(8,128)(2,1)S(1)}, u32[]{:S(2)}, u32[]{:S(2)}) collective-permute-start(bf16[256,1024]{1,0:T(8,128)(2,1)} %get-tuple-element.41), channel_id=1, source_target_pairs={{2,0},{3,1},{4,6},{5,7},{10,8},{11,9},{12,14},{13,15},{18,16},{19,... | collective-permute-start | bytes 1572872 | tf_op jit(solution)/shard_map/ppermute | solution.py:251
  23.8 27.2 %collective-permute-start.7 = (bf16[288,1024]{1,0:T(8,128)(2,1)}, bf16[288,1024]{1,0:T(8,128)(2,1)}, u32[]{:S(2)}, u32[]{:S(2)}) collective-permute-start(bf16[288,1024]{1,0:T(8,128)(2,1)} %collective-permute-done.6), channel_id=1, source_target_pairs={{2,0},{3,1},{4,6},{5,7},{10,8},{11,9},{12,14},{13,15},{18,16},{19,... | collective-permute-start | bytes 1769480 | tf_op jit(solution)/shard_map/ppermute | solution.py:251
  25.0 25.9 %collective-permute-start.8 = (bf16[256,1024]{1,0:T(8,128)(2,1)}, bf16[256,1024]{1,0:T(8,128)(2,1)S(1)}, u32[]{:S(2)}, u32[]{:S(2)}) collective-permute-start(bf16[256,1024]{1,0:T(8,128)(2,1)} %get-tuple-element.40), channel_id=1, source_target_pairs={{0,4},{1,5},{6,2},{7,3},{8,12},{9,13},{14,10},{15,11},{16,20},{17,... | collective-permute-start | bytes 1572872 | tf_op jit(solution)/shard_map/ppermute | solution.py:251
  38.2 0.8 copy-start.6
  39.0 23.9 %collective-permute-start.5 = (bf16[288,1024]{1,0:T(8,128)(2,1)}, bf16[288,1024]{1,0:T(8,128)(2,1)}, u32[]{:S(2)}, u32[]{:S(2)}) collective-permute-start(bf16[288,1024]{1,0:T(8,128)(2,1)} %collective-permute-done.1), channel_id=1, source_target_pairs={{2,0},{3,1},{4,6},{5,7},{10,8},{11,9},{12,14},{13,15},{18,16},{19,... | collective-permute-start | bytes 1769480 | tf_op jit(solution)/shard_map/ppermute | solution.py:251
  40.3 11.9 %collective-permute-start.2 = (bf16[256,1024]{1,0:T(8,128)(2,1)}, bf16[256,1024]{1,0:T(8,128)(2,1)S(1)}, u32[]{:S(2)}, u32[]{:S(2)}) collective-permute-start(bf16[256,1024]{1,0:T(8,128)(2,1)} %get-tuple-element.42), channel_id=1, source_target_pairs={{2,4},{3,5},{4,2},{5,3},{10,12},{11,13},{12,10},{13,11},{18,20},{1... | collective-permute-start | bytes 1572872 | tf_op jit(solution)/shard_map/ppermute | solution.py:251
  41.1 29.8 %collective-permute-start.9 = (bf16[288,1024]{1,0:T(8,128)(2,1)}, bf16[288,1024]{1,0:T(8,128)(2,1)}, u32[]{:S(2)}, u32[]{:S(2)}) collective-permute-start(bf16[288,1024]{1,0:T(8,128)(2,1)} %collective-permute-done.4.refs_1_), channel_id=1, source_target_pairs={{0,1},{1,0},{2,3},{3,2},{4,5},{5,4},{6,7},{7,6},{8,9},{9,8},{10,11... | collective-permute-start | bytes 1769480 | tf_op jit(solution)/shard_map/ppermute | solution.py:246
  52.1 23.2 %collective-permute-start.11 = (bf16[288,1024]{1,0:T(8,128)(2,1)S(1)}, bf16[288,1024]{1,0:T(8,128)(2,1)}, u32[]{:S(2)}, u32[]{:S(2)}) collective-permute-start(bf16[288,1024]{1,0:T(8,128)(2,1)S(1)} %broadcast_select_fusion.refs_3_), channel_id=1, source_target_pairs={{0,1},{1,0},{2,3},{3,2},{4,5},{5,4},{6,7},{7,6},{8,9},{9,8},{10,11... | collective-permute-start | bytes 1769480 | tf_op jit(solution)/shard_map/ppermute | solution.py:246
  52.2 0.8 copy-start.8
  64.0 11.3 %collective-permute-start.10 = (bf16[288,1024]{1,0:T(8,128)(2,1)S(1)}, bf16[288,1024]{1,0:T(8,128)(2,1)}, u32[]{:S(2)}, u32[]{:S(2)}) collective-permute-start(bf16[288,1024]{1,0:T(8,128)(2,1)S(1)} %broadcast_select_fusion.1.refs_2_), channel_id=1, source_target_pairs={{0,1},{1,0},{2,3},{3,2},{4,5},{5,4},{6,7},{7,6},{8,9},{9,8},{10,11... | collective-permute-start | bytes 1769480 | tf_op jit(solution)/shard_map/ppermute | solution.py:246
  64.4 17.3 %collective-permute-start.12 = (bf16[256,1024]{1,0:T(8,128)(2,1)}, bf16[256,1024]{1,0:T(8,128)(2,1)S(1)}, u32[]{:S(2)}, u32[]{:S(2)}) collective-permute-start(bf16[256,1024]{1,0:T(8,128)(2,1)} %get-tuple-element.40), channel_id=1, source_target_pairs={{2,6},{3,7},{4,0},{5,1},{10,14},{11,15},{12,8},{13,9},{18,22},{19,... | collective-permute-start | bytes 1572872 | tf_op jit(solution)/shard_map/ppermute | solution.py:251
  66.1 15.7 %copy-start = (bf16[1,1024,1024]{2,1,0:T(8,128)(2,1)S(1)}, bf16[1,1024,1024]{2,1,0:T(8,128)(2,1)}, u32[]{:S(2)}) copy-start(bf16[1,1024,1024]{2,1,0:T(8,128)(2,1)} %param.13) | copy-start | bytes 6291460
  66.1 15.7 %copy-start.1 = (bf16[1,1024,256]{2,1,0:T(8,128)(2,1)S(1)}, bf16[1,1024,256]{2,1,0:T(8,128)(2,1)}, u32[]{:S(2)}) copy-start(bf16[1,1024,256]{2,1,0:T(8,128)(2,1)} %param.11) | copy-start | bytes 1572868
  66.1 15.7 %copy-start.2 = (bf16[1,8,32,1024]{3,2,1,0:T(8,128)(2,1)S(1)}, bf16[1,8,32,1024]{3,2,1,0:T(8,128)(2,1)}, u32[]{:S(2)}) copy-start(bf16[1,8,32,1024]{3,2,1,0:T(8,128)(2,1)} %param.15) | copy-start | bytes 1572868
  66.1 26.6 %collective-permute-start.13 = (bf16[256,1024]{1,0:T(8,128)(2,1)}, bf16[256,1024]{1,0:T(8,128)(2,1)S(1)}, u32[]{:S(2)}, u32[]{:S(2)}) collective-permute-start(bf16[256,1024]{1,0:T(8,128)(2,1)} %get-tuple-element.41), channel_id=1, source_target_pairs={{0,2},{1,3},{6,4},{7,5},{8,10},{9,11},{14,12},{15,13},{16,18},{17,... | collective-permute-start | bytes 1572872 | tf_op jit(solution)/shard_map/ppermute | solution.py:251
  70.9 25.9 %collective-permute-start.14 = (bf16[256,1024]{1,0:T(8,128)(2,1)}, bf16[256,1024]{1,0:T(8,128)(2,1)S(1)}, u32[]{:S(2)}, u32[]{:S(2)}) collective-permute-start(bf16[256,1024]{1,0:T(8,128)(2,1)} %get-tuple-element.42), channel_id=1, source_target_pairs={{0,6},{1,7},{6,0},{7,1},{8,14},{9,15},{14,8},{15,9},{16,22},{17,23... | collective-permute-start | bytes 1572872 | tf_op jit(solution)/shard_map/ppermute | solution.py:251
  75.3 1.1 copy-start.5
  81.8 4.1 %copy-start.7 = (bf16[256,1024]{1,0:T(8,128)(2,1)S(1)}, bf16[256,1024]{1,0:T(8,128)(2,1)}, u32[]{:S(2)}) copy-start(bf16[256,1024]{1,0:T(8,128)(2,1)} %copy-done.6) | copy-start | bytes 1572868
  81.8 4.1 %copy-start.9 = (bf16[256,1024]{1,0:T(8,128)(2,1)S(1)}, bf16[256,1024]{1,0:T(8,128)(2,1)}, u32[]{:S(2)}) copy-start(bf16[256,1024]{1,0:T(8,128)(2,1)} %copy-done.8) | copy-start | bytes 1572868
  81.8 4.1 %copy-start.10 = (bf16[128,1024]{1,0:T(8,128)(2,1)S(1)}, bf16[128,1024]{1,0:T(8,128)(2,1)}, u32[]{:S(2)}) copy-start(bf16[128,1024]{1,0:T(8,128)(2,1)} %get-tuple-element.24.refs_0_) | copy-start | bytes 786436
  96.7 4.4 %copy-start.12 = (s32[8]{0:T(128)S(1)}, s32[8]{0:T(128)}, u32[]{:S(2)}) copy-start(s32[8]{0:T(128)} %param.17) | copy-start | bytes 100

commit v3 on v2

--- a/solution.py
+++ b/solution.py
@@ -78,20 +78,17 @@
     )(beside, *parts)
 
 
-def rotate_kernel(count, sizes, starts, place, *refs):
-    pieces = refs[:count]
-    out, left, basis, grads, sem = refs[count:]
+def rotate_kernel(count, sizes, sources, parts, place, *refs):
+    out, left, basis, grads, sem = refs[parts:]
     copies = []
     for j in range(count):
-        first = starts[j]
         for part, (rows, buffer) in enumerate(zip(sizes, (basis, grads, left))):
+            array, first = sources[j][part]
             at = pl.multiple_of(place[j] * rows, rows)
+            src = refs[array].at[pl.ds(first, rows)]
             copies.append(
-                pltpu.make_async_copy(
-                    pieces[j].at[pl.ds(first, rows)], buffer.at[pl.ds(at, rows)], sem.at[part, j]
-                )
+                pltpu.make_async_copy(src, buffer.at[pl.ds(at, rows)], sem.at[part, j])
             )
-            first += rows
     for copy in copies:
         copy.start()
     for copy in copies:
@@ -102,18 +99,26 @@
         out[:, j : j + size] = contract(grads[...], basis[:, j : j + size], 1, 0).astype(BF16)
 
 
+def index_in(arrays, x):
+    if not any(x is y for y in arrays):
+        arrays.append(x)
+    return [x is y for y in arrays].index(True)
+
+
 def rotate_grads(place, pieces, sizes):
     count = len(pieces)
-    width = pieces[0][0].shape[1]
+    width = pieces[0][0][0].shape[1]
+    arrays = []
+    sources = tuple(tuple((index_in(arrays, x), at) for x, at in piece) for piece in pieces)
     basis_rows, grad_rows, left_rows = (count * rows for rows in sizes)
     return pl.pallas_call(
-        functools.partial(rotate_kernel, count, sizes, tuple(at for _, at in pieces)),
+        functools.partial(rotate_kernel, count, sizes, sources, len(arrays)),
         out_shape=(
             jax.ShapeDtypeStruct((grad_rows, width), BF16),
             jax.ShapeDtypeStruct((left_rows, width), BF16),
         ),
         in_specs=[pl.BlockSpec(memory_space=pltpu.SMEM)]
-        + [pl.BlockSpec(memory_space=pltpu.HBM)] * count,
+        + [pl.BlockSpec(memory_space=pltpu.HBM)] * len(arrays),
         out_specs=[pl.BlockSpec(memory_space=pltpu.VMEM)] * 2,
         scratch_shapes=[
             pltpu.VMEM((basis_rows, width), BF16),
@@ -124,11 +129,11 @@
             vmem_limit_bytes=8 * 2**20 + 2 * width * (basis_rows + 2 * grad_rows + left_rows)
         ),
         cost_estimate=pl.CostEstimate(
-            flops=2 * grad_rows * basis_rows * width,
-            bytes_accessed=2 * (basis_rows + 2 * grad_rows + 2 * left_rows) * width,
+            flops=1,
+            bytes_accessed=1,
             transcendentals=0,
         ),
-    )(place.astype(jnp.int32), *[array for array, _ in pieces])
+    )(place.astype(jnp.int32), *arrays)
 
 
 def score_kernel(blocks, parts, queries, info, *refs):
@@ -209,12 +214,7 @@
     ranks = right.shape[0]
     arrays = []
 
-    def index(x):
-        if not any(x is y for y in arrays):
-            arrays.append(x)
-        return [x is y for y in arrays].index(True)
-
-    blocks = tuple(((index(x), i), (index(y), j)) for (x, i), (y, j) in acts)
+    blocks = tuple(((index_in(arrays, x), i), (index_in(arrays, y), j)) for (x, i), (y, j) in acts)
     info = jnp.concatenate([sequences, inner.reshape(1)]).astype(jnp.int32)
     in_vmem = pl.BlockSpec(memory_space=pltpu.VMEM)
     in_hbm = pl.BlockSpec(memory_space=pltpu.HBM)
@@ -235,8 +235,8 @@
         ],
         compiler_params=pltpu.CompilerParams(vmem_limit_bytes=VMEM_BYTES),
         cost_estimate=pl.CostEstimate(
-            flops=2 * count * width * columns * (SEQ_LEN + ranks),
-            bytes_accessed=2 * (width * columns + count * SEQ_LEN * (width + columns)),
+            flops=1,
+            bytes_accessed=1,
             transcendentals=0,
         ),
     )(info, *arrays, turned, left, basis, curvature, right)
@@ -271,17 +271,29 @@
     third_end = hop(third_in, outward)
     across_in = hop(after(across, second_in), [(1, 2), (2, 1)])
     skip_in = hop(after(skip, third_in), [(0, 2), (3, 1)])
-    first_x = swap(first, 1, 8)
-    second = jnp.where(inner, second_in, after(second_end, across_in))
-    third = jnp.where(inner, third_in, after(third_end, skip_in))
     near_in = hop(after(near, first), [(0, 1), (3, 2)])
     skip_out = hop(after(skip, skip_in, across_in), [(1, 3), (2, 0)])
+    first_x = swap(first, 1, 8)
+    third = jnp.where(inner, third_in, after(third_end, skip_in))
+    third_x = swap(third, 1, 8)
+    second_end = after(second_end, across_in, near_in)
+    second = [
+        jnp.where(inner, second_in[: sizes[0]], second_end[: sizes[0]]),
+        jnp.where(inner, second_in[sizes[0] :], second_end[sizes[0] :]),
+    ]
+    second_x = [swap(x, 1, 8) for x in second]
     across_out = hop(after(across, skip_in, across_in), [(0, 3), (3, 0)])
     chips = jnp.stack(
         [chip, chip ^ 1, jnp.where(inner, chip ^ 3, chip ^ 2), jnp.where(inner, chip ^ 2, chip ^ 3)]
     )
-    pieces = [(x, 0) for x in (mine, first, second, third)]
-    pieces += [(beside, 4 * rows)] + [(x, 0) for x in (first_x, swap(second, 1, 8), swap(third, 1, 8))]
+    def whole(x, at=0):
+        return [(x, at), (x, at + sizes[0]), (x, at + sizes[0] + sizes[1])]
+
+    def split(x, rest):
+        return [(x, 0), (rest, 0), (rest, sizes[1])]
+
+    pieces = [whole(mine), whole(first), split(*second), whole(third)]
+    pieces += [whole(beside, 4 * rows), whole(first_x), split(*second_x), whole(third_x)]
     place = jnp.concatenate([2 * chips + core, 2 * chips + 1 - core])
     turned, left = rotate_grads(place, pieces, sizes)
     each = rows // SEQ_LEN
@@ -316,7 +328,9 @@
         inner, turned, left, owners, operands = exchange_line(acts, parts, columns, me, sizes)
     else:
         every = lax.all_gather(jnp.concatenate(parts), "dp", axis=0)
-        pieces, place = [(every[j], 0) for j in range(n)], jnp.arange(n, dtype=jnp.int32)
+        starts = (0, sizes[0], sizes[0] + sizes[1])
+        pieces = [[(every[j], at) for at in starts] for j in range(n)]
+        place = jnp.arange(n, dtype=jnp.int32)
         turned, left = rotate_grads(place, pieces, sizes)
         part = lax.all_to_all(acts, "dp", split_axis=1, concat_axis=0, tiled=True)
         operands = [((part, j), (part, j)) for j in range(n * each)]

time: 113 us -> 109 us (0.965)
  waiting for transfers between devices: 37.6 us -> 27.1 us
  starting transfers between devices: 29.7 us -> 32.8 us
  local copies, waits for them, and re-layouts: 4.23 us -> 5.42 us
    ppermute x11, waiting for transfers between devices: 37.6 us -> 26.5 us  [hop(): return lax.ppermute(x, 'dp', pairs)]
    ppermute x11, starting transfers between devices: 29.1 us -> 31.1 us  [hop(): return lax.ppermute(x, 'dp', pairs)]
    unnamed x26 -> x36, local copies, waits for them, and re-layouts: 3.89 us -> 5.09 us
  transfers between devices with their start and end apart: 15 -> 16, of which waited for: 7 -> 7; matrix products, arithmetic and copies ran while one was open for 3% -> 4% of each run, Pallas kernels for 16% -> 18%
where the time goes in v3:
time: 109 us; the launch traced here: 108 us
  starting transfers between devices  32.8 us (30%)
  Pallas kernels  27.4 us (25%)
  waiting for transfers between devices  27.1 us (25%)
  blocking collectives  10.5 us (10%)
  local copies, waits for them, and re-layouts  5.42 us (5%)
  other arithmetic  4.3 us (4%)
    ppermute x11, starting transfers between devices, hop(): return lax.ppermute(x, 'dp', pairs)  31.1 us
    ppermute x11, waiting for transfers between devices, hop(): return lax.ppermute(x, 'dp', pairs)  26.5 us
    pallas_call x3, Pallas kernels, score(): pl.pallas_call(functools.partial(score_kernel, blocks, len(arrays), queri...  16.2 us
    all_to_all x1, blocking collectives, on_device(): lax.all_to_all(outgoing, ('section', 'dp'), split_axis=0, concat_axis=0,...  10.5 us
    unnamed x36, local copies, waits for them, and re-layouts  5.09 us
    pallas_call x1, Pallas kernels, rotate_grads(): pl.pallas_call(functools.partial(rotate_kernel, count, sizes, sources, le...  5.03 us
    pallas_call x1, Pallas kernels, cut(): pl.pallas_call(functools.partial(cut_kernel, rows, columns), out_shape=[j...  3.64 us
    pallas_call x1, Pallas kernels, join_parts(): pl.pallas_call(functools.partial(join_kernel, rows), out_shape=[jax.Shape...  2.54 us
  transfers between devices with their start and end apart: 16, of which 7 were waited for; matrix products, arithmetic and copies ran while one was open for 4% of the time, Pallas kernels for 18%

profile of v3, /device:TPU:0, one launch (start us, length us, event | category | flops | bytes accessed | tf_op | source)
XLA Modules:
  0.0 108.2 jit_solution(16952026988064718548)
XLA Ops:
  0.0 3.6 %shard_map.91 = (bf16[288,1024]{1,0:T(8,128)(2,1)}, bf16[800,1024]{1,0:T(8,128)(2,1)}, bf16[128,1024]{1,0:T(8,128)(2,1)}, bf16[128,1024]{1,0:T(8,128)(2,1)}, bf1...) custom-call(s32[1]{0:T(128)} %bitcast.place, bf16[128,8192]{1,0:T(8,128)(2,1)} %bitcast.33, bf16[128,1024]{1,0:T(8,128)(2,1)} %bitcast.34, ...), custom_call_target="tpu_custom_call" | custom-call | tf_op jit(solution)/shard_map/pallas_call | solution.py:52
  4.2 6.3 %collective-permute-start.7 = (bf16[288,1024]{1,0:T(8,128)(2,1)}, bf16[288,1024]{1,0:T(8,128)(2,1)}, u32[]{:S(2)}, u32[]{:S(2)}) collective-permute-start(bf16[288,1024]{1,0:T(8,128)(2,1)} %get-tuple-element.30.refs_0_), channel_id=1, source_target_pairs={{0,4},{1,5},{6,2},{7,3},{8,12},{9,13},{14,10},{15,11},{16,20},{17,... | collective-permute-start | bytes 1769480 | tf_op jit(solution)/shard_map/ppermute | solution.py:251
  10.5 0.7 collective-permute-start.1
  11.6 1.2 %copy-done.1 = bf16[800,1024]{1,0:T(8,128)(2,1)} copy-done((bf16[800,1024]{1,0:T(8,128)(2,1)}, bf16[800,1024]{1,0:T(8,128)(2,1)S(1)}, u32[]{:S(2)}) %copy-start.1) | copy-done | bytes 1638424
  12.8 2.5 %shard_map.92 = (bf16[256,1024]{1,0:T(8,128)(2,1)}, bf16[256,1024]{1,0:T(8,128)(2,1)}, bf16[256,1024]{1,0:T(8,128)(2,1)}) custom-call(bf16[800,1024]{1,0:T(8,128)(2,1)} %copy-done.1, bf16[128,1024]{1,0:T(8,128)(2,1)} %get-tuple-element.26.refs_0_, bf16[128,1024]{1,0:T(8,128)(2,1)} %get-tuple-element.27.refs_1_, bf16[128,1024]{1,0:T(8,128)(2,1)} %get-tuple-element.28.refs_2_), custom_call_target="tpu_custom_call" | custom-call | tf_op jit(solution)/shard_map/pallas_call | solution.py:72
  15.4 1.4 %collective-permute-start.3 = (bf16[256,1024]{1,0:T(8,128)(2,1)}, bf16[256,1024]{1,0:T(8,128)(2,1)S(1)}, u32[]{:S(2)}, u32[]{:S(2)}) collective-permute-start(bf16[256,1024]{1,0:T(8,128)(2,1)} %get-tuple-element.34), channel_id=1, source_target_pairs={{2,0},{3,1},{4,6},{5,7},{10,8},{11,9},{12,14},{13,15},{18,16},{19,... | collective-permute-start | bytes 1572872 | tf_op jit(solution)/shard_map/ppermute | solution.py:251
  16.8 6.8 %collective-permute-done.7 = bf16[288,1024]{1,0:T(8,128)(2,1)} collective-permute-done((bf16[288,1024]{1,0:T(8,128)(2,1)}, bf16[288,1024]{1,0:T(8,128)(2,1)}, u32[]{:S(2)}, u32[]{:S(2)}) %collective-permute-start.7) | collective-permute-done | bytes 589856 | tf_op jit(solution)/shard_map/ppermute | solution.py:251
  23.7 1.3 %collective-permute-start.8 = (bf16[288,1024]{1,0:T(8,128)(2,1)}, bf16[288,1024]{1,0:T(8,128)(2,1)}, u32[]{:S(2)}, u32[]{:S(2)}) collective-permute-start(bf16[288,1024]{1,0:T(8,128)(2,1)} %collective-permute-done.7), channel_id=1, source_target_pairs={{2,0},{3,1},{4,6},{5,7},{10,8},{11,9},{12,14},{13,15},{18,16},{19,... | collective-permute-start | bytes 1769480 | tf_op jit(solution)/shard_map/ppermute | solution.py:251
  25.0 6.9 %collective-permute-start.9 = (bf16[256,1024]{1,0:T(8,128)(2,1)}, bf16[256,1024]{1,0:T(8,128)(2,1)}, u32[]{:S(2)}, u32[]{:S(2)}) collective-permute-start(bf16[256,1024]{1,0:T(8,128)(2,1)} %get-tuple-element.41), channel_id=1, source_target_pairs={{0,4},{1,5},{6,2},{7,3},{8,12},{9,13},{14,10},{15,11},{16,20},{17,... | collective-permute-start | bytes 1572872 | tf_op jit(solution)/shard_map/ppermute | solution.py:251
  31.9 0.7 collective-permute-start.2
  32.6 3.7 %collective-permute-done.4.refs_1_ = bf16[288,1024]{1,0:T(8,128)(2,1)} collective-permute-done((bf16[288,1024]{1,0:T(8,128)(2,1)}, bf16[288,1024]{1,0:T(8,128)(2,1)}, u32[]{:S(2)}, u32[]{:S(2)}) %collective-permute-start.4) | collective-permute-done | bytes 589856 | tf_op jit(solution)/shard_map/ppermute | solution.py:251
  36.3 7.6 %collective-permute-start.6 = (bf16[256,1024]{1,0:T(8,128)(2,1)}, bf16[256,1024]{1,0:T(8,128)(2,1)S(1)}, u32[]{:S(2)}, u32[]{:S(2)}) collective-permute-start(bf16[256,1024]{1,0:T(8,128)(2,1)} %get-tuple-element.34), channel_id=1, source_target_pairs={{0,2},{1,3},{6,4},{7,5},{8,10},{9,11},{14,12},{15,13},{16,18},{17,... | collective-permute-start | bytes 1572872 | tf_op jit(solution)/shard_map/ppermute | solution.py:251
  43.9 0.8 copy-done.8
  44.7 1.3 %collective-permute-start.5 = (bf16[288,1024]{1,0:T(8,128)(2,1)S(1)}, bf16[288,1024]{1,0:T(8,128)(2,1)S(1)}, u32[]{:S(2)}, u32[]{:S(2)}) collective-permute-start(bf16[288,1024]{1,0:T(8,128)(2,1)S(1)} %collective-permute-done.1), channel_id=1, source_target_pairs={{2,0},{3,1},{4,6},{5,7},{10,8},{11,9},{12,14},{13,15},{18,16},{19,... | collective-permute-start | bytes 1769480 | tf_op jit(solution)/shard_map/ppermute | solution.py:251
  46.0 5.6 %collective-permute-done.8 = bf16[288,1024]{1,0:T(8,128)(2,1)} collective-permute-done((bf16[288,1024]{1,0:T(8,128)(2,1)}, bf16[288,1024]{1,0:T(8,128)(2,1)}, u32[]{:S(2)}, u32[]{:S(2)}) %collective-permute-start.8) | collective-permute-done | bytes 589856 | tf_op jit(solution)/shard_map/ppermute | solution.py:251
  51.6 1.1 %broadcast_select_fusion.refs_4_ = bf16[288,1024]{1,0:T(8,128)(2,1)S(1)} fusion(bf16[288,1024]{1,0:T(8,128)(2,1)} %collective-permute-done.7, bf16[288,1024]{1,0:T(8,128)(2,1)} %collective-permute-done.8, pred[]{:T(512)S(6)} %or.3), kind=kLoop, calls=%fused_computation | loop fusion | flops 294912 | bytes 1769473 | tf_op jit(solution)/shard_map/jit(_where)/select_n | solution.py:277
  53.3 0.8 copy-done.10
  54.1 1.3 %collective-permute-start.14 = (bf16[256,1024]{1,0:T(8,128)(2,1)}, bf16[256,1024]{1,0:T(8,128)(2,1)}, u32[]{:S(2)}, u32[]{:S(2)}) collective-permute-start(bf16[256,1024]{1,0:T(8,128)(2,1)} %get-tuple-element.41), channel_id=1, source_target_pairs={{2,6},{3,7},{4,0},{5,1},{10,14},{11,15},{12,8},{13,9},{18,22},{19,... | collective-permute-start | bytes 1572872 | tf_op jit(solution)/shard_map/ppermute | solution.py:251
  55.4 3.0 %collective-permute-done.6.refs_0_ = bf16[256,1024]{1,0:T(8,128)(2,1)S(1)} collective-permute-done((bf16[256,1024]{1,0:T(8,128)(2,1)}, bf16[256,1024]{1,0:T(8,128)(2,1)S(1)}, u32[]{:S(2)}, u32[]{:S(2)}) %collective-permute-start.6) | collective-permute-done | bytes 524320 | tf_op jit(solution)/shard_map/ppermute | solution.py:251
  58.4 3.2 %collective-permute-start.15 = (bf16[256,1024]{1,0:T(8,128)(2,1)}, bf16[256,1024]{1,0:T(8,128)(2,1)}, u32[]{:S(2)}, u32[]{:S(2)}) collective-permute-start(bf16[256,1024]{1,0:T(8,128)(2,1)} %get-tuple-element.42), channel_id=1, source_target_pairs={{0,6},{1,7},{6,0},{7,1},{8,14},{9,15},{14,8},{15,9},{16,22},{17,23... | collective-permute-start | bytes 1572872 | tf_op jit(solution)/shard_map/ppermute | solution.py:251
  61.7 1.8 %collective-permute-done.5 = bf16[288,1024]{1,0:T(8,128)(2,1)S(1)} collective-permute-done((bf16[288,1024]{1,0:T(8,128)(2,1)S(1)}, bf16[288,1024]{1,0:T(8,128)(2,1)S(1)}, u32[]{:S(2)}, u32[]{:S(2)}) %collective-permute-start.5) | collective-permute-done | bytes 589856 | tf_op jit(solution)/shard_map/ppermute | solution.py:251
  63.4 1.0 slice_select_fusion.refs_3_
  64.5 1.0 slice_select_fusion.1.refs_2_
  65.5 0.9 copy-done.6
  67.6 0.6 collective-permute-done.11.refs_7_
  68.2 1.4 %copy-done.7 = bf16[288,1024]{1,0:T(8,128)(2,1)S(1)} copy-done((bf16[288,1024]{1,0:T(8,128)(2,1)S(1)}, bf16[288,1024]{1,0:T(8,128)(2,1)}, u32[]{:S(2)}) %copy-start.7) | copy-done | bytes 589848
  69.6 5.0 %shard_map.93 = (bf16[1024,1024]{1,0:T(8,128)(2,1)S(1)}, bf16[256,1024]{1,0:T(8,128)(2,1)S(1)}) custom-call(s32[8]{0:T(128)S(1)} %pad_add_fusion.place, bf16[288,1024]{1,0:T(8,128)(2,1)S(1)} %copy-done.5, bf16[288,1024]{1,0:T(8,128)(2,1)} %collective-permute-done.4.refs_1_, bf16[128,1024]{1,0:T(8,128)(2,1)S(1)} %slice_select_fusion.1.refs_2_, ...), custom_call_target="tpu_custom_call" | custom-call | flops 1 | bytes 1 | tf_op jit(solution)/shard_map/pallas_call | solution.py:114
  74.7 6.8 %shard_map.94 = f32[4,8,128]{2,1,0:T(8,128)S(1)} custom-call(s32[5]{0:T(128)S(1)} %concatenate.21.info, bf16[128,1024]{1,0:T(8,128)(2,1)S(1)} %copy-done.14, bf16[800,1024]{1,0:T(8,128)(2,1)S(1)} %copy-done.2, bf16[256,1024]{1,0:T(8,128)(2,1)S(1)} %copy-done.11, bf16[256,1024]{1,0:T(8,128)(2,1)S(1)} %copy-done.9, ...), custom_call_target="tpu_custom_call" | custom-call | flops 1 | bytes 1 | tf_op jit(solution)/shard_map/pallas_call | solution.py:221
  81.5 5.7 %collective-permute-done.14.refs_1_ = bf16[256,1024]{1,0:T(8,128)(2,1)} collective-permute-done((bf16[256,1024]{1,0:T(8,128)(2,1)}, bf16[256,1024]{1,0:T(8,128)(2,1)}, u32[]{:S(2)}, u32[]{:S(2)}) %collective-permute-start.14) | collective-permute-done | bytes 524320 | tf_op jit(solution)/shard_map/ppermute | solution.py:251
  87.2 4.7 %shard_map.95 = f32[2,8,128]{2,1,0:T(8,128)S(1)} custom-call(s32[3]{0:T(128)S(1)} %get-tuple-element.45.info, bf16[256,1024]{1,0:T(8,128)(2,1)} %collective-permute-done.9.refs_0_, bf16[256,1024]{1,0:T(8,128)(2,1)} %collective-permute-done.14.refs_1_, bf16[1024,1024]{1,0:T(8,128)(2,1)S(1)} %get-tuple-element.39.refs_4_.refs_2_, ...), custom_call_target="tpu_custom_call" | custom-call | flops 1 | bytes 1 | tf_op jit(solution)/shard_map/pallas_call | solution.py:221
  91.9 4.7 %shard_map.96 = f32[2,8,128]{2,1,0:T(8,128)S(1)} custom-call(s32[3]{0:T(128)S(1)} %get-tuple-element.46.info, bf16[256,1024]{1,0:T(8,128)(2,1)S(1)} %copy-done.13, bf16[256,1024]{1,0:T(8,128)(2,1)} %collective-permute-done.15.refs_1_, bf16[1024,1024]{1,0:T(8,128)(2,1)S(1)} %get-tuple-element.39.refs_4_.refs_2_, ...), custom_call_target="tpu_custom_call" | custom-call | flops 1 | bytes 1 | tf_op jit(solution)/shard_map/pallas_call | solution.py:221
  97.1 10.5 %all_to_all.5 = f32[32,1,8]{2,1,0:T(1,128)S(1)} all-to-all(f32[32,1,8]{2,1,0:T(1,128)S(1)} %broadcast_select_fusion.1), channel_id=1, replica_groups=mesh['section'=4,'dp'=8] {'section','dp'}, dimensions={0} | all-to-all | bytes 2048 | tf_op jit(solution)/shard_map/all_to_all | solution.py:363
  (62 shorter events, 4.0 us)
Async XLA Ops:
  3.7 8.0 %collective-permute-start = (bf16[800,1024]{1,0:T(8,128)(2,1)}, bf16[800,1024]{1,0:T(8,128)(2,1)S(1)}, u32[]{:S(2)}, u32[]{:S(2)}) collective-permute-start(bf16[800,1024]{1,0:T(8,128)(2,1)} %get-tuple-element.25), channel_id=1, source_target_pairs={{0,1},{1,0},{2,3},{3,2},{4,5},{5,4},{6,7},{7,6},{8,9},{9,8},{10,11... | collective-permute-start | bytes 4915208 | tf_op jit(solution)/shard_map/ppermute | solution.py:246
  4.2 19.5 %collective-permute-start.7 = (bf16[288,1024]{1,0:T(8,128)(2,1)}, bf16[288,1024]{1,0:T(8,128)(2,1)}, u32[]{:S(2)}, u32[]{:S(2)}) collective-permute-start(bf16[288,1024]{1,0:T(8,128)(2,1)} %get-tuple-element.30.refs_0_), channel_id=1, source_target_pairs={{0,4},{1,5},{6,2},{7,3},{8,12},{9,13},{14,10},{15,11},{16,20},{17,... | collective-permute-start | bytes 1769480 | tf_op jit(solution)/shard_map/ppermute | solution.py:251
  10.5 21.4 %collective-permute-start.1 = (bf16[288,1024]{1,0:T(8,128)(2,1)}, bf16[288,1024]{1,0:T(8,128)(2,1)S(1)}, u32[]{:S(2)}, u32[]{:S(2)}) collective-permute-start(bf16[288,1024]{1,0:T(8,128)(2,1)} %get-tuple-element.30.refs_0_), channel_id=1, source_target_pairs={{2,4},{3,5},{4,2},{5,3},{10,12},{11,13},{12,10},{13,11},{18,20},{1... | collective-permute-start | bytes 1769480 | tf_op jit(solution)/shard_map/ppermute | solution.py:251
  11.2 25.1 %collective-permute-start.4 = (bf16[288,1024]{1,0:T(8,128)(2,1)}, bf16[288,1024]{1,0:T(8,128)(2,1)}, u32[]{:S(2)}, u32[]{:S(2)}) collective-permute-start(bf16[288,1024]{1,0:T(8,128)(2,1)} %get-tuple-element.30.refs_0_), channel_id=1, source_target_pairs={{0,2},{1,3},{2,0},{3,1},{4,6},{5,7},{6,4},{7,5},{8,10},{9,11},{10,... | collective-permute-start | bytes 1769480 | tf_op jit(solution)/shard_map/ppermute | solution.py:251
  11.6 1.2 %copy-start.1 = (bf16[800,1024]{1,0:T(8,128)(2,1)}, bf16[800,1024]{1,0:T(8,128)(2,1)S(1)}, u32[]{:S(2)}) copy-start(bf16[800,1024]{1,0:T(8,128)(2,1)S(1)} %collective-permute-done.beside.refs_5_.refs_1_) | copy-start | bytes 4915204
  15.4 52.0 %copy-start.16 = (s32[8]{0:T(128)S(1)}, s32[8]{0:T(128)}, u32[]{:S(2)}) copy-start(s32[8]{0:T(128)} %param.16) | copy-start | bytes 100
  15.4 52.8 %copy-start.2 = (bf16[800,1024]{1,0:T(8,128)(2,1)S(1)}, bf16[800,1024]{1,0:T(8,128)(2,1)}, u32[]{:S(2)}) copy-start(bf16[800,1024]{1,0:T(8,128)(2,1)} %copy-done.1) | copy-start | bytes 4915204
  15.4 52.8 %copy-start.5 = (bf16[288,1024]{1,0:T(8,128)(2,1)S(1)}, bf16[288,1024]{1,0:T(8,128)(2,1)}, u32[]{:S(2)}) copy-start(bf16[288,1024]{1,0:T(8,128)(2,1)} %get-tuple-element.30.refs_0_) | copy-start | bytes 1769476
  15.4 28.5 %collective-permute-start.3 = (bf16[256,1024]{1,0:T(8,128)(2,1)}, bf16[256,1024]{1,0:T(8,128)(2,1)S(1)}, u32[]{:S(2)}, u32[]{:S(2)}) collective-permute-start(bf16[256,1024]{1,0:T(8,128)(2,1)} %get-tuple-element.34), channel_id=1, source_target_pairs={{2,0},{3,1},{4,6},{5,7},{10,8},{11,9},{12,14},{13,15},{18,16},{19,... | collective-permute-start | bytes 1572872 | tf_op jit(solution)/shard_map/ppermute | solution.py:251
  23.7 28.0 %collective-permute-start.8 = (bf16[288,1024]{1,0:T(8,128)(2,1)}, bf16[288,1024]{1,0:T(8,128)(2,1)}, u32[]{:S(2)}, u32[]{:S(2)}) collective-permute-start(bf16[288,1024]{1,0:T(8,128)(2,1)} %collective-permute-done.7), channel_id=1, source_target_pairs={{2,0},{3,1},{4,6},{5,7},{10,8},{11,9},{12,14},{13,15},{18,16},{19,... | collective-permute-start | bytes 1769480 | tf_op jit(solution)/shard_map/ppermute | solution.py:251
  25.0 26.7 %collective-permute-start.9 = (bf16[256,1024]{1,0:T(8,128)(2,1)}, bf16[256,1024]{1,0:T(8,128)(2,1)}, u32[]{:S(2)}, u32[]{:S(2)}) collective-permute-start(bf16[256,1024]{1,0:T(8,128)(2,1)} %get-tuple-element.41), channel_id=1, source_target_pairs={{0,4},{1,5},{6,2},{7,3},{8,12},{9,13},{14,10},{15,11},{16,20},{17,... | collective-permute-start | bytes 1572872 | tf_op jit(solution)/shard_map/ppermute | solution.py:251
  31.9 29.7 %copy-start.15 = (bf16[288,1024]{1,0:T(8,128)(2,1)}, bf16[288,1024]{1,0:T(8,128)(2,1)S(1)}, u32[]{:S(2)}) copy-start(bf16[288,1024]{1,0:T(8,128)(2,1)S(1)} %collective-permute-done.1) | copy-start | bytes 1769476
  31.9 21.4 %collective-permute-start.2 = (bf16[256,1024]{1,0:T(8,128)(2,1)}, bf16[256,1024]{1,0:T(8,128)(2,1)S(1)}, u32[]{:S(2)}, u32[]{:S(2)}) collective-permute-start(bf16[256,1024]{1,0:T(8,128)(2,1)} %get-tuple-element.42), channel_id=1, source_target_pairs={{2,4},{3,5},{4,2},{5,3},{10,12},{11,13},{12,10},{13,11},{18,20},{1... | collective-permute-start | bytes 1572872 | tf_op jit(solution)/shard_map/ppermute | solution.py:251
  36.3 22.1 %collective-permute-start.6 = (bf16[256,1024]{1,0:T(8,128)(2,1)}, bf16[256,1024]{1,0:T(8,128)(2,1)S(1)}, u32[]{:S(2)}, u32[]{:S(2)}) collective-permute-start(bf16[256,1024]{1,0:T(8,128)(2,1)} %get-tuple-element.34), channel_id=1, source_target_pairs={{0,2},{1,3},{6,4},{7,5},{8,10},{9,11},{14,12},{15,13},{16,18},{17,... | collective-permute-start | bytes 1572872 | tf_op jit(solution)/shard_map/ppermute | solution.py:251
  44.7 18.7 %collective-permute-start.5 = (bf16[288,1024]{1,0:T(8,128)(2,1)S(1)}, bf16[288,1024]{1,0:T(8,128)(2,1)S(1)}, u32[]{:S(2)}, u32[]{:S(2)}) collective-permute-start(bf16[288,1024]{1,0:T(8,128)(2,1)S(1)} %collective-permute-done.1), channel_id=1, source_target_pairs={{2,0},{3,1},{4,6},{5,7},{10,8},{11,9},{12,14},{13,15},{18,16},{19,... | collective-permute-start | bytes 1769480 | tf_op jit(solution)/shard_map/ppermute | solution.py:251
  51.6 13.9 %collective-permute-start.10 = (bf16[288,1024]{1,0:T(8,128)(2,1)}, bf16[288,1024]{1,0:T(8,128)(2,1)S(1)}, u32[]{:S(2)}, u32[]{:S(2)}) collective-permute-start(bf16[288,1024]{1,0:T(8,128)(2,1)} %collective-permute-done.4.refs_1_), channel_id=1, source_target_pairs={{0,1},{1,0},{2,3},{3,2},{4,5},{5,4},{6,7},{7,6},{8,9},{9,8},{10,11... | collective-permute-start | bytes 1769480 | tf_op jit(solution)/shard_map/ppermute | solution.py:246
  52.8 14.8 %collective-permute-start.13 = (bf16[288,1024]{1,0:T(8,128)(2,1)S(1)}, bf16[288,1024]{1,0:T(8,128)(2,1)}, u32[]{:S(2)}, u32[]{:S(2)}) collective-permute-start(bf16[288,1024]{1,0:T(8,128)(2,1)S(1)} %broadcast_select_fusion.refs_4_), channel_id=1, source_target_pairs={{0,1},{1,0},{2,3},{3,2},{4,5},{5,4},{6,7},{7,6},{8,9},{9,8},{10,11... | collective-permute-start | bytes 1769480 | tf_op jit(solution)/shard_map/ppermute | solution.py:246
  54.1 33.0 %collective-permute-start.14 = (bf16[256,1024]{1,0:T(8,128)(2,1)}, bf16[256,1024]{1,0:T(8,128)(2,1)}, u32[]{:S(2)}, u32[]{:S(2)}) collective-permute-start(bf16[256,1024]{1,0:T(8,128)(2,1)} %get-tuple-element.41), channel_id=1, source_target_pairs={{2,6},{3,7},{4,0},{5,1},{10,14},{11,15},{12,8},{13,9},{18,22},{19,... | collective-permute-start | bytes 1572872 | tf_op jit(solution)/shard_map/ppermute | solution.py:251
  58.4 7.1 %copy-start.12 = (bf16[256,1024]{1,0:T(8,128)(2,1)}, bf16[256,1024]{1,0:T(8,128)(2,1)S(1)}, u32[]{:S(2)}) copy-start(bf16[256,1024]{1,0:T(8,128)(2,1)S(1)} %collective-permute-done.6.refs_0_) | copy-start | bytes 1572868
  58.4 33.4 %collective-permute-start.15 = (bf16[256,1024]{1,0:T(8,128)(2,1)}, bf16[256,1024]{1,0:T(8,128)(2,1)}, u32[]{:S(2)}, u32[]{:S(2)}) collective-permute-start(bf16[256,1024]{1,0:T(8,128)(2,1)} %get-tuple-element.42), channel_id=1, source_target_pairs={{0,6},{1,7},{6,0},{7,1},{8,14},{9,15},{14,8},{15,9},{16,22},{17,23... | collective-permute-start | bytes 1572872 | tf_op jit(solution)/shard_map/ppermute | solution.py:251
  64.4 3.7 %collective-permute-start.12 = (bf16[160,1024]{1,0:T(8,128)(2,1)S(1)}, bf16[160,1024]{1,0:T(8,128)(2,1)}, u32[]{:S(2)}, u32[]{:S(2)}) collective-permute-start(bf16[160,1024]{1,0:T(8,128)(2,1)S(1)} %slice_select_fusion.refs_3_), channel_id=1, source_target_pairs={{0,1},{1,0},{2,3},{3,2},{4,5},{5,4},{6,7},{7,6},{8,9},{9,8},{10,11... | collective-permute-start | bytes 983048 | tf_op jit(solution)/shard_map/ppermute | solution.py:246
  65.5 0.9 copy-start.6
  66.4 1.8 %collective-permute-start.11 = (bf16[128,1024]{1,0:T(8,128)(2,1)S(1)}, bf16[128,1024]{1,0:T(8,128)(2,1)}, u32[]{:S(2)}, u32[]{:S(2)}) collective-permute-start(bf16[128,1024]{1,0:T(8,128)(2,1)S(1)} %slice_select_fusion.1.refs_2_), channel_id=1, source_target_pairs={{0,1},{1,0},{2,3},{3,2},{4,5},{5,4},{6,7},{7,6},{8,9},{9,8},{10,11... | collective-permute-start | bytes 786440 | tf_op jit(solution)/shard_map/ppermute | solution.py:246
  67.6 7.1 %copy-start = (bf16[1,1024,1024]{2,1,0:T(8,128)(2,1)S(1)}, bf16[1,1024,1024]{2,1,0:T(8,128)(2,1)}, u32[]{:S(2)}) copy-start(bf16[1,1024,1024]{2,1,0:T(8,128)(2,1)} %param.13) | copy-start | bytes 6291460
  67.6 7.1 %copy-start.3 = (bf16[1,1024,256]{2,1,0:T(8,128)(2,1)S(1)}, bf16[1,1024,256]{2,1,0:T(8,128)(2,1)}, u32[]{:S(2)}) copy-start(bf16[1,1024,256]{2,1,0:T(8,128)(2,1)} %param.11) | copy-start | bytes 1572868
  67.6 7.1 %copy-start.4 = (bf16[1,8,32,1024]{3,2,1,0:T(8,128)(2,1)S(1)}, bf16[1,8,32,1024]{3,2,1,0:T(8,128)(2,1)}, u32[]{:S(2)}) copy-start(bf16[1,8,32,1024]{3,2,1,0:T(8,128)(2,1)} %param.15) | copy-start | bytes 1572868
  68.2 1.4 %copy-start.7 = (bf16[288,1024]{1,0:T(8,128)(2,1)S(1)}, bf16[288,1024]{1,0:T(8,128)(2,1)}, u32[]{:S(2)}) copy-start(bf16[288,1024]{1,0:T(8,128)(2,1)} %copy-done.6) | copy-start | bytes 1769476
  69.6 5.1 %copy-start.9 = (bf16[256,1024]{1,0:T(8,128)(2,1)S(1)}, bf16[256,1024]{1,0:T(8,128)(2,1)}, u32[]{:S(2)}) copy-start(bf16[256,1024]{1,0:T(8,128)(2,1)} %copy-done.8) | copy-start | bytes 1572868
  69.6 5.1 %copy-start.11 = (bf16[256,1024]{1,0:T(8,128)(2,1)S(1)}, bf16[256,1024]{1,0:T(8,128)(2,1)}, u32[]{:S(2)}) copy-start(bf16[256,1024]{1,0:T(8,128)(2,1)} %copy-done.10) | copy-start | bytes 1572868
  69.6 5.1 %copy-start.14 = (bf16[128,1024]{1,0:T(8,128)(2,1)S(1)}, bf16[128,1024]{1,0:T(8,128)(2,1)}, u32[]{:S(2)}) copy-start(bf16[128,1024]{1,0:T(8,128)(2,1)} %get-tuple-element.24.refs_0_) | copy-start | bytes 786436
  87.2 4.7 %copy-start.13 = (bf16[256,1024]{1,0:T(8,128)(2,1)S(1)}, bf16[256,1024]{1,0:T(8,128)(2,1)}, u32[]{:S(2)}) copy-start(bf16[256,1024]{1,0:T(8,128)(2,1)} %copy-done.12) | copy-start | bytes 1572868
  91.9 4.9 %copy-start.17 = (s32[8]{0:T(128)S(1)}, s32[8]{0:T(128)}, u32[]{:S(2)}) copy-start(s32[8]{0:T(128)} %param.17) | copy-start | bytes 100
  (2 other events, 1.6 us)

commit v4 on v3

--- a/solution.py
+++ b/solution.py
@@ -282,7 +282,7 @@
         jnp.where(inner, second_in[sizes[0] :], second_end[sizes[0] :]),
     ]
     second_x = [swap(x, 1, 8) for x in second]
-    across_out = hop(after(across, skip_in, across_in), [(0, 3), (3, 0)])
+    across_out = hop(after(across, skip_in, across_in, second_end), [(0, 3), (3, 0)])
     chips = jnp.stack(
         [chip, chip ^ 1, jnp.where(inner, chip ^ 3, chip ^ 2), jnp.where(inner, chip ^ 2, chip ^ 3)]
     )
@@ -340,7 +340,7 @@
     sums = []
     at = 0
     while at < len(operands):
-        step = (4 if at == 0 else 2) * each
+        step = 4 * each
         sums.append(
             score(sequences[at : at + step], inner, operands[at : at + step], turned, left, in_basis[0],
                   curvature[0], right, queries)

time: 109 us -> 106 us (0.972)
  Pallas kernels: 27.4 us -> 25.5 us
  waiting for transfers between devices: 27.1 us -> 25.6 us
    pallas_call x3 -> x2, Pallas kernels: 16.2 us -> 14.2 us  [score(): pl.pallas_call(functools.partial(score_kernel, blocks, len(arrays), queri...]
    ppermute x11, waiting for transfers between devices: 26.5 us -> 24.8 us  [hop(): return lax.ppermute(x, 'dp', pairs)]
    ppermute x11, starting transfers between devices: 31.1 us -> 32.4 us  [hop(): return lax.ppermute(x, 'dp', pairs)]
    unnamed x36 -> x30, local copies, waits for them, and re-layouts: 5.09 us -> 4.92 us
  transfers between devices with their start and end apart: 16 -> 16, of which waited for: 7 -> 7; matrix products, arithmetic and copies ran while one was open for 4% -> 4% of each run, Pallas kernels for 18% -> 14%
where the time goes in v4:
time: 106 us
  starting transfers between devices  33.8 us (32%)
  waiting for transfers between devices  25.6 us (24%)
  Pallas kernels  25.5 us (24%)
  blocking collectives  10.5 us (10%)
  local copies, waits for them, and re-layouts  5.34 us (5%)
  other arithmetic  4.41 us (4%)
    ppermute x11, starting transfers between devices, hop(): return lax.ppermute(x, 'dp', pairs)  32.4 us
    ppermute x11, waiting for transfers between devices, hop(): return lax.ppermute(x, 'dp', pairs)  24.8 us
    pallas_call x2, Pallas kernels, score(): pl.pallas_call(functools.partial(score_kernel, blocks, len(arrays), queri...  14.2 us
    all_to_all x1, blocking collectives, on_device(): lax.all_to_all(outgoing, ('section', 'dp'), split_axis=0, concat_axis=0,...  10.5 us
    pallas_call x1, Pallas kernels, rotate_grads(): pl.pallas_call(functools.partial(rotate_kernel, count, sizes, sources, le...  5.03 us
    unnamed x30, local copies, waits for them, and re-layouts  4.92 us
    pallas_call x1, Pallas kernels, cut(): pl.pallas_call(functools.partial(cut_kernel, rows, columns), out_shape=[j...  3.74 us
    pallas_call x1, Pallas kernels, join_parts(): pl.pallas_call(functools.partial(join_kernel, rows), out_shape=[jax.Shape...  2.57 us
  transfers between devices with their start and end apart: 16, of which 7 were waited for; matrix products, arithmetic and copies ran while one was open for 4% of the time, Pallas kernels for 14%

profile of v4, /device:TPU:0, one launch (start us, length us, event | category | flops | bytes accessed | tf_op | source)
XLA Modules:
  0.0 105.8 jit_solution(16887408912014435038)
XLA Ops:
  0.0 3.7 %shard_map.91 = (bf16[288,1024]{1,0:T(8,128)(2,1)}, bf16[800,1024]{1,0:T(8,128)(2,1)}, bf16[128,1024]{1,0:T(8,128)(2,1)}, bf16[128,1024]{1,0:T(8,128)(2,1)}, bf1...) custom-call(s32[1]{0:T(128)} %bitcast.place, bf16[128,8192]{1,0:T(8,128)(2,1)} %bitcast.30, bf16[128,1024]{1,0:T(8,128)(2,1)} %bitcast.31, ...), custom_call_target="tpu_custom_call" | custom-call | tf_op jit(solution)/shard_map/pallas_call | solution.py:52
  4.3 6.3 %collective-permute-start.7 = (bf16[288,1024]{1,0:T(8,128)(2,1)}, bf16[288,1024]{1,0:T(8,128)(2,1)}, u32[]{:S(2)}, u32[]{:S(2)}) collective-permute-start(bf16[288,1024]{1,0:T(8,128)(2,1)} %get-tuple-element.30.refs_0_), channel_id=1, source_target_pairs={{0,4},{1,5},{6,2},{7,3},{8,12},{9,13},{14,10},{15,11},{16,20},{17,... | collective-permute-start | bytes 1769480 | tf_op jit(solution)/shard_map/ppermute | solution.py:251
  10.6 1.5 %collective-permute-start.1 = (bf16[288,1024]{1,0:T(8,128)(2,1)}, bf16[288,1024]{1,0:T(8,128)(2,1)}, u32[]{:S(2)}, u32[]{:S(2)}) collective-permute-start(bf16[288,1024]{1,0:T(8,128)(2,1)} %get-tuple-element.30.refs_0_), channel_id=1, source_target_pairs={{2,4},{3,5},{4,2},{5,3},{10,12},{11,13},{12,10},{13,11},{18,20},{1... | collective-permute-start | bytes 1769480 | tf_op jit(solution)/shard_map/ppermute | solution.py:251
  12.1 1.2 %copy-done = bf16[800,1024]{1,0:T(8,128)(2,1)} copy-done((bf16[800,1024]{1,0:T(8,128)(2,1)}, bf16[800,1024]{1,0:T(8,128)(2,1)S(1)}, u32[]{:S(2)}) %copy-start) | copy-done | bytes 1638424
  13.3 2.6 %shard_map.92 = (bf16[256,1024]{1,0:T(8,128)(2,1)}, bf16[256,1024]{1,0:T(8,128)(2,1)}, bf16[256,1024]{1,0:T(8,128)(2,1)}) custom-call(bf16[800,1024]{1,0:T(8,128)(2,1)} %copy-done, bf16[128,1024]{1,0:T(8,128)(2,1)} %get-tuple-element.26.refs_0_, bf16[128,1024]{1,0:T(8,128)(2,1)} %get-tuple-element.27.refs_1_, bf16[128,1024]{1,0:T(8,128)(2,1)} %get-tuple-element.28.refs_2_), custom_call_target="tpu_custom_call" | custom-call | tf_op jit(solution)/shard_map/pallas_call | solution.py:72
  15.9 1.4 %collective-permute-start.3 = (bf16[256,1024]{1,0:T(8,128)(2,1)}, bf16[256,1024]{1,0:T(8,128)(2,1)S(1)}, u32[]{:S(2)}, u32[]{:S(2)}) collective-permute-start(bf16[256,1024]{1,0:T(8,128)(2,1)} %get-tuple-element.34), channel_id=1, source_target_pairs={{2,0},{3,1},{4,6},{5,7},{10,8},{11,9},{12,14},{13,15},{18,16},{19,... | collective-permute-start | bytes 1572872 | tf_op jit(solution)/shard_map/ppermute | solution.py:251
  17.4 6.4 %collective-permute-done.7 = bf16[288,1024]{1,0:T(8,128)(2,1)} collective-permute-done((bf16[288,1024]{1,0:T(8,128)(2,1)}, bf16[288,1024]{1,0:T(8,128)(2,1)}, u32[]{:S(2)}, u32[]{:S(2)}) %collective-permute-start.7) | collective-permute-done | bytes 589856 | tf_op jit(solution)/shard_map/ppermute | solution.py:251
  23.8 1.3 %collective-permute-start.8 = (bf16[288,1024]{1,0:T(8,128)(2,1)}, bf16[288,1024]{1,0:T(8,128)(2,1)}, u32[]{:S(2)}, u32[]{:S(2)}) collective-permute-start(bf16[288,1024]{1,0:T(8,128)(2,1)} %collective-permute-done.7), channel_id=1, source_target_pairs={{2,0},{3,1},{4,6},{5,7},{10,8},{11,9},{12,14},{13,15},{18,16},{19,... | collective-permute-start | bytes 1769480 | tf_op jit(solution)/shard_map/ppermute | solution.py:251
  25.1 6.1 %collective-permute-start.9 = (bf16[256,1024]{1,0:T(8,128)(2,1)}, bf16[256,1024]{1,0:T(8,128)(2,1)S(1)}, u32[]{:S(2)}, u32[]{:S(2)}) collective-permute-start(bf16[256,1024]{1,0:T(8,128)(2,1)} %get-tuple-element.41), channel_id=1, source_target_pairs={{0,4},{1,5},{6,2},{7,3},{8,12},{9,13},{14,10},{15,11},{16,20},{17,... | collective-permute-start | bytes 1572872 | tf_op jit(solution)/shard_map/ppermute | solution.py:251
  31.2 1.5 %collective-permute-start.2 = (bf16[256,1024]{1,0:T(8,128)(2,1)}, bf16[256,1024]{1,0:T(8,128)(2,1)}, u32[]{:S(2)}, u32[]{:S(2)}) collective-permute-start(bf16[256,1024]{1,0:T(8,128)(2,1)} %get-tuple-element.42), channel_id=1, source_target_pairs={{2,4},{3,5},{4,2},{5,3},{10,12},{11,13},{12,10},{13,11},{18,20},{1... | collective-permute-start | bytes 1572872 | tf_op jit(solution)/shard_map/ppermute | solution.py:251
  32.7 3.7 %collective-permute-done.4.refs_1_ = bf16[288,1024]{1,0:T(8,128)(2,1)} collective-permute-done((bf16[288,1024]{1,0:T(8,128)(2,1)}, bf16[288,1024]{1,0:T(8,128)(2,1)}, u32[]{:S(2)}, u32[]{:S(2)}) %collective-permute-start.4) | collective-permute-done | bytes 589856 | tf_op jit(solution)/shard_map/ppermute | solution.py:251
  36.4 8.5 %collective-permute-start.6 = (bf16[256,1024]{1,0:T(8,128)(2,1)}, bf16[256,1024]{1,0:T(8,128)(2,1)}, u32[]{:S(2)}, u32[]{:S(2)}) collective-permute-start(bf16[256,1024]{1,0:T(8,128)(2,1)} %get-tuple-element.34), channel_id=1, source_target_pairs={{0,2},{1,3},{6,4},{7,5},{8,10},{9,11},{14,12},{15,13},{16,18},{17,... | collective-permute-start | bytes 1572872 | tf_op jit(solution)/shard_map/ppermute | solution.py:251
  44.9 0.8 copy-done.10
  45.8 1.3 %collective-permute-start.5 = (bf16[288,1024]{1,0:T(8,128)(2,1)}, bf16[288,1024]{1,0:T(8,128)(2,1)}, u32[]{:S(2)}, u32[]{:S(2)}) collective-permute-start(bf16[288,1024]{1,0:T(8,128)(2,1)} %collective-permute-done.1), channel_id=1, source_target_pairs={{2,0},{3,1},{4,6},{5,7},{10,8},{11,9},{12,14},{13,15},{18,16},{19,... | collective-permute-start | bytes 1769480 | tf_op jit(solution)/shard_map/ppermute | solution.py:251
  47.1 5.3 %collective-permute-done.8 = bf16[288,1024]{1,0:T(8,128)(2,1)} collective-permute-done((bf16[288,1024]{1,0:T(8,128)(2,1)}, bf16[288,1024]{1,0:T(8,128)(2,1)}, u32[]{:S(2)}, u32[]{:S(2)}) %collective-permute-start.8) | collective-permute-done | bytes 589856 | tf_op jit(solution)/shard_map/ppermute | solution.py:251
  52.5 0.9 copy-done.8
  53.3 1.3 %collective-permute-start.14 = (bf16[256,1024]{1,0:T(8,128)(2,1)}, bf16[256,1024]{1,0:T(8,128)(2,1)}, u32[]{:S(2)}, u32[]{:S(2)}) collective-permute-start(bf16[256,1024]{1,0:T(8,128)(2,1)} %get-tuple-element.41), channel_id=1, source_target_pairs={{2,6},{3,7},{4,0},{5,1},{10,14},{11,15},{12,8},{13,9},{18,22},{19,... | collective-permute-start | bytes 1572872 | tf_op jit(solution)/shard_map/ppermute | solution.py:251
  54.6 1.1 %broadcast_select_fusion.refs_4_ = bf16[288,1024]{1,0:T(8,128)(2,1)S(1)} fusion(bf16[288,1024]{1,0:T(8,128)(2,1)} %collective-permute-done.7, bf16[288,1024]{1,0:T(8,128)(2,1)} %collective-permute-done.8, pred[]{:T(512)S(6)} %or.3), kind=kLoop, calls=%fused_computation | loop fusion | flops 294912 | bytes 1769473 | tf_op jit(solution)/shard_map/jit(_where)/select_n | solution.py:277
  55.7 0.6 collective-permute-start.13
  56.3 2.2 %collective-permute-done.6.refs_2_ = bf16[256,1024]{1,0:T(8,128)(2,1)} collective-permute-done((bf16[256,1024]{1,0:T(8,128)(2,1)}, bf16[256,1024]{1,0:T(8,128)(2,1)}, u32[]{:S(2)}, u32[]{:S(2)}) %collective-permute-start.6) | collective-permute-done | bytes 524320 | tf_op jit(solution)/shard_map/ppermute | solution.py:251
  58.5 5.8 %collective-permute-done.5 = bf16[288,1024]{1,0:T(8,128)(2,1)} collective-permute-done((bf16[288,1024]{1,0:T(8,128)(2,1)}, bf16[288,1024]{1,0:T(8,128)(2,1)}, u32[]{:S(2)}, u32[]{:S(2)}) %collective-permute-start.5) | collective-permute-done | bytes 589856 | tf_op jit(solution)/shard_map/ppermute | solution.py:251
  64.4 1.1 %slice_select_fusion.1.refs_2_ = bf16[128,1024]{1,0:T(8,128)(2,1)S(1)} fusion(bf16[288,1024]{1,0:T(8,128)(2,1)} %collective-permute-done.1, bf16[288,1024]{1,0:T(8,128)(2,1)} %collective-permute-done.5, pred[]{:T(512)S(6)} %or.3), kind=kLoop, calls=%fused_computation.2 | loop fusion | flops 131072 | bytes 786433 | tf_op jit(solution)/shard_map/jit(_where)/select_n | solution.py:281
  65.5 3.3 %collective-permute-start.15 = (bf16[256,1024]{1,0:T(8,128)(2,1)}, bf16[256,1024]{1,0:T(8,128)(2,1)}, u32[]{:S(2)}, u32[]{:S(2)}) collective-permute-start(bf16[256,1024]{1,0:T(8,128)(2,1)} %get-tuple-element.42), channel_id=1, source_target_pairs={{0,6},{1,7},{6,0},{7,1},{8,14},{9,15},{14,8},{15,9},{16,22},{17,23... | collective-permute-start | bytes 1572872 | tf_op jit(solution)/shard_map/ppermute | solution.py:251
  68.8 1.1 %slice_select_fusion.refs_3_ = bf16[160,1024]{1,0:T(8,128)(2,1)S(1)} fusion(bf16[288,1024]{1,0:T(8,128)(2,1)} %collective-permute-done.1, bf16[288,1024]{1,0:T(8,128)(2,1)} %collective-permute-done.5, pred[]{:T(512)S(6)} %or.3), kind=kLoop, calls=%fused_computation.1 | loop fusion | flops 163840 | bytes 983041 | tf_op jit(solution)/shard_map/jit(_where)/select_n | solution.py:282
  69.9 0.8 copy-done.6
  71.7 0.8 collective-permute-done.12.refs_8_
  72.5 1.1 %copy-done.7 = bf16[288,1024]{1,0:T(8,128)(2,1)S(1)} copy-done((bf16[288,1024]{1,0:T(8,128)(2,1)S(1)}, bf16[288,1024]{1,0:T(8,128)(2,1)}, u32[]{:S(2)}) %copy-start.7) | copy-done | bytes 589848
  73.6 5.0 %shard_map.93 = (bf16[1024,1024]{1,0:T(8,128)(2,1)S(1)}, bf16[256,1024]{1,0:T(8,128)(2,1)S(1)}) custom-call(s32[8]{0:T(128)S(1)} %pad_add_fusion.place, bf16[288,1024]{1,0:T(8,128)(2,1)S(1)} %copy-done.5, bf16[288,1024]{1,0:T(8,128)(2,1)} %collective-permute-done.4.refs_1_, bf16[128,1024]{1,0:T(8,128)(2,1)S(1)} %slice_select_fusion.1.refs_2_, ...), custom_call_target="tpu_custom_call" | custom-call | flops 1 | bytes 1 | tf_op jit(solution)/shard_map/pallas_call | solution.py:114
  78.7 6.8 %shard_map.94 = f32[4,8,128]{2,1,0:T(8,128)S(1)} custom-call(s32[5]{0:T(128)S(1)} %concatenate.16.info, bf16[128,1024]{1,0:T(8,128)(2,1)S(1)} %copy-done.12, bf16[800,1024]{1,0:T(8,128)(2,1)S(1)} %copy-done.1, bf16[256,1024]{1,0:T(8,128)(2,1)} %collective-permute-done.2.refs_2_, bf16[256,1024]{1,0:T(8,128)(2,1)S(1)} %copy-done.11, ...), custom_call_target="tpu_custom_call" | custom-call | flops 1 | bytes 1 | tf_op jit(solution)/shard_map/pallas_call | solution.py:221
  85.6 1.3 %collective-permute-done.14.refs_1_ = bf16[256,1024]{1,0:T(8,128)(2,1)} collective-permute-done((bf16[256,1024]{1,0:T(8,128)(2,1)}, bf16[256,1024]{1,0:T(8,128)(2,1)}, u32[]{:S(2)}, u32[]{:S(2)}) %collective-permute-start.14) | collective-permute-done | bytes 524320 | tf_op jit(solution)/shard_map/ppermute | solution.py:251
  86.8 7.4 %shard_map.95 = f32[4,8,128]{2,1,0:T(8,128)S(1)} custom-call(s32[5]{0:T(128)S(1)} %concatenate.18.info, bf16[256,1024]{1,0:T(8,128)(2,1)S(1)} %copy-done.9, bf16[256,1024]{1,0:T(8,128)(2,1)} %collective-permute-done.14.refs_1_, bf16[256,1024]{1,0:T(8,128)(2,1)} %collective-permute-done.6.refs_2_, bf16[256,1024]{1,0:T(8,128)(2,1)} %collective-permute-done.15.refs_3_, ...), custom_call_target="tpu_custom_call" | custom-call | flops 1 | bytes 1 | tf_op jit(solution)/shard_map/pallas_call | solution.py:221
  94.7 10.5 %all_to_all.5 = f32[32,1,8]{2,1,0:T(1,128)S(1)} all-to-all(f32[32,1,8]{2,1,0:T(1,128)S(1)} %broadcast_select_fusion.1), channel_id=1, replica_groups=mesh['section'=4,'dp'=8] {'section','dp'}, dimensions={0} | all-to-all | bytes 2048 | tf_op jit(solution)/shard_map/all_to_all | solution.py:363
  (55 shorter events, 2.7 us)
Async XLA Ops:
  3.8 8.3 %collective-permute-start = (bf16[800,1024]{1,0:T(8,128)(2,1)}, bf16[800,1024]{1,0:T(8,128)(2,1)S(1)}, u32[]{:S(2)}, u32[]{:S(2)}) collective-permute-start(bf16[800,1024]{1,0:T(8,128)(2,1)} %get-tuple-element.25), channel_id=1, source_target_pairs={{0,1},{1,0},{2,3},{3,2},{4,5},{5,4},{6,7},{7,6},{8,9},{9,8},{10,11... | collective-permute-start | bytes 4915208 | tf_op jit(solution)/shard_map/ppermute | solution.py:246
  4.3 19.5 %collective-permute-start.7 = (bf16[288,1024]{1,0:T(8,128)(2,1)}, bf16[288,1024]{1,0:T(8,128)(2,1)}, u32[]{:S(2)}, u32[]{:S(2)}) collective-permute-start(bf16[288,1024]{1,0:T(8,128)(2,1)} %get-tuple-element.30.refs_0_), channel_id=1, source_target_pairs={{0,4},{1,5},{6,2},{7,3},{8,12},{9,13},{14,10},{15,11},{16,20},{17,... | collective-permute-start | bytes 1769480 | tf_op jit(solution)/shard_map/ppermute | solution.py:251
  10.6 20.6 %collective-permute-start.1 = (bf16[288,1024]{1,0:T(8,128)(2,1)}, bf16[288,1024]{1,0:T(8,128)(2,1)}, u32[]{:S(2)}, u32[]{:S(2)}) collective-permute-start(bf16[288,1024]{1,0:T(8,128)(2,1)} %get-tuple-element.30.refs_0_), channel_id=1, source_target_pairs={{2,4},{3,5},{4,2},{5,3},{10,12},{11,13},{12,10},{13,11},{18,20},{1... | collective-permute-start | bytes 1769480 | tf_op jit(solution)/shard_map/ppermute | solution.py:251
  12.1 24.3 %collective-permute-start.4 = (bf16[288,1024]{1,0:T(8,128)(2,1)}, bf16[288,1024]{1,0:T(8,128)(2,1)}, u32[]{:S(2)}, u32[]{:S(2)}) collective-permute-start(bf16[288,1024]{1,0:T(8,128)(2,1)} %get-tuple-element.30.refs_0_), channel_id=1, source_target_pairs={{0,2},{1,3},{2,0},{3,1},{4,6},{5,7},{6,4},{7,5},{8,10},{9,11},{10,... | collective-permute-start | bytes 1769480 | tf_op jit(solution)/shard_map/ppermute | solution.py:251
  12.1 1.2 %copy-start = (bf16[800,1024]{1,0:T(8,128)(2,1)}, bf16[800,1024]{1,0:T(8,128)(2,1)S(1)}, u32[]{:S(2)}) copy-start(bf16[800,1024]{1,0:T(8,128)(2,1)S(1)} %collective-permute-done.beside.refs_5_.refs_1_) | copy-start | bytes 4915204
  15.9 55.5 %copy-start.13 = (s32[8]{0:T(128)S(1)}, s32[8]{0:T(128)}, u32[]{:S(2)}) copy-start(s32[8]{0:T(128)} %param.16) | copy-start | bytes 100
  15.9 56.6 %copy-start.1 = (bf16[800,1024]{1,0:T(8,128)(2,1)S(1)}, bf16[800,1024]{1,0:T(8,128)(2,1)}, u32[]{:S(2)}) copy-start(bf16[800,1024]{1,0:T(8,128)(2,1)} %copy-done) | copy-start | bytes 4915204
  15.9 56.6 %copy-start.5 = (bf16[288,1024]{1,0:T(8,128)(2,1)S(1)}, bf16[288,1024]{1,0:T(8,128)(2,1)}, u32[]{:S(2)}) copy-start(bf16[288,1024]{1,0:T(8,128)(2,1)} %get-tuple-element.30.refs_0_) | copy-start | bytes 1769476
  15.9 29.0 %collective-permute-start.3 = (bf16[256,1024]{1,0:T(8,128)(2,1)}, bf16[256,1024]{1,0:T(8,128)(2,1)S(1)}, u32[]{:S(2)}, u32[]{:S(2)}) collective-permute-start(bf16[256,1024]{1,0:T(8,128)(2,1)} %get-tuple-element.34), channel_id=1, source_target_pairs={{2,0},{3,1},{4,6},{5,7},{10,8},{11,9},{12,14},{13,15},{18,16},{19,... | collective-permute-start | bytes 1572872 | tf_op jit(solution)/shard_map/ppermute | solution.py:251
  23.8 28.7 %collective-permute-start.8 = (bf16[288,1024]{1,0:T(8,128)(2,1)}, bf16[288,1024]{1,0:T(8,128)(2,1)}, u32[]{:S(2)}, u32[]{:S(2)}) collective-permute-start(bf16[288,1024]{1,0:T(8,128)(2,1)} %collective-permute-done.7), channel_id=1, source_target_pairs={{2,0},{3,1},{4,6},{5,7},{10,8},{11,9},{12,14},{13,15},{18,16},{19,... | collective-permute-start | bytes 1769480 | tf_op jit(solution)/shard_map/ppermute | solution.py:251
  25.1 27.4 %collective-permute-start.9 = (bf16[256,1024]{1,0:T(8,128)(2,1)}, bf16[256,1024]{1,0:T(8,128)(2,1)S(1)}, u32[]{:S(2)}, u32[]{:S(2)}) collective-permute-start(bf16[256,1024]{1,0:T(8,128)(2,1)} %get-tuple-element.41), channel_id=1, source_target_pairs={{0,4},{1,5},{6,2},{7,3},{8,12},{9,13},{14,10},{15,11},{16,20},{17,... | collective-permute-start | bytes 1572872 | tf_op jit(solution)/shard_map/ppermute | solution.py:251
  31.2 22.1 %collective-permute-start.2 = (bf16[256,1024]{1,0:T(8,128)(2,1)}, bf16[256,1024]{1,0:T(8,128)(2,1)}, u32[]{:S(2)}, u32[]{:S(2)}) collective-permute-start(bf16[256,1024]{1,0:T(8,128)(2,1)} %get-tuple-element.42), channel_id=1, source_target_pairs={{2,4},{3,5},{4,2},{5,3},{10,12},{11,13},{12,10},{13,11},{18,20},{1... | collective-permute-start | bytes 1572872 | tf_op jit(solution)/shard_map/ppermute | solution.py:251
  36.4 22.1 %collective-permute-start.6 = (bf16[256,1024]{1,0:T(8,128)(2,1)}, bf16[256,1024]{1,0:T(8,128)(2,1)}, u32[]{:S(2)}, u32[]{:S(2)}) collective-permute-start(bf16[256,1024]{1,0:T(8,128)(2,1)} %get-tuple-element.34), channel_id=1, source_target_pairs={{0,2},{1,3},{6,4},{7,5},{8,10},{9,11},{14,12},{15,13},{16,18},{17,... | collective-permute-start | bytes 1572872 | tf_op jit(solution)/shard_map/ppermute | solution.py:251
  44.9 0.8 copy-start.10
  45.8 18.6 %collective-permute-start.5 = (bf16[288,1024]{1,0:T(8,128)(2,1)}, bf16[288,1024]{1,0:T(8,128)(2,1)}, u32[]{:S(2)}, u32[]{:S(2)}) collective-permute-start(bf16[288,1024]{1,0:T(8,128)(2,1)} %collective-permute-done.1), channel_id=1, source_target_pairs={{2,0},{3,1},{4,6},{5,7},{10,8},{11,9},{12,14},{13,15},{18,16},{19,... | collective-permute-start | bytes 1769480 | tf_op jit(solution)/shard_map/ppermute | solution.py:251
  52.4 17.4 %collective-permute-start.10 = (bf16[288,1024]{1,0:T(8,128)(2,1)}, bf16[288,1024]{1,0:T(8,128)(2,1)S(1)}, u32[]{:S(2)}, u32[]{:S(2)}) collective-permute-start(bf16[288,1024]{1,0:T(8,128)(2,1)} %collective-permute-done.4.refs_1_), channel_id=1, source_target_pairs={{0,1},{1,0},{2,3},{3,2},{4,5},{5,4},{6,7},{7,6},{8,9},{9,8},{10,11... | collective-permute-start | bytes 1769480 | tf_op jit(solution)/shard_map/ppermute | solution.py:246
  52.5 0.9 copy-start.8
  53.3 33.5 %collective-permute-start.14 = (bf16[256,1024]{1,0:T(8,128)(2,1)}, bf16[256,1024]{1,0:T(8,128)(2,1)}, u32[]{:S(2)}, u32[]{:S(2)}) collective-permute-start(bf16[256,1024]{1,0:T(8,128)(2,1)} %get-tuple-element.41), channel_id=1, source_target_pairs={{2,6},{3,7},{4,0},{5,1},{10,14},{11,15},{12,8},{13,9},{18,22},{19,... | collective-permute-start | bytes 1572872 | tf_op jit(solution)/shard_map/ppermute | solution.py:251
  55.7 15.9 %collective-permute-start.13 = (bf16[288,1024]{1,0:T(8,128)(2,1)S(1)}, bf16[288,1024]{1,0:T(8,128)(2,1)}, u32[]{:S(2)}, u32[]{:S(2)}) collective-permute-start(bf16[288,1024]{1,0:T(8,128)(2,1)S(1)} %broadcast_select_fusion.refs_4_), channel_id=1, source_target_pairs={{0,1},{1,0},{2,3},{3,2},{4,5},{5,4},{6,7},{7,6},{8,9},{9,8},{10,11... | collective-permute-start | bytes 1769480 | tf_op jit(solution)/shard_map/ppermute | solution.py:246
  65.4 6.2 %collective-permute-start.11 = (bf16[128,1024]{1,0:T(8,128)(2,1)S(1)}, bf16[128,1024]{1,0:T(8,128)(2,1)}, u32[]{:S(2)}, u32[]{:S(2)}) collective-permute-start(bf16[128,1024]{1,0:T(8,128)(2,1)S(1)} %slice_select_fusion.1.refs_2_), channel_id=1, source_target_pairs={{0,1},{1,0},{2,3},{3,2},{4,5},{5,4},{6,7},{7,6},{8,9},{9,8},{10,11... | collective-permute-start | bytes 786440 | tf_op jit(solution)/shard_map/ppermute | solution.py:246
  65.5 21.3 %collective-permute-start.15 = (bf16[256,1024]{1,0:T(8,128)(2,1)}, bf16[256,1024]{1,0:T(8,128)(2,1)}, u32[]{:S(2)}, u32[]{:S(2)}) collective-permute-start(bf16[256,1024]{1,0:T(8,128)(2,1)} %get-tuple-element.42), channel_id=1, source_target_pairs={{0,6},{1,7},{6,0},{7,1},{8,14},{9,15},{14,8},{15,9},{16,22},{17,23... | collective-permute-start | bytes 1572872 | tf_op jit(solution)/shard_map/ppermute | solution.py:251
  69.9 0.8 copy-start.6
  70.7 1.8 %collective-permute-start.12 = (bf16[160,1024]{1,0:T(8,128)(2,1)S(1)}, bf16[160,1024]{1,0:T(8,128)(2,1)}, u32[]{:S(2)}, u32[]{:S(2)}) collective-permute-start(bf16[160,1024]{1,0:T(8,128)(2,1)S(1)} %slice_select_fusion.refs_3_), channel_id=1, source_target_pairs={{0,1},{1,0},{2,3},{3,2},{4,5},{5,4},{6,7},{7,6},{8,9},{9,8},{10,11... | collective-permute-start | bytes 983048 | tf_op jit(solution)/shard_map/ppermute | solution.py:246
  71.6 7.1 %copy-start.2 = (bf16[1,1024,1024]{2,1,0:T(8,128)(2,1)S(1)}, bf16[1,1024,1024]{2,1,0:T(8,128)(2,1)}, u32[]{:S(2)}) copy-start(bf16[1,1024,1024]{2,1,0:T(8,128)(2,1)} %param.13) | copy-start | bytes 6291460
  71.6 7.1 %copy-start.3 = (bf16[1,1024,256]{2,1,0:T(8,128)(2,1)S(1)}, bf16[1,1024,256]{2,1,0:T(8,128)(2,1)}, u32[]{:S(2)}) copy-start(bf16[1,1024,256]{2,1,0:T(8,128)(2,1)} %param.11) | copy-start | bytes 1572868
  71.6 7.1 %copy-start.4 = (bf16[1,8,32,1024]{3,2,1,0:T(8,128)(2,1)S(1)}, bf16[1,8,32,1024]{3,2,1,0:T(8,128)(2,1)}, u32[]{:S(2)}) copy-start(bf16[1,8,32,1024]{3,2,1,0:T(8,128)(2,1)} %param.15) | copy-start | bytes 1572868
  72.5 1.1 %copy-start.7 = (bf16[288,1024]{1,0:T(8,128)(2,1)S(1)}, bf16[288,1024]{1,0:T(8,128)(2,1)}, u32[]{:S(2)}) copy-start(bf16[288,1024]{1,0:T(8,128)(2,1)} %copy-done.6) | copy-start | bytes 1769476
  73.6 5.1 %copy-start.11 = (bf16[256,1024]{1,0:T(8,128)(2,1)S(1)}, bf16[256,1024]{1,0:T(8,128)(2,1)}, u32[]{:S(2)}) copy-start(bf16[256,1024]{1,0:T(8,128)(2,1)} %copy-done.10) | copy-start | bytes 1572868
  73.6 5.1 %copy-start.12 = (bf16[128,1024]{1,0:T(8,128)(2,1)S(1)}, bf16[128,1024]{1,0:T(8,128)(2,1)}, u32[]{:S(2)}) copy-start(bf16[128,1024]{1,0:T(8,128)(2,1)} %get-tuple-element.24.refs_0_) | copy-start | bytes 786436
  78.7 8.1 %copy-start.9 = (bf16[256,1024]{1,0:T(8,128)(2,1)S(1)}, bf16[256,1024]{1,0:T(8,128)(2,1)}, u32[]{:S(2)}) copy-start(bf16[256,1024]{1,0:T(8,128)(2,1)} %copy-done.8) | copy-start | bytes 1572868
  85.5 8.9 %copy-start.14 = (s32[8]{0:T(128)S(1)}, s32[8]{0:T(128)}, u32[]{:S(2)}) copy-start(s32[8]{0:T(128)} %param.17) | copy-start | bytes 100

commit v5 on v4

--- a/solution.py
+++ b/solution.py
@@ -26,7 +26,7 @@
 
 
 def cut_kernel(rows, columns, place, acts, *refs):
-    parts, (mine, beside, own, near, skip, across, sem) = refs[:3], refs[3:]
+    parts, (mine, beside, sem) = refs[:3], refs[3:]
     chip, core = place[0] // 2, place[0] % 2
 
     def part(m, c):
@@ -39,43 +39,48 @@
         pairs.append((x, mine.at[pl.ds(at, length)]))
         pairs.append((x, beside.at[pl.ds(4 * rows + at, length)]))
         at += length
-    for m, out in enumerate((own, near, skip, across)):
+    for m in range(4):
         pairs.append((part(m, 1 - core), beside.at[pl.ds(m * rows, rows)]))
-        pairs.append((part(m, core), out))
     run_copies(pairs, sem)
 
 
 def cut(me, acts, parts, columns):
     rows = acts.shape[0]
     total = sum(part.shape[0] for part in parts)
-    lengths = (total, 4 * rows + total, rows, rows, rows, rows)
+    lengths = (total, 4 * rows + total)
     return pl.pallas_call(
         functools.partial(cut_kernel, rows, columns),
         out_shape=[jax.ShapeDtypeStruct((length, columns), BF16) for length in lengths],
         in_specs=[pl.BlockSpec(memory_space=pltpu.SMEM)]
         + [pl.BlockSpec(memory_space=pltpu.HBM)] * (1 + len(parts)),
         out_specs=[pl.BlockSpec(memory_space=pltpu.VMEM)] * len(lengths),
-        scratch_shapes=[pltpu.SemaphoreType.DMA((14,))],
+        scratch_shapes=[pltpu.SemaphoreType.DMA((10,))],
     )(me.reshape(1).astype(jnp.int32), acts, *parts)
 
 
-def join_kernel(rows, beside, *refs):
-    parts, outs, sem = refs[:3], refs[3:6], refs[6]
-    pairs = [(part, out.at[pl.ds(0, rows)]) for part, out in zip(parts, outs)]
-    for m, out in enumerate(outs):
-        pairs.append((beside.at[pl.ds((m + 1) * rows, rows)], out.at[pl.ds(rows, rows)]))
+def join_kernel(rows, columns, place, acts, beside, own, *refs):
+    outs, sem = refs[:3], refs[3]
+    chip, core = place[0] // 2, place[0] % 2
+    pairs = []
+    for m, out in enumerate((own, *outs)):
+        first = pl.multiple_of((2 * (chip ^ m) + core) * columns, columns)
+        pairs.append((acts.at[:, pl.ds(first, columns)], out.at[pl.ds(0, rows)]))
+        if m:
+            pairs.append((beside.at[pl.ds(m * rows, rows)], out.at[pl.ds(rows, rows)]))
     run_copies(pairs, sem)
 
 
-def join_parts(rows, beside, parts):
-    columns = beside.shape[1]
+def join_parts(me, acts, beside, columns):
+    rows = acts.shape[0]
+    lengths = (rows, 2 * rows, 2 * rows, 2 * rows)
     return pl.pallas_call(
-        functools.partial(join_kernel, rows),
-        out_shape=[jax.ShapeDtypeStruct((2 * rows, columns), BF16)] * 3,
-        in_specs=[pl.BlockSpec(memory_space=pltpu.HBM)] * 4,
-        out_specs=[pl.BlockSpec(memory_space=pltpu.VMEM)] * 3,
-        scratch_shapes=[pltpu.SemaphoreType.DMA((6,))],
-    )(beside, *parts)
+        functools.partial(join_kernel, rows, columns),
+        out_shape=[jax.ShapeDtypeStruct((length, columns), BF16) for length in lengths],
+        in_specs=[pl.BlockSpec(memory_space=pltpu.SMEM)]
+        + [pl.BlockSpec(memory_space=pltpu.HBM)] * 2,
+        out_specs=[pl.BlockSpec(memory_space=pltpu.VMEM)] * 4,
+        scratch_shapes=[pltpu.SemaphoreType.DMA((7,))],
+    )(me.reshape(1).astype(jnp.int32), acts, beside)
 
 
 def rotate_kernel(count, sizes, sources, parts, place, *refs):
@@ -260,12 +265,12 @@
     inner = (chip == 1) | (chip == 2)
     rows = acts.shape[0]
     outward = [(1, 0), (2, 3)]
-    mine, to_beside, own, near, skip, across = cut(me, acts, parts, columns)
+    mine, to_beside = cut(me, acts, parts, columns)
     second_in = hop(mine, [(1, 2), (2, 1)])
     third_in = hop(mine, [(0, 2), (3, 1)])
     first = hop(mine, [(0, 1), (1, 0), (2, 3), (3, 2)])
     beside = swap(to_beside, 1, 8)
-    near, skip, across = join_parts(rows, beside, (near, skip, across))
+    own, near, skip, across = join_parts(me, acts, beside, columns)
     near_out = hop(near, outward)
     second_end = hop(after(second_in, first, near_out), outward)
     third_end = hop(third_in, outward)

time: 106 us -> 106 us (level)
  no operation moved by 1% of the time
where the time goes in v5:
time: 106 us; the launch traced here: 105 us
  starting transfers between devices  33.8 us (32%)
  waiting for transfers between devices  25.4 us (24%)
  Pallas kernels  25 us (24%)
  blocking collectives  10.6 us (10%)
  local copies, waits for them, and re-layouts  5.34 us (5%)
  other arithmetic  4.41 us (4%)
    ppermute x11, starting transfers between devices, hop(): return lax.ppermute(x, 'dp', pairs)  32.5 us
    ppermute x11, waiting for transfers between devices, hop(): return lax.ppermute(x, 'dp', pairs)  24.6 us
    pallas_call x2, Pallas kernels, score(): pl.pallas_call(functools.partial(score_kernel, blocks, len(arrays), queri...  14.2 us
    all_to_all x1, blocking collectives, on_device(): lax.all_to_all(outgoing, ('section', 'dp'), split_axis=0, concat_axis=0,...  10.6 us
    pallas_call x1, Pallas kernels, rotate_grads(): pl.pallas_call(functools.partial(rotate_kernel, count, sizes, sources, le...  5.04 us
    unnamed x30, local copies, waits for them, and re-layouts  4.92 us
    pallas_call x1, Pallas kernels, cut(): pl.pallas_call(functools.partial(cut_kernel, rows, columns), out_shape=[j...  3.05 us
    pallas_call x1, Pallas kernels, join_parts(): pl.pallas_call(functools.partial(join_kernel, rows, columns), out_shape=[...  2.77 us
  transfers between devices with their start and end apart: 16, of which 7 were waited for; matrix products, arithmetic and copies ran while one was open for 4% of the time, Pallas kernels for 14%

profile of v5, /device:TPU:0, one launch (start us, length us, event | category | flops | bytes accessed | tf_op | source)
XLA Modules:
  0.0 105.2 jit_solution(13367829481851867089)
XLA Ops:
  0.0 3.1 %shard_map.91 = (bf16[288,1024]{1,0:T(8,128)(2,1)}, bf16[800,1024]{1,0:T(8,128)(2,1)}) custom-call(s32[1]{0:T(128)} %bitcast.place, bf16[128,8192]{1,0:T(8,128)(2,1)} %bitcast.30, bf16[128,1024]{1,0:T(8,128)(2,1)} %bitcast.32, bf16[128,1024]{1,0:T(8,128)(2,1)} %bitcast.33, bf16[32,1024]{1,0:T(8,128)(2,1)} %bitcast.34), custom_call_target="tpu_custom_call" | custom-call | tf_op jit(solution)/shard_map/pallas_call | solution.py:51
  3.6 6.4 %collective-permute-start.7 = (bf16[288,1024]{1,0:T(8,128)(2,1)}, bf16[288,1024]{1,0:T(8,128)(2,1)}, u32[]{:S(2)}, u32[]{:S(2)}) collective-permute-start(bf16[288,1024]{1,0:T(8,128)(2,1)} %get-tuple-element.24.refs_0_), channel_id=1, source_target_pairs={{0,4},{1,5},{6,2},{7,3},{8,12},{9,13},{14,10},{15,11},{16,20},{17,... | collective-permute-start | bytes 1769480 | tf_op jit(solution)/shard_map/ppermute | solution.py:256
  9.9 1.5 %collective-permute-start.1 = (bf16[288,1024]{1,0:T(8,128)(2,1)}, bf16[288,1024]{1,0:T(8,128)(2,1)}, u32[]{:S(2)}, u32[]{:S(2)}) collective-permute-start(bf16[288,1024]{1,0:T(8,128)(2,1)} %get-tuple-element.24.refs_0_), channel_id=1, source_target_pairs={{2,4},{3,5},{4,2},{5,3},{10,12},{11,13},{12,10},{13,11},{18,20},{1... | collective-permute-start | bytes 1769480 | tf_op jit(solution)/shard_map/ppermute | solution.py:256
  11.4 1.2 %copy-done = bf16[800,1024]{1,0:T(8,128)(2,1)} copy-done((bf16[800,1024]{1,0:T(8,128)(2,1)}, bf16[800,1024]{1,0:T(8,128)(2,1)S(1)}, u32[]{:S(2)}) %copy-start) | copy-done | bytes 1638424
  12.6 2.8 %shard_map.92 = (bf16[128,1024]{1,0:T(8,128)(2,1)}, bf16[256,1024]{1,0:T(8,128)(2,1)}, bf16[256,1024]{1,0:T(8,128)(2,1)}, bf16[256,1024]{1,0:T(8,128)(2,1)}) custom-call(s32[1]{0:T(128)} %bitcast.place, bf16[128,8192]{1,0:T(8,128)(2,1)} %bitcast.31, bf16[800,1024]{1,0:T(8,128)(2,1)} %copy-done), custom_call_target="tpu_custom_call" | custom-call | tf_op jit(solution)/shard_map/pallas_call | solution.py:76
  15.4 1.4 %collective-permute-start.3 = (bf16[256,1024]{1,0:T(8,128)(2,1)}, bf16[256,1024]{1,0:T(8,128)(2,1)S(1)}, u32[]{:S(2)}, u32[]{:S(2)}) collective-permute-start(bf16[256,1024]{1,0:T(8,128)(2,1)} %get-tuple-element.28), channel_id=1, source_target_pairs={{2,0},{3,1},{4,6},{5,7},{10,8},{11,9},{12,14},{13,15},{18,16},{19,... | collective-permute-start | bytes 1572872 | tf_op jit(solution)/shard_map/ppermute | solution.py:256
  16.9 6.2 %collective-permute-done.7 = bf16[288,1024]{1,0:T(8,128)(2,1)} collective-permute-done((bf16[288,1024]{1,0:T(8,128)(2,1)}, bf16[288,1024]{1,0:T(8,128)(2,1)}, u32[]{:S(2)}, u32[]{:S(2)}) %collective-permute-start.7) | collective-permute-done | bytes 589856 | tf_op jit(solution)/shard_map/ppermute | solution.py:256
  23.1 1.3 %collective-permute-start.8 = (bf16[288,1024]{1,0:T(8,128)(2,1)}, bf16[288,1024]{1,0:T(8,128)(2,1)}, u32[]{:S(2)}, u32[]{:S(2)}) collective-permute-start(bf16[288,1024]{1,0:T(8,128)(2,1)} %collective-permute-done.7), channel_id=1, source_target_pairs={{2,0},{3,1},{4,6},{5,7},{10,8},{11,9},{12,14},{13,15},{18,16},{19,... | collective-permute-start | bytes 1769480 | tf_op jit(solution)/shard_map/ppermute | solution.py:256
  24.4 6.1 %collective-permute-start.9 = (bf16[256,1024]{1,0:T(8,128)(2,1)}, bf16[256,1024]{1,0:T(8,128)(2,1)S(1)}, u32[]{:S(2)}, u32[]{:S(2)}) collective-permute-start(bf16[256,1024]{1,0:T(8,128)(2,1)} %get-tuple-element.35), channel_id=1, source_target_pairs={{0,4},{1,5},{6,2},{7,3},{8,12},{9,13},{14,10},{15,11},{16,20},{17,... | collective-permute-start | bytes 1572872 | tf_op jit(solution)/shard_map/ppermute | solution.py:256
  30.5 1.5 %collective-permute-start.2 = (bf16[256,1024]{1,0:T(8,128)(2,1)}, bf16[256,1024]{1,0:T(8,128)(2,1)}, u32[]{:S(2)}, u32[]{:S(2)}) collective-permute-start(bf16[256,1024]{1,0:T(8,128)(2,1)} %get-tuple-element.36), channel_id=1, source_target_pairs={{2,4},{3,5},{4,2},{5,3},{10,12},{11,13},{12,10},{13,11},{18,20},{1... | collective-permute-start | bytes 1572872 | tf_op jit(solution)/shard_map/ppermute | solution.py:256
  32.0 3.7 %collective-permute-done.4.refs_1_ = bf16[288,1024]{1,0:T(8,128)(2,1)} collective-permute-done((bf16[288,1024]{1,0:T(8,128)(2,1)}, bf16[288,1024]{1,0:T(8,128)(2,1)}, u32[]{:S(2)}, u32[]{:S(2)}) %collective-permute-start.4) | collective-permute-done | bytes 589856 | tf_op jit(solution)/shard_map/ppermute | solution.py:256
  35.7 8.5 %collective-permute-start.6 = (bf16[256,1024]{1,0:T(8,128)(2,1)}, bf16[256,1024]{1,0:T(8,128)(2,1)}, u32[]{:S(2)}, u32[]{:S(2)}) collective-permute-start(bf16[256,1024]{1,0:T(8,128)(2,1)} %get-tuple-element.28), channel_id=1, source_target_pairs={{0,2},{1,3},{6,4},{7,5},{8,10},{9,11},{14,12},{15,13},{16,18},{17,... | collective-permute-start | bytes 1572872 | tf_op jit(solution)/shard_map/ppermute | solution.py:256
  44.2 0.8 copy-done.10
  45.1 1.3 %collective-permute-start.5 = (bf16[288,1024]{1,0:T(8,128)(2,1)}, bf16[288,1024]{1,0:T(8,128)(2,1)}, u32[]{:S(2)}, u32[]{:S(2)}) collective-permute-start(bf16[288,1024]{1,0:T(8,128)(2,1)} %collective-permute-done.1), channel_id=1, source_target_pairs={{2,0},{3,1},{4,6},{5,7},{10,8},{11,9},{12,14},{13,15},{18,16},{19,... | collective-permute-start | bytes 1769480 | tf_op jit(solution)/shard_map/ppermute | solution.py:256
  46.4 5.3 %collective-permute-done.8 = bf16[288,1024]{1,0:T(8,128)(2,1)} collective-permute-done((bf16[288,1024]{1,0:T(8,128)(2,1)}, bf16[288,1024]{1,0:T(8,128)(2,1)}, u32[]{:S(2)}, u32[]{:S(2)}) %collective-permute-start.8) | collective-permute-done | bytes 589856 | tf_op jit(solution)/shard_map/ppermute | solution.py:256
  51.8 0.9 copy-done.8
  52.6 1.3 %collective-permute-start.14 = (bf16[256,1024]{1,0:T(8,128)(2,1)}, bf16[256,1024]{1,0:T(8,128)(2,1)}, u32[]{:S(2)}, u32[]{:S(2)}) collective-permute-start(bf16[256,1024]{1,0:T(8,128)(2,1)} %get-tuple-element.35), channel_id=1, source_target_pairs={{2,6},{3,7},{4,0},{5,1},{10,14},{11,15},{12,8},{13,9},{18,22},{19,... | collective-permute-start | bytes 1572872 | tf_op jit(solution)/shard_map/ppermute | solution.py:256
  53.9 1.1 %broadcast_select_fusion.refs_4_ = bf16[288,1024]{1,0:T(8,128)(2,1)S(1)} fusion(bf16[288,1024]{1,0:T(8,128)(2,1)} %collective-permute-done.7, bf16[288,1024]{1,0:T(8,128)(2,1)} %collective-permute-done.8, pred[]{:T(512)S(6)} %or.3), kind=kLoop, calls=%fused_computation | loop fusion | flops 294912 | bytes 1769473 | tf_op jit(solution)/shard_map/jit(_where)/select_n | solution.py:282
  55.1 0.6 collective-permute-start.13
  55.6 2.2 %collective-permute-done.6.refs_2_ = bf16[256,1024]{1,0:T(8,128)(2,1)} collective-permute-done((bf16[256,1024]{1,0:T(8,128)(2,1)}, bf16[256,1024]{1,0:T(8,128)(2,1)}, u32[]{:S(2)}, u32[]{:S(2)}) %collective-permute-start.6) | collective-permute-done | bytes 524320 | tf_op jit(solution)/shard_map/ppermute | solution.py:256
  57.8 5.8 %collective-permute-done.5 = bf16[288,1024]{1,0:T(8,128)(2,1)} collective-permute-done((bf16[288,1024]{1,0:T(8,128)(2,1)}, bf16[288,1024]{1,0:T(8,128)(2,1)}, u32[]{:S(2)}, u32[]{:S(2)}) %collective-permute-start.5) | collective-permute-done | bytes 589856 | tf_op jit(solution)/shard_map/ppermute | solution.py:256
  63.7 1.1 %slice_select_fusion.1.refs_2_ = bf16[128,1024]{1,0:T(8,128)(2,1)S(1)} fusion(bf16[288,1024]{1,0:T(8,128)(2,1)} %collective-permute-done.1, bf16[288,1024]{1,0:T(8,128)(2,1)} %collective-permute-done.5, pred[]{:T(512)S(6)} %or.3), kind=kLoop, calls=%fused_computation.2 | loop fusion | flops 131072 | bytes 786433 | tf_op jit(solution)/shard_map/jit(_where)/select_n | solution.py:286
  64.8 3.3 %collective-permute-start.15 = (bf16[256,1024]{1,0:T(8,128)(2,1)}, bf16[256,1024]{1,0:T(8,128)(2,1)}, u32[]{:S(2)}, u32[]{:S(2)}) collective-permute-start(bf16[256,1024]{1,0:T(8,128)(2,1)} %get-tuple-element.36), channel_id=1, source_target_pairs={{0,6},{1,7},{6,0},{7,1},{8,14},{9,15},{14,8},{15,9},{16,22},{17,23... | collective-permute-start | bytes 1572872 | tf_op jit(solution)/shard_map/ppermute | solution.py:256
  68.1 1.1 %slice_select_fusion.refs_3_ = bf16[160,1024]{1,0:T(8,128)(2,1)S(1)} fusion(bf16[288,1024]{1,0:T(8,128)(2,1)} %collective-permute-done.1, bf16[288,1024]{1,0:T(8,128)(2,1)} %collective-permute-done.5, pred[]{:T(512)S(6)} %or.3), kind=kLoop, calls=%fused_computation.1 | loop fusion | flops 163840 | bytes 983041 | tf_op jit(solution)/shard_map/jit(_where)/select_n | solution.py:287
  69.2 0.8 copy-done.6
  71.0 0.8 collective-permute-done.12.refs_8_
  71.8 1.1 %copy-done.7 = bf16[288,1024]{1,0:T(8,128)(2,1)S(1)} copy-done((bf16[288,1024]{1,0:T(8,128)(2,1)S(1)}, bf16[288,1024]{1,0:T(8,128)(2,1)}, u32[]{:S(2)}) %copy-start.7) | copy-done | bytes 589848
  72.9 5.0 %shard_map.93 = (bf16[1024,1024]{1,0:T(8,128)(2,1)S(1)}, bf16[256,1024]{1,0:T(8,128)(2,1)S(1)}) custom-call(s32[8]{0:T(128)S(1)} %pad_add_fusion.place, bf16[288,1024]{1,0:T(8,128)(2,1)S(1)} %copy-done.5, bf16[288,1024]{1,0:T(8,128)(2,1)} %collective-permute-done.4.refs_1_, bf16[128,1024]{1,0:T(8,128)(2,1)S(1)} %slice_select_fusion.1.refs_2_, ...), custom_call_target="tpu_custom_call" | custom-call | flops 1 | bytes 1 | tf_op jit(solution)/shard_map/pallas_call | solution.py:119
  78.0 6.8 %shard_map.94 = f32[4,8,128]{2,1,0:T(8,128)S(1)} custom-call(s32[5]{0:T(128)S(1)} %concatenate.16.info, bf16[128,1024]{1,0:T(8,128)(2,1)S(1)} %copy-done.12, bf16[800,1024]{1,0:T(8,128)(2,1)S(1)} %copy-done.1, bf16[256,1024]{1,0:T(8,128)(2,1)} %collective-permute-done.2.refs_2_, bf16[256,1024]{1,0:T(8,128)(2,1)S(1)} %copy-done.11, ...), custom_call_target="tpu_custom_call" | custom-call | flops 1 | bytes 1 | tf_op jit(solution)/shard_map/pallas_call | solution.py:226
  84.9 1.3 %collective-permute-done.14.refs_1_ = bf16[256,1024]{1,0:T(8,128)(2,1)} collective-permute-done((bf16[256,1024]{1,0:T(8,128)(2,1)}, bf16[256,1024]{1,0:T(8,128)(2,1)}, u32[]{:S(2)}, u32[]{:S(2)}) %collective-permute-start.14) | collective-permute-done | bytes 524320 | tf_op jit(solution)/shard_map/ppermute | solution.py:256
  86.1 7.4 %shard_map.95 = f32[4,8,128]{2,1,0:T(8,128)S(1)} custom-call(s32[5]{0:T(128)S(1)} %concatenate.18.info, bf16[256,1024]{1,0:T(8,128)(2,1)S(1)} %copy-done.9, bf16[256,1024]{1,0:T(8,128)(2,1)} %collective-permute-done.14.refs_1_, bf16[256,1024]{1,0:T(8,128)(2,1)} %collective-permute-done.6.refs_2_, bf16[256,1024]{1,0:T(8,128)(2,1)} %collective-permute-done.15.refs_3_, ...), custom_call_target="tpu_custom_call" | custom-call | flops 1 | bytes 1 | tf_op jit(solution)/shard_map/pallas_call | solution.py:226
  94.0 10.6 %all_to_all.5 = f32[32,1,8]{2,1,0:T(1,128)S(1)} all-to-all(f32[32,1,8]{2,1,0:T(1,128)S(1)} %broadcast_select_fusion.1), channel_id=1, replica_groups=mesh['section'=4,'dp'=8] {'section','dp'}, dimensions={0} | all-to-all | bytes 2048 | tf_op jit(solution)/shard_map/all_to_all | solution.py:368
  (55 shorter events, 2.7 us)
Async XLA Ops:
  3.1 8.3 %collective-permute-start = (bf16[800,1024]{1,0:T(8,128)(2,1)}, bf16[800,1024]{1,0:T(8,128)(2,1)S(1)}, u32[]{:S(2)}, u32[]{:S(2)}) collective-permute-start(bf16[800,1024]{1,0:T(8,128)(2,1)} %get-tuple-element.21), channel_id=1, source_target_pairs={{0,1},{1,0},{2,3},{3,2},{4,5},{5,4},{6,7},{7,6},{8,9},{9,8},{10,11... | collective-permute-start | bytes 4915208 | tf_op jit(solution)/shard_map/ppermute | solution.py:251
  3.6 19.5 %collective-permute-start.7 = (bf16[288,1024]{1,0:T(8,128)(2,1)}, bf16[288,1024]{1,0:T(8,128)(2,1)}, u32[]{:S(2)}, u32[]{:S(2)}) collective-permute-start(bf16[288,1024]{1,0:T(8,128)(2,1)} %get-tuple-element.24.refs_0_), channel_id=1, source_target_pairs={{0,4},{1,5},{6,2},{7,3},{8,12},{9,13},{14,10},{15,11},{16,20},{17,... | collective-permute-start | bytes 1769480 | tf_op jit(solution)/shard_map/ppermute | solution.py:256
  9.9 20.6 %collective-permute-start.1 = (bf16[288,1024]{1,0:T(8,128)(2,1)}, bf16[288,1024]{1,0:T(8,128)(2,1)}, u32[]{:S(2)}, u32[]{:S(2)}) collective-permute-start(bf16[288,1024]{1,0:T(8,128)(2,1)} %get-tuple-element.24.refs_0_), channel_id=1, source_target_pairs={{2,4},{3,5},{4,2},{5,3},{10,12},{11,13},{12,10},{13,11},{18,20},{1... | collective-permute-start | bytes 1769480 | tf_op jit(solution)/shard_map/ppermute | solution.py:256
  11.4 24.3 %collective-permute-start.4 = (bf16[288,1024]{1,0:T(8,128)(2,1)}, bf16[288,1024]{1,0:T(8,128)(2,1)}, u32[]{:S(2)}, u32[]{:S(2)}) collective-permute-start(bf16[288,1024]{1,0:T(8,128)(2,1)} %get-tuple-element.24.refs_0_), channel_id=1, source_target_pairs={{0,2},{1,3},{2,0},{3,1},{4,6},{5,7},{6,4},{7,5},{8,10},{9,11},{10,... | collective-permute-start | bytes 1769480 | tf_op jit(solution)/shard_map/ppermute | solution.py:256
  11.4 1.2 %copy-start = (bf16[800,1024]{1,0:T(8,128)(2,1)}, bf16[800,1024]{1,0:T(8,128)(2,1)S(1)}, u32[]{:S(2)}) copy-start(bf16[800,1024]{1,0:T(8,128)(2,1)S(1)} %collective-permute-done.beside.refs_5_.refs_1_) | copy-start | bytes 4915204
  15.4 55.3 %copy-start.13 = (s32[8]{0:T(128)S(1)}, s32[8]{0:T(128)}, u32[]{:S(2)}) copy-start(s32[8]{0:T(128)} %param.16) | copy-start | bytes 100
  15.4 56.4 %copy-start.1 = (bf16[800,1024]{1,0:T(8,128)(2,1)S(1)}, bf16[800,1024]{1,0:T(8,128)(2,1)}, u32[]{:S(2)}) copy-start(bf16[800,1024]{1,0:T(8,128)(2,1)} %copy-done) | copy-start | bytes 4915204
  15.4 56.4 %copy-start.5 = (bf16[288,1024]{1,0:T(8,128)(2,1)S(1)}, bf16[288,1024]{1,0:T(8,128)(2,1)}, u32[]{:S(2)}) copy-start(bf16[288,1024]{1,0:T(8,128)(2,1)} %get-tuple-element.24.refs_0_) | copy-start | bytes 1769476
  15.4 28.8 %collective-permute-start.3 = (bf16[256,1024]{1,0:T(8,128)(2,1)}, bf16[256,1024]{1,0:T(8,128)(2,1)S(1)}, u32[]{:S(2)}, u32[]{:S(2)}) collective-permute-start(bf16[256,1024]{1,0:T(8,128)(2,1)} %get-tuple-element.28), channel_id=1, source_target_pairs={{2,0},{3,1},{4,6},{5,7},{10,8},{11,9},{12,14},{13,15},{18,16},{19,... | collective-permute-start | bytes 1572872 | tf_op jit(solution)/shard_map/ppermute | solution.py:256
  23.1 28.7 %collective-permute-start.8 = (bf16[288,1024]{1,0:T(8,128)(2,1)}, bf16[288,1024]{1,0:T(8,128)(2,1)}, u32[]{:S(2)}, u32[]{:S(2)}) collective-permute-start(bf16[288,1024]{1,0:T(8,128)(2,1)} %collective-permute-done.7), channel_id=1, source_target_pairs={{2,0},{3,1},{4,6},{5,7},{10,8},{11,9},{12,14},{13,15},{18,16},{19,... | collective-permute-start | bytes 1769480 | tf_op jit(solution)/shard_map/ppermute | solution.py:256
  24.4 27.4 %collective-permute-start.9 = (bf16[256,1024]{1,0:T(8,128)(2,1)}, bf16[256,1024]{1,0:T(8,128)(2,1)S(1)}, u32[]{:S(2)}, u32[]{:S(2)}) collective-permute-start(bf16[256,1024]{1,0:T(8,128)(2,1)} %get-tuple-element.35), channel_id=1, source_target_pairs={{0,4},{1,5},{6,2},{7,3},{8,12},{9,13},{14,10},{15,11},{16,20},{17,... | collective-permute-start | bytes 1572872 | tf_op jit(solution)/shard_map/ppermute | solution.py:256
  30.5 22.1 %collective-permute-start.2 = (bf16[256,1024]{1,0:T(8,128)(2,1)}, bf16[256,1024]{1,0:T(8,128)(2,1)}, u32[]{:S(2)}, u32[]{:S(2)}) collective-permute-start(bf16[256,1024]{1,0:T(8,128)(2,1)} %get-tuple-element.36), channel_id=1, source_target_pairs={{2,4},{3,5},{4,2},{5,3},{10,12},{11,13},{12,10},{13,11},{18,20},{1... | collective-permute-start | bytes 1572872 | tf_op jit(solution)/shard_map/ppermute | solution.py:256
  35.7 22.1 %collective-permute-start.6 = (bf16[256,1024]{1,0:T(8,128)(2,1)}, bf16[256,1024]{1,0:T(8,128)(2,1)}, u32[]{:S(2)}, u32[]{:S(2)}) collective-permute-start(bf16[256,1024]{1,0:T(8,128)(2,1)} %get-tuple-element.28), channel_id=1, source_target_pairs={{0,2},{1,3},{6,4},{7,5},{8,10},{9,11},{14,12},{15,13},{16,18},{17,... | collective-permute-start | bytes 1572872 | tf_op jit(solution)/shard_map/ppermute | solution.py:256
  44.2 0.8 copy-start.10
  45.1 18.6 %collective-permute-start.5 = (bf16[288,1024]{1,0:T(8,128)(2,1)}, bf16[288,1024]{1,0:T(8,128)(2,1)}, u32[]{:S(2)}, u32[]{:S(2)}) collective-permute-start(bf16[288,1024]{1,0:T(8,128)(2,1)} %collective-permute-done.1), channel_id=1, source_target_pairs={{2,0},{3,1},{4,6},{5,7},{10,8},{11,9},{12,14},{13,15},{18,16},{19,... | collective-permute-start | bytes 1769480 | tf_op jit(solution)/shard_map/ppermute | solution.py:256
  51.7 17.4 %collective-permute-start.10 = (bf16[288,1024]{1,0:T(8,128)(2,1)}, bf16[288,1024]{1,0:T(8,128)(2,1)S(1)}, u32[]{:S(2)}, u32[]{:S(2)}) collective-permute-start(bf16[288,1024]{1,0:T(8,128)(2,1)} %collective-permute-done.4.refs_1_), channel_id=1, source_target_pairs={{0,1},{1,0},{2,3},{3,2},{4,5},{5,4},{6,7},{7,6},{8,9},{9,8},{10,11... | collective-permute-start | bytes 1769480 | tf_op jit(solution)/shard_map/ppermute | solution.py:251
  51.8 0.9 copy-start.8
  52.6 33.5 %collective-permute-start.14 = (bf16[256,1024]{1,0:T(8,128)(2,1)}, bf16[256,1024]{1,0:T(8,128)(2,1)}, u32[]{:S(2)}, u32[]{:S(2)}) collective-permute-start(bf16[256,1024]{1,0:T(8,128)(2,1)} %get-tuple-element.35), channel_id=1, source_target_pairs={{2,6},{3,7},{4,0},{5,1},{10,14},{11,15},{12,8},{13,9},{18,22},{19,... | collective-permute-start | bytes 1572872 | tf_op jit(solution)/shard_map/ppermute | solution.py:256
  55.1 15.9 %collective-permute-start.13 = (bf16[288,1024]{1,0:T(8,128)(2,1)S(1)}, bf16[288,1024]{1,0:T(8,128)(2,1)}, u32[]{:S(2)}, u32[]{:S(2)}) collective-permute-start(bf16[288,1024]{1,0:T(8,128)(2,1)S(1)} %broadcast_select_fusion.refs_4_), channel_id=1, source_target_pairs={{0,1},{1,0},{2,3},{3,2},{4,5},{5,4},{6,7},{7,6},{8,9},{9,8},{10,11... | collective-permute-start | bytes 1769480 | tf_op jit(solution)/shard_map/ppermute | solution.py:251
  64.7 6.2 %collective-permute-start.11 = (bf16[128,1024]{1,0:T(8,128)(2,1)S(1)}, bf16[128,1024]{1,0:T(8,128)(2,1)}, u32[]{:S(2)}, u32[]{:S(2)}) collective-permute-start(bf16[128,1024]{1,0:T(8,128)(2,1)S(1)} %slice_select_fusion.1.refs_2_), channel_id=1, source_target_pairs={{0,1},{1,0},{2,3},{3,2},{4,5},{5,4},{6,7},{7,6},{8,9},{9,8},{10,11... | collective-permute-start | bytes 786440 | tf_op jit(solution)/shard_map/ppermute | solution.py:251
  64.8 21.3 %collective-permute-start.15 = (bf16[256,1024]{1,0:T(8,128)(2,1)}, bf16[256,1024]{1,0:T(8,128)(2,1)}, u32[]{:S(2)}, u32[]{:S(2)}) collective-permute-start(bf16[256,1024]{1,0:T(8,128)(2,1)} %get-tuple-element.36), channel_id=1, source_target_pairs={{0,6},{1,7},{6,0},{7,1},{8,14},{9,15},{14,8},{15,9},{16,22},{17,23... | collective-permute-start | bytes 1572872 | tf_op jit(solution)/shard_map/ppermute | solution.py:256
  69.2 0.8 copy-start.6
  70.0 1.8 %collective-permute-start.12 = (bf16[160,1024]{1,0:T(8,128)(2,1)S(1)}, bf16[160,1024]{1,0:T(8,128)(2,1)}, u32[]{:S(2)}, u32[]{:S(2)}) collective-permute-start(bf16[160,1024]{1,0:T(8,128)(2,1)S(1)} %slice_select_fusion.refs_3_), channel_id=1, source_target_pairs={{0,1},{1,0},{2,3},{3,2},{4,5},{5,4},{6,7},{7,6},{8,9},{9,8},{10,11... | collective-permute-start | bytes 983048 | tf_op jit(solution)/shard_map/ppermute | solution.py:251
  70.9 7.1 %copy-start.2 = (bf16[1,1024,1024]{2,1,0:T(8,128)(2,1)S(1)}, bf16[1,1024,1024]{2,1,0:T(8,128)(2,1)}, u32[]{:S(2)}) copy-start(bf16[1,1024,1024]{2,1,0:T(8,128)(2,1)} %param.13) | copy-start | bytes 6291460
  70.9 7.1 %copy-start.3 = (bf16[1,1024,256]{2,1,0:T(8,128)(2,1)S(1)}, bf16[1,1024,256]{2,1,0:T(8,128)(2,1)}, u32[]{:S(2)}) copy-start(bf16[1,1024,256]{2,1,0:T(8,128)(2,1)} %param.11) | copy-start | bytes 1572868
  70.9 7.1 %copy-start.4 = (bf16[1,8,32,1024]{3,2,1,0:T(8,128)(2,1)S(1)}, bf16[1,8,32,1024]{3,2,1,0:T(8,128)(2,1)}, u32[]{:S(2)}) copy-start(bf16[1,8,32,1024]{3,2,1,0:T(8,128)(2,1)} %param.15) | copy-start | bytes 1572868
  71.8 1.1 %copy-start.7 = (bf16[288,1024]{1,0:T(8,128)(2,1)S(1)}, bf16[288,1024]{1,0:T(8,128)(2,1)}, u32[]{:S(2)}) copy-start(bf16[288,1024]{1,0:T(8,128)(2,1)} %copy-done.6) | copy-start | bytes 1769476
  72.9 5.1 %copy-start.11 = (bf16[256,1024]{1,0:T(8,128)(2,1)S(1)}, bf16[256,1024]{1,0:T(8,128)(2,1)}, u32[]{:S(2)}) copy-start(bf16[256,1024]{1,0:T(8,128)(2,1)} %copy-done.10) | copy-start | bytes 1572868
  72.9 5.1 %copy-start.12 = (bf16[128,1024]{1,0:T(8,128)(2,1)S(1)}, bf16[128,1024]{1,0:T(8,128)(2,1)}, u32[]{:S(2)}) copy-start(bf16[128,1024]{1,0:T(8,128)(2,1)} %get-tuple-element.22.refs_0_) | copy-start | bytes 786436
  78.0 8.1 %copy-start.9 = (bf16[256,1024]{1,0:T(8,128)(2,1)S(1)}, bf16[256,1024]{1,0:T(8,128)(2,1)}, u32[]{:S(2)}) copy-start(bf16[256,1024]{1,0:T(8,128)(2,1)} %copy-done.8) | copy-start | bytes 1572868
  84.9 8.9 %copy-start.14 = (s32[8]{0:T(128)S(1)}, s32[8]{0:T(128)}, u32[]{:S(2)}) copy-start(s32[8]{0:T(128)} %param.17) | copy-start | bytes 100

commit v6 on v5

--- a/solution.py
+++ b/solution.py
@@ -149,7 +149,7 @@
     columns, size = basis.shape
     width = curvature.shape[0]
     ranks = right.shape[0]
-    step = min(width, 512)
+    step = min(width, 1024)
 
     def acts_copy(q, array, at):
         src = arrays[array].at[pl.ds(at * SEQ_LEN, SEQ_LEN)]
@@ -236,7 +236,7 @@
             pltpu.VMEM(basis.shape, BF16),
             pltpu.VMEM(curvature.shape, BF16),
             pltpu.VMEM(right.shape, BF16),
-            pltpu.SemaphoreType.DMA((2 * count + 3 + width // min(width, 512),)),
+            pltpu.SemaphoreType.DMA((2 * count + 3 + width // min(width, 1024),)),
         ],
         compiler_params=pltpu.CompilerParams(vmem_limit_bytes=VMEM_BYTES),
         cost_estimate=pl.CostEstimate(

time: 106 us -> 105 us (level)
  no operation moved by 1% of the time
where the time goes in v6:
time: 105 us
  starting transfers between devices  33.8 us (32%)
  waiting for transfers between devices  25.6 us (24%)
  Pallas kernels  24.7 us (24%)
  blocking collectives  10.6 us (10%)
  local copies, waits for them, and re-layouts  5.34 us (5%)
  other arithmetic  4.41 us (4%)
    ppermute x11, starting transfers between devices, hop(): return lax.ppermute(x, 'dp', pairs)  32.5 us
    ppermute x11, waiting for transfers between devices, hop(): return lax.ppermute(x, 'dp', pairs)  24.8 us
    pallas_call x2, Pallas kernels, score(): pl.pallas_call(functools.partial(score_kernel, blocks, len(arrays), queri...  13.8 us
    all_to_all x1, blocking collectives, on_device(): lax.all_to_all(outgoing, ('section', 'dp'), split_axis=0, concat_axis=0,...  10.6 us
    pallas_call x1, Pallas kernels, rotate_grads(): pl.pallas_call(functools.partial(rotate_kernel, count, sizes, sources, le...  5.04 us
    unnamed x30, local copies, waits for them, and re-layouts  4.92 us
    pallas_call x1, Pallas kernels, cut(): pl.pallas_call(functools.partial(cut_kernel, rows, columns), out_shape=[j...  3.05 us
    pallas_call x1, Pallas kernels, join_parts(): pl.pallas_call(functools.partial(join_kernel, rows, columns), out_shape=[...  2.77 us
  transfers between devices with their start and end apart: 16, of which 7 were waited for; matrix products, arithmetic and copies ran while one was open for 4% of the time, Pallas kernels for 14%

profile of v6, /device:TPU:0, one launch (start us, length us, event | category | flops | bytes accessed | tf_op | source)
XLA Modules:
  0.0 105.0 jit_solution(4894298871659267597)
XLA Ops:
  0.0 3.1 %shard_map.91 = (bf16[288,1024]{1,0:T(8,128)(2,1)}, bf16[800,1024]{1,0:T(8,128)(2,1)}) custom-call(s32[1]{0:T(128)} %bitcast.place, bf16[128,8192]{1,0:T(8,128)(2,1)} %bitcast.30, bf16[128,1024]{1,0:T(8,128)(2,1)} %bitcast.32, bf16[128,1024]{1,0:T(8,128)(2,1)} %bitcast.33, bf16[32,1024]{1,0:T(8,128)(2,1)} %bitcast.34), custom_call_target="tpu_custom_call" | custom-call | tf_op jit(solution)/shard_map/pallas_call | solution.py:51
  3.6 6.4 %collective-permute-start.7 = (bf16[288,1024]{1,0:T(8,128)(2,1)}, bf16[288,1024]{1,0:T(8,128)(2,1)}, u32[]{:S(2)}, u32[]{:S(2)}) collective-permute-start(bf16[288,1024]{1,0:T(8,128)(2,1)} %get-tuple-element.24.refs_0_), channel_id=1, source_target_pairs={{0,4},{1,5},{6,2},{7,3},{8,12},{9,13},{14,10},{15,11},{16,20},{17,... | collective-permute-start | bytes 1769480 | tf_op jit(solution)/shard_map/ppermute | solution.py:256
  9.9 1.5 %collective-permute-start.1 = (bf16[288,1024]{1,0:T(8,128)(2,1)}, bf16[288,1024]{1,0:T(8,128)(2,1)}, u32[]{:S(2)}, u32[]{:S(2)}) collective-permute-start(bf16[288,1024]{1,0:T(8,128)(2,1)} %get-tuple-element.24.refs_0_), channel_id=1, source_target_pairs={{2,4},{3,5},{4,2},{5,3},{10,12},{11,13},{12,10},{13,11},{18,20},{1... | collective-permute-start | bytes 1769480 | tf_op jit(solution)/shard_map/ppermute | solution.py:256
  11.4 1.2 %copy-done = bf16[800,1024]{1,0:T(8,128)(2,1)} copy-done((bf16[800,1024]{1,0:T(8,128)(2,1)}, bf16[800,1024]{1,0:T(8,128)(2,1)S(1)}, u32[]{:S(2)}) %copy-start) | copy-done | bytes 1638424
  12.6 2.8 %shard_map.92 = (bf16[128,1024]{1,0:T(8,128)(2,1)}, bf16[256,1024]{1,0:T(8,128)(2,1)}, bf16[256,1024]{1,0:T(8,128)(2,1)}, bf16[256,1024]{1,0:T(8,128)(2,1)}) custom-call(s32[1]{0:T(128)} %bitcast.place, bf16[128,8192]{1,0:T(8,128)(2,1)} %bitcast.31, bf16[800,1024]{1,0:T(8,128)(2,1)} %copy-done), custom_call_target="tpu_custom_call" | custom-call | tf_op jit(solution)/shard_map/pallas_call | solution.py:76
  15.4 1.4 %collective-permute-start.3 = (bf16[256,1024]{1,0:T(8,128)(2,1)}, bf16[256,1024]{1,0:T(8,128)(2,1)S(1)}, u32[]{:S(2)}, u32[]{:S(2)}) collective-permute-start(bf16[256,1024]{1,0:T(8,128)(2,1)} %get-tuple-element.28), channel_id=1, source_target_pairs={{2,0},{3,1},{4,6},{5,7},{10,8},{11,9},{12,14},{13,15},{18,16},{19,... | collective-permute-start | bytes 1572872 | tf_op jit(solution)/shard_map/ppermute | solution.py:256
  16.9 6.2 %collective-permute-done.7 = bf16[288,1024]{1,0:T(8,128)(2,1)} collective-permute-done((bf16[288,1024]{1,0:T(8,128)(2,1)}, bf16[288,1024]{1,0:T(8,128)(2,1)}, u32[]{:S(2)}, u32[]{:S(2)}) %collective-permute-start.7) | collective-permute-done | bytes 589856 | tf_op jit(solution)/shard_map/ppermute | solution.py:256
  23.1 1.3 %collective-permute-start.8 = (bf16[288,1024]{1,0:T(8,128)(2,1)}, bf16[288,1024]{1,0:T(8,128)(2,1)}, u32[]{:S(2)}, u32[]{:S(2)}) collective-permute-start(bf16[288,1024]{1,0:T(8,128)(2,1)} %collective-permute-done.7), channel_id=1, source_target_pairs={{2,0},{3,1},{4,6},{5,7},{10,8},{11,9},{12,14},{13,15},{18,16},{19,... | collective-permute-start | bytes 1769480 | tf_op jit(solution)/shard_map/ppermute | solution.py:256
  24.4 6.1 %collective-permute-start.9 = (bf16[256,1024]{1,0:T(8,128)(2,1)}, bf16[256,1024]{1,0:T(8,128)(2,1)S(1)}, u32[]{:S(2)}, u32[]{:S(2)}) collective-permute-start(bf16[256,1024]{1,0:T(8,128)(2,1)} %get-tuple-element.35), channel_id=1, source_target_pairs={{0,4},{1,5},{6,2},{7,3},{8,12},{9,13},{14,10},{15,11},{16,20},{17,... | collective-permute-start | bytes 1572872 | tf_op jit(solution)/shard_map/ppermute | solution.py:256
  30.5 1.5 %collective-permute-start.2 = (bf16[256,1024]{1,0:T(8,128)(2,1)}, bf16[256,1024]{1,0:T(8,128)(2,1)}, u32[]{:S(2)}, u32[]{:S(2)}) collective-permute-start(bf16[256,1024]{1,0:T(8,128)(2,1)} %get-tuple-element.36), channel_id=1, source_target_pairs={{2,4},{3,5},{4,2},{5,3},{10,12},{11,13},{12,10},{13,11},{18,20},{1... | collective-permute-start | bytes 1572872 | tf_op jit(solution)/shard_map/ppermute | solution.py:256
  32.0 3.7 %collective-permute-done.4.refs_1_ = bf16[288,1024]{1,0:T(8,128)(2,1)} collective-permute-done((bf16[288,1024]{1,0:T(8,128)(2,1)}, bf16[288,1024]{1,0:T(8,128)(2,1)}, u32[]{:S(2)}, u32[]{:S(2)}) %collective-permute-start.4) | collective-permute-done | bytes 589856 | tf_op jit(solution)/shard_map/ppermute | solution.py:256
  35.7 8.5 %collective-permute-start.6 = (bf16[256,1024]{1,0:T(8,128)(2,1)}, bf16[256,1024]{1,0:T(8,128)(2,1)}, u32[]{:S(2)}, u32[]{:S(2)}) collective-permute-start(bf16[256,1024]{1,0:T(8,128)(2,1)} %get-tuple-element.28), channel_id=1, source_target_pairs={{0,2},{1,3},{6,4},{7,5},{8,10},{9,11},{14,12},{15,13},{16,18},{17,... | collective-permute-start | bytes 1572872 | tf_op jit(solution)/shard_map/ppermute | solution.py:256
  44.2 0.8 copy-done.10
  45.1 1.3 %collective-permute-start.5 = (bf16[288,1024]{1,0:T(8,128)(2,1)}, bf16[288,1024]{1,0:T(8,128)(2,1)}, u32[]{:S(2)}, u32[]{:S(2)}) collective-permute-start(bf16[288,1024]{1,0:T(8,128)(2,1)} %collective-permute-done.1), channel_id=1, source_target_pairs={{2,0},{3,1},{4,6},{5,7},{10,8},{11,9},{12,14},{13,15},{18,16},{19,... | collective-permute-start | bytes 1769480 | tf_op jit(solution)/shard_map/ppermute | solution.py:256
  46.4 5.3 %collective-permute-done.8 = bf16[288,1024]{1,0:T(8,128)(2,1)} collective-permute-done((bf16[288,1024]{1,0:T(8,128)(2,1)}, bf16[288,1024]{1,0:T(8,128)(2,1)}, u32[]{:S(2)}, u32[]{:S(2)}) %collective-permute-start.8) | collective-permute-done | bytes 589856 | tf_op jit(solution)/shard_map/ppermute | solution.py:256
  51.8 0.9 copy-done.8
  52.6 1.3 %collective-permute-start.14 = (bf16[256,1024]{1,0:T(8,128)(2,1)}, bf16[256,1024]{1,0:T(8,128)(2,1)}, u32[]{:S(2)}, u32[]{:S(2)}) collective-permute-start(bf16[256,1024]{1,0:T(8,128)(2,1)} %get-tuple-element.35), channel_id=1, source_target_pairs={{2,6},{3,7},{4,0},{5,1},{10,14},{11,15},{12,8},{13,9},{18,22},{19,... | collective-permute-start | bytes 1572872 | tf_op jit(solution)/shard_map/ppermute | solution.py:256
  53.9 1.1 %broadcast_select_fusion.refs_4_ = bf16[288,1024]{1,0:T(8,128)(2,1)S(1)} fusion(bf16[288,1024]{1,0:T(8,128)(2,1)} %collective-permute-done.7, bf16[288,1024]{1,0:T(8,128)(2,1)} %collective-permute-done.8, pred[]{:T(512)S(6)} %or.3), kind=kLoop, calls=%fused_computation | loop fusion | flops 294912 | bytes 1769473 | tf_op jit(solution)/shard_map/jit(_where)/select_n | solution.py:282
  55.1 0.6 collective-permute-start.13
  55.6 2.2 %collective-permute-done.6.refs_2_ = bf16[256,1024]{1,0:T(8,128)(2,1)} collective-permute-done((bf16[256,1024]{1,0:T(8,128)(2,1)}, bf16[256,1024]{1,0:T(8,128)(2,1)}, u32[]{:S(2)}, u32[]{:S(2)}) %collective-permute-start.6) | collective-permute-done | bytes 524320 | tf_op jit(solution)/shard_map/ppermute | solution.py:256
  57.8 5.8 %collective-permute-done.5 = bf16[288,1024]{1,0:T(8,128)(2,1)} collective-permute-done((bf16[288,1024]{1,0:T(8,128)(2,1)}, bf16[288,1024]{1,0:T(8,128)(2,1)}, u32[]{:S(2)}, u32[]{:S(2)}) %collective-permute-start.5) | collective-permute-done | bytes 589856 | tf_op jit(solution)/shard_map/ppermute | solution.py:256
  63.7 1.1 %slice_select_fusion.1.refs_2_ = bf16[128,1024]{1,0:T(8,128)(2,1)S(1)} fusion(bf16[288,1024]{1,0:T(8,128)(2,1)} %collective-permute-done.1, bf16[288,1024]{1,0:T(8,128)(2,1)} %collective-permute-done.5, pred[]{:T(512)S(6)} %or.3), kind=kLoop, calls=%fused_computation.2 | loop fusion | flops 131072 | bytes 786433 | tf_op jit(solution)/shard_map/jit(_where)/select_n | solution.py:286
  64.8 3.3 %collective-permute-start.15 = (bf16[256,1024]{1,0:T(8,128)(2,1)}, bf16[256,1024]{1,0:T(8,128)(2,1)}, u32[]{:S(2)}, u32[]{:S(2)}) collective-permute-start(bf16[256,1024]{1,0:T(8,128)(2,1)} %get-tuple-element.36), channel_id=1, source_target_pairs={{0,6},{1,7},{6,0},{7,1},{8,14},{9,15},{14,8},{15,9},{16,22},{17,23... | collective-permute-start | bytes 1572872 | tf_op jit(solution)/shard_map/ppermute | solution.py:256
  68.1 1.1 %slice_select_fusion.refs_3_ = bf16[160,1024]{1,0:T(8,128)(2,1)S(1)} fusion(bf16[288,1024]{1,0:T(8,128)(2,1)} %collective-permute-done.1, bf16[288,1024]{1,0:T(8,128)(2,1)} %collective-permute-done.5, pred[]{:T(512)S(6)} %or.3), kind=kLoop, calls=%fused_computation.1 | loop fusion | flops 163840 | bytes 983041 | tf_op jit(solution)/shard_map/jit(_where)/select_n | solution.py:287
  69.2 0.8 copy-done.6
  71.0 0.8 collective-permute-done.12.refs_8_
  71.8 1.1 %copy-done.7 = bf16[288,1024]{1,0:T(8,128)(2,1)S(1)} copy-done((bf16[288,1024]{1,0:T(8,128)(2,1)S(1)}, bf16[288,1024]{1,0:T(8,128)(2,1)}, u32[]{:S(2)}) %copy-start.7) | copy-done | bytes 589848
  72.9 5.0 %shard_map.93 = (bf16[1024,1024]{1,0:T(8,128)(2,1)S(1)}, bf16[256,1024]{1,0:T(8,128)(2,1)S(1)}) custom-call(s32[8]{0:T(128)S(1)} %pad_add_fusion.place, bf16[288,1024]{1,0:T(8,128)(2,1)S(1)} %copy-done.5, bf16[288,1024]{1,0:T(8,128)(2,1)} %collective-permute-done.4.refs_1_, bf16[128,1024]{1,0:T(8,128)(2,1)S(1)} %slice_select_fusion.1.refs_2_, ...), custom_call_target="tpu_custom_call" | custom-call | flops 1 | bytes 1 | tf_op jit(solution)/shard_map/pallas_call | solution.py:119
  78.0 6.6 %shard_map.94 = f32[4,8,128]{2,1,0:T(8,128)S(1)} custom-call(s32[5]{0:T(128)S(1)} %concatenate.16.info, bf16[128,1024]{1,0:T(8,128)(2,1)S(1)} %copy-done.12, bf16[800,1024]{1,0:T(8,128)(2,1)S(1)} %copy-done.1, bf16[256,1024]{1,0:T(8,128)(2,1)} %collective-permute-done.2.refs_2_, bf16[256,1024]{1,0:T(8,128)(2,1)S(1)} %copy-done.11, ...), custom_call_target="tpu_custom_call" | custom-call | flops 1 | bytes 1 | tf_op jit(solution)/shard_map/pallas_call | solution.py:226
  84.7 1.4 %collective-permute-done.14.refs_1_ = bf16[256,1024]{1,0:T(8,128)(2,1)} collective-permute-done((bf16[256,1024]{1,0:T(8,128)(2,1)}, bf16[256,1024]{1,0:T(8,128)(2,1)}, u32[]{:S(2)}, u32[]{:S(2)}) %collective-permute-start.14) | collective-permute-done | bytes 524320 | tf_op jit(solution)/shard_map/ppermute | solution.py:256
  86.1 7.2 %shard_map.95 = f32[4,8,128]{2,1,0:T(8,128)S(1)} custom-call(s32[5]{0:T(128)S(1)} %concatenate.18.info, bf16[256,1024]{1,0:T(8,128)(2,1)S(1)} %copy-done.9, bf16[256,1024]{1,0:T(8,128)(2,1)} %collective-permute-done.14.refs_1_, bf16[256,1024]{1,0:T(8,128)(2,1)} %collective-permute-done.6.refs_2_, bf16[256,1024]{1,0:T(8,128)(2,1)} %collective-permute-done.15.refs_3_, ...), custom_call_target="tpu_custom_call" | custom-call | flops 1 | bytes 1 | tf_op jit(solution)/shard_map/pallas_call | solution.py:226
  93.8 10.6 %all_to_all.5 = f32[32,1,8]{2,1,0:T(1,128)S(1)} all-to-all(f32[32,1,8]{2,1,0:T(1,128)S(1)} %broadcast_select_fusion.1), channel_id=1, replica_groups=mesh['section'=4,'dp'=8] {'section','dp'}, dimensions={0} | all-to-all | bytes 2048 | tf_op jit(solution)/shard_map/all_to_all | solution.py:368
  (55 shorter events, 2.7 us)
Async XLA Ops:
  3.1 8.3 %collective-permute-start = (bf16[800,1024]{1,0:T(8,128)(2,1)}, bf16[800,1024]{1,0:T(8,128)(2,1)S(1)}, u32[]{:S(2)}, u32[]{:S(2)}) collective-permute-start(bf16[800,1024]{1,0:T(8,128)(2,1)} %get-tuple-element.21), channel_id=1, source_target_pairs={{0,1},{1,0},{2,3},{3,2},{4,5},{5,4},{6,7},{7,6},{8,9},{9,8},{10,11... | collective-permute-start | bytes 4915208 | tf_op jit(solution)/shard_map/ppermute | solution.py:251
  3.6 19.5 %collective-permute-start.7 = (bf16[288,1024]{1,0:T(8,128)(2,1)}, bf16[288,1024]{1,0:T(8,128)(2,1)}, u32[]{:S(2)}, u32[]{:S(2)}) collective-permute-start(bf16[288,1024]{1,0:T(8,128)(2,1)} %get-tuple-element.24.refs_0_), channel_id=1, source_target_pairs={{0,4},{1,5},{6,2},{7,3},{8,12},{9,13},{14,10},{15,11},{16,20},{17,... | collective-permute-start | bytes 1769480 | tf_op jit(solution)/shard_map/ppermute | solution.py:256
  9.9 20.6 %collective-permute-start.1 = (bf16[288,1024]{1,0:T(8,128)(2,1)}, bf16[288,1024]{1,0:T(8,128)(2,1)}, u32[]{:S(2)}, u32[]{:S(2)}) collective-permute-start(bf16[288,1024]{1,0:T(8,128)(2,1)} %get-tuple-element.24.refs_0_), channel_id=1, source_target_pairs={{2,4},{3,5},{4,2},{5,3},{10,12},{11,13},{12,10},{13,11},{18,20},{1... | collective-permute-start | bytes 1769480 | tf_op jit(solution)/shard_map/ppermute | solution.py:256
  11.4 24.3 %collective-permute-start.4 = (bf16[288,1024]{1,0:T(8,128)(2,1)}, bf16[288,1024]{1,0:T(8,128)(2,1)}, u32[]{:S(2)}, u32[]{:S(2)}) collective-permute-start(bf16[288,1024]{1,0:T(8,128)(2,1)} %get-tuple-element.24.refs_0_), channel_id=1, source_target_pairs={{0,2},{1,3},{2,0},{3,1},{4,6},{5,7},{6,4},{7,5},{8,10},{9,11},{10,... | collective-permute-start | bytes 1769480 | tf_op jit(solution)/shard_map/ppermute | solution.py:256
  11.4 1.2 %copy-start = (bf16[800,1024]{1,0:T(8,128)(2,1)}, bf16[800,1024]{1,0:T(8,128)(2,1)S(1)}, u32[]{:S(2)}) copy-start(bf16[800,1024]{1,0:T(8,128)(2,1)S(1)} %collective-permute-done.beside.refs_5_.refs_1_) | copy-start | bytes 4915204
  15.4 55.3 %copy-start.13 = (s32[8]{0:T(128)S(1)}, s32[8]{0:T(128)}, u32[]{:S(2)}) copy-start(s32[8]{0:T(128)} %param.16) | copy-start | bytes 100
  15.4 56.4 %copy-start.1 = (bf16[800,1024]{1,0:T(8,128)(2,1)S(1)}, bf16[800,1024]{1,0:T(8,128)(2,1)}, u32[]{:S(2)}) copy-start(bf16[800,1024]{1,0:T(8,128)(2,1)} %copy-done) | copy-start | bytes 4915204
  15.4 56.4 %copy-start.5 = (bf16[288,1024]{1,0:T(8,128)(2,1)S(1)}, bf16[288,1024]{1,0:T(8,128)(2,1)}, u32[]{:S(2)}) copy-start(bf16[288,1024]{1,0:T(8,128)(2,1)} %get-tuple-element.24.refs_0_) | copy-start | bytes 1769476
  15.4 28.8 %collective-permute-start.3 = (bf16[256,1024]{1,0:T(8,128)(2,1)}, bf16[256,1024]{1,0:T(8,128)(2,1)S(1)}, u32[]{:S(2)}, u32[]{:S(2)}) collective-permute-start(bf16[256,1024]{1,0:T(8,128)(2,1)} %get-tuple-element.28), channel_id=1, source_target_pairs={{2,0},{3,1},{4,6},{5,7},{10,8},{11,9},{12,14},{13,15},{18,16},{19,... | collective-permute-start | bytes 1572872 | tf_op jit(solution)/shard_map/ppermute | solution.py:256
  23.1 28.7 %collective-permute-start.8 = (bf16[288,1024]{1,0:T(8,128)(2,1)}, bf16[288,1024]{1,0:T(8,128)(2,1)}, u32[]{:S(2)}, u32[]{:S(2)}) collective-permute-start(bf16[288,1024]{1,0:T(8,128)(2,1)} %collective-permute-done.7), channel_id=1, source_target_pairs={{2,0},{3,1},{4,6},{5,7},{10,8},{11,9},{12,14},{13,15},{18,16},{19,... | collective-permute-start | bytes 1769480 | tf_op jit(solution)/shard_map/ppermute | solution.py:256
  24.4 27.4 %collective-permute-start.9 = (bf16[256,1024]{1,0:T(8,128)(2,1)}, bf16[256,1024]{1,0:T(8,128)(2,1)S(1)}, u32[]{:S(2)}, u32[]{:S(2)}) collective-permute-start(bf16[256,1024]{1,0:T(8,128)(2,1)} %get-tuple-element.35), channel_id=1, source_target_pairs={{0,4},{1,5},{6,2},{7,3},{8,12},{9,13},{14,10},{15,11},{16,20},{17,... | collective-permute-start | bytes 1572872 | tf_op jit(solution)/shard_map/ppermute | solution.py:256
  30.5 22.1 %collective-permute-start.2 = (bf16[256,1024]{1,0:T(8,128)(2,1)}, bf16[256,1024]{1,0:T(8,128)(2,1)}, u32[]{:S(2)}, u32[]{:S(2)}) collective-permute-start(bf16[256,1024]{1,0:T(8,128)(2,1)} %get-tuple-element.36), channel_id=1, source_target_pairs={{2,4},{3,5},{4,2},{5,3},{10,12},{11,13},{12,10},{13,11},{18,20},{1... | collective-permute-start | bytes 1572872 | tf_op jit(solution)/shard_map/ppermute | solution.py:256
  35.7 22.1 %collective-permute-start.6 = (bf16[256,1024]{1,0:T(8,128)(2,1)}, bf16[256,1024]{1,0:T(8,128)(2,1)}, u32[]{:S(2)}, u32[]{:S(2)}) collective-permute-start(bf16[256,1024]{1,0:T(8,128)(2,1)} %get-tuple-element.28), channel_id=1, source_target_pairs={{0,2},{1,3},{6,4},{7,5},{8,10},{9,11},{14,12},{15,13},{16,18},{17,... | collective-permute-start | bytes 1572872 | tf_op jit(solution)/shard_map/ppermute | solution.py:256
  44.2 0.8 copy-start.10
  45.1 18.6 %collective-permute-start.5 = (bf16[288,1024]{1,0:T(8,128)(2,1)}, bf16[288,1024]{1,0:T(8,128)(2,1)}, u32[]{:S(2)}, u32[]{:S(2)}) collective-permute-start(bf16[288,1024]{1,0:T(8,128)(2,1)} %collective-permute-done.1), channel_id=1, source_target_pairs={{2,0},{3,1},{4,6},{5,7},{10,8},{11,9},{12,14},{13,15},{18,16},{19,... | collective-permute-start | bytes 1769480 | tf_op jit(solution)/shard_map/ppermute | solution.py:256
  51.7 17.4 %collective-permute-start.10 = (bf16[288,1024]{1,0:T(8,128)(2,1)}, bf16[288,1024]{1,0:T(8,128)(2,1)S(1)}, u32[]{:S(2)}, u32[]{:S(2)}) collective-permute-start(bf16[288,1024]{1,0:T(8,128)(2,1)} %collective-permute-done.4.refs_1_), channel_id=1, source_target_pairs={{0,1},{1,0},{2,3},{3,2},{4,5},{5,4},{6,7},{7,6},{8,9},{9,8},{10,11... | collective-permute-start | bytes 1769480 | tf_op jit(solution)/shard_map/ppermute | solution.py:251
  51.8 0.9 copy-start.8
  52.6 33.5 %collective-permute-start.14 = (bf16[256,1024]{1,0:T(8,128)(2,1)}, bf16[256,1024]{1,0:T(8,128)(2,1)}, u32[]{:S(2)}, u32[]{:S(2)}) collective-permute-start(bf16[256,1024]{1,0:T(8,128)(2,1)} %get-tuple-element.35), channel_id=1, source_target_pairs={{2,6},{3,7},{4,0},{5,1},{10,14},{11,15},{12,8},{13,9},{18,22},{19,... | collective-permute-start | bytes 1572872 | tf_op jit(solution)/shard_map/ppermute | solution.py:256
  55.1 15.9 %collective-permute-start.13 = (bf16[288,1024]{1,0:T(8,128)(2,1)S(1)}, bf16[288,1024]{1,0:T(8,128)(2,1)}, u32[]{:S(2)}, u32[]{:S(2)}) collective-permute-start(bf16[288,1024]{1,0:T(8,128)(2,1)S(1)} %broadcast_select_fusion.refs_4_), channel_id=1, source_target_pairs={{0,1},{1,0},{2,3},{3,2},{4,5},{5,4},{6,7},{7,6},{8,9},{9,8},{10,11... | collective-permute-start | bytes 1769480 | tf_op jit(solution)/shard_map/ppermute | solution.py:251
  64.7 6.2 %collective-permute-start.11 = (bf16[128,1024]{1,0:T(8,128)(2,1)S(1)}, bf16[128,1024]{1,0:T(8,128)(2,1)}, u32[]{:S(2)}, u32[]{:S(2)}) collective-permute-start(bf16[128,1024]{1,0:T(8,128)(2,1)S(1)} %slice_select_fusion.1.refs_2_), channel_id=1, source_target_pairs={{0,1},{1,0},{2,3},{3,2},{4,5},{5,4},{6,7},{7,6},{8,9},{9,8},{10,11... | collective-permute-start | bytes 786440 | tf_op jit(solution)/shard_map/ppermute | solution.py:251
  64.8 21.3 %collective-permute-start.15 = (bf16[256,1024]{1,0:T(8,128)(2,1)}, bf16[256,1024]{1,0:T(8,128)(2,1)}, u32[]{:S(2)}, u32[]{:S(2)}) collective-permute-start(bf16[256,1024]{1,0:T(8,128)(2,1)} %get-tuple-element.36), channel_id=1, source_target_pairs={{0,6},{1,7},{6,0},{7,1},{8,14},{9,15},{14,8},{15,9},{16,22},{17,23... | collective-permute-start | bytes 1572872 | tf_op jit(solution)/shard_map/ppermute | solution.py:256
  69.2 0.8 copy-start.6
  70.0 1.8 %collective-permute-start.12 = (bf16[160,1024]{1,0:T(8,128)(2,1)S(1)}, bf16[160,1024]{1,0:T(8,128)(2,1)}, u32[]{:S(2)}, u32[]{:S(2)}) collective-permute-start(bf16[160,1024]{1,0:T(8,128)(2,1)S(1)} %slice_select_fusion.refs_3_), channel_id=1, source_target_pairs={{0,1},{1,0},{2,3},{3,2},{4,5},{5,4},{6,7},{7,6},{8,9},{9,8},{10,11... | collective-permute-start | bytes 983048 | tf_op jit(solution)/shard_map/ppermute | solution.py:251
  70.9 7.1 %copy-start.2 = (bf16[1,1024,1024]{2,1,0:T(8,128)(2,1)S(1)}, bf16[1,1024,1024]{2,1,0:T(8,128)(2,1)}, u32[]{:S(2)}) copy-start(bf16[1,1024,1024]{2,1,0:T(8,128)(2,1)} %param.13) | copy-start | bytes 6291460
  70.9 7.1 %copy-start.3 = (bf16[1,1024,256]{2,1,0:T(8,128)(2,1)S(1)}, bf16[1,1024,256]{2,1,0:T(8,128)(2,1)}, u32[]{:S(2)}) copy-start(bf16[1,1024,256]{2,1,0:T(8,128)(2,1)} %param.11) | copy-start | bytes 1572868
  70.9 7.1 %copy-start.4 = (bf16[1,8,32,1024]{3,2,1,0:T(8,128)(2,1)S(1)}, bf16[1,8,32,1024]{3,2,1,0:T(8,128)(2,1)}, u32[]{:S(2)}) copy-start(bf16[1,8,32,1024]{3,2,1,0:T(8,128)(2,1)} %param.15) | copy-start | bytes 1572868
  71.8 1.1 %copy-start.7 = (bf16[288,1024]{1,0:T(8,128)(2,1)S(1)}, bf16[288,1024]{1,0:T(8,128)(2,1)}, u32[]{:S(2)}) copy-start(bf16[288,1024]{1,0:T(8,128)(2,1)} %copy-done.6) | copy-start | bytes 1769476
  72.9 5.1 %copy-start.11 = (bf16[256,1024]{1,0:T(8,128)(2,1)S(1)}, bf16[256,1024]{1,0:T(8,128)(2,1)}, u32[]{:S(2)}) copy-start(bf16[256,1024]{1,0:T(8,128)(2,1)} %copy-done.10) | copy-start | bytes 1572868
  72.9 5.1 %copy-start.12 = (bf16[128,1024]{1,0:T(8,128)(2,1)S(1)}, bf16[128,1024]{1,0:T(8,128)(2,1)}, u32[]{:S(2)}) copy-start(bf16[128,1024]{1,0:T(8,128)(2,1)} %get-tuple-element.22.refs_0_) | copy-start | bytes 786436
  78.0 8.1 %copy-start.9 = (bf16[256,1024]{1,0:T(8,128)(2,1)S(1)}, bf16[256,1024]{1,0:T(8,128)(2,1)}, u32[]{:S(2)}) copy-start(bf16[256,1024]{1,0:T(8,128)(2,1)} %copy-done.8) | copy-start | bytes 1572868
  84.7 8.8 %copy-start.14 = (s32[8]{0:T(128)S(1)}, s32[8]{0:T(128)}, u32[]{:S(2)}) copy-start(s32[8]{0:T(128)} %param.17) | copy-start | bytes 100
